TPU v7x, 32 devices: a whole 2x2x4 slice. The times are simulated.
32 devices in a mesh: fsdp: 8 (over z, y), rep: 4 (over x, core).
Axes of the slice: x: 2, y: 2, z: 4, core: 2. Of those that a mesh axis runs over, the one named last changes fastest.
Arguments:
- tokens: bfloat16 [2, 32, 128, 1024], P(None, 'rep', 'fsdp'), may hold values from -6 to 6
- cotangent: bfloat16 [2, 32, 128, 1024], P(None, 'rep', 'fsdp'), may hold values from -6 to 6
- deal: int32 [2, 4, 8], P(None, 'rep'), may hold values from 0 to 7, each once within a row
- lengths: int32 [2, 4, 8], P(None, 'rep', 'fsdp'), may hold values from 16 to 128, as said below
- ln1_gain: float32 [1024], P('fsdp'), may hold values from 0.5 to 1.5
- w_qkv: float32 [1024, 3072], P('fsdp'), may hold values from -0.1875 to 0.1875
- w_out: float32 [1024, 1024], P('fsdp'), may hold values from -2 to 2
- ln2_gain: float32 [1024], P('fsdp'), may hold values from 0.5 to 1.5
- w_in: float32 [1024, 5248], P('fsdp'), may hold values from -0.1875 to 0.1875
- w_down: float32 [2624, 1024], P('fsdp'), may hold values from -0.125 to 0.125
Outputs:
- mixed: bfloat16 [2, 32, 128, 1024], P(None, 'rep', 'fsdp')
- grad_tokens: bfloat16 [2, 32, 128, 1024], P(None, 'rep', 'fsdp')
- grad_ln1: float32 [1024], P('fsdp')
- grad_qkv: float32 [1024, 3072], P('fsdp')
- grad_out: float32 [1024, 1024], P('fsdp')
- grad_ln2: float32 [1024], P('fsdp')
- grad_in: float32 [1024, 5248], P('fsdp')
- grad_down: float32 [2624, 1024], P('fsdp')
Inputs may be any that keep to these rules, and one draw needn't show every extreme that they name: For every micro-batch and replica, deal lists each fsdp index exactly once. `lengths`: in every micro-batch and replica one sequence has length exactly 128.
All inputs are finite; a program needn't handle non-finite values.
Results may differ from a plain program's by a relative error of at most 0.017.
The roundings to bfloat16 on the way count: a program that leaves them out, or rounds other values in their place, can miss the bound.
Values may be sent and summed in bfloat16 or wider, within the bound.
A program may use at most 192 MiB of HBM per device.

v0:
```python
import jax
import jax.numpy as jnp
from jax import lax
from jax.sharding import PartitionSpec as P

HEADS = 16


rope_base = 160000.0
norm_eps = 1e-05


def shortened(array):

    def short(part):
        return part.astype(jnp.bfloat16) if part.dtype == jnp.float32 else part

    return jax.tree.map(short, array)


def layer_norm(values, norm_gain):
    center = values - jnp.mean(values, axis=-1, keepdims=True)
    spread = jnp.mean(center * center, axis=-1, keepdims=True)
    return center * lax.rsqrt(spread + norm_eps) * norm_gain


def rope_tables(slot_count, head_size):
    half_size = head_size // 2
    frequency = rope_base ** (-(jnp.arange(half_size, dtype=jnp.float32) * 2.0 / head_size))
    angles = jnp.arange(slot_count, dtype=jnp.float32)[:, None] * frequency[None, :]
    return (jnp.cos(angles), jnp.sin(angles))


def rotate(tensor, cosine_table, sine_table):
    half_size = tensor.shape[-1] // 2
    front_half = tensor[..., :half_size]
    back_half = tensor[..., half_size:]
    cos_wide = cosine_table[:, None, :]
    sin_wide = sine_table[:, None, :]
    return jnp.concatenate(
        [
            front_half * cos_wide - back_half * sin_wide,
            back_half * cos_wide + front_half * sin_wide,
        ],
        axis=-1,
    )


def gated_gelu(hidden):
    half_size = hidden.shape[-1] // 2
    return jax.nn.gelu(hidden[..., :half_size], approximate=False) * hidden[..., half_size:]


def masked_scores(query_low, key_low, live_mask, scale_factor):
    raw_scores = (
        jnp.einsum("qhd,khd->hqk", query_low, key_low, preferred_element_type=jnp.float32)
        * scale_factor
    )
    return jnp.where(live_mask[None, None, :] > 0, raw_scores, -1e30)


def forward_pass(params, rows, live_mask):
    gain_one, qkv_weight, out_weight, gain_two, in_weight, down_weight = params
    token_values = rows.astype(jnp.float32)
    slot_count, model_width = token_values.shape
    head_count = HEADS
    head_size = model_width // head_count
    normed, norm_one_back = jax.vjp(layer_norm, token_values, gain_one.astype(jnp.float32))
    normed_low = normed.astype(jnp.bfloat16)
    packed = jnp.dot(normed_low, qkv_weight, preferred_element_type=jnp.float32)
    sections = packed.reshape(slot_count, 3, head_count, head_size)
    cosine_table, sine_table = rope_tables(slot_count, head_size)

    def rotate_pair(query_part, key_part):
        return (
            rotate(query_part, cosine_table, sine_table),
            rotate(key_part, cosine_table, sine_table),
        )

    (queries, key_rows), rope_back = jax.vjp(rotate_pair, sections[:, 0], sections[:, 1])
    query_low = queries.astype(jnp.bfloat16)
    key_low = key_rows.astype(jnp.bfloat16)
    value_low = sections[:, 2].astype(jnp.bfloat16)
    scale_factor = head_size ** (-0.5)
    scores = masked_scores(query_low, key_low, live_mask, scale_factor)
    row_max = jnp.max(scores, axis=-1, keepdims=True)
    row_lse = row_max + jnp.log(jnp.sum(jnp.exp(scores - row_max), axis=-1, keepdims=True))
    prob_low = jnp.exp(scores - row_lse).astype(jnp.bfloat16)
    attended = jnp.einsum("hqk,khd->qhd", prob_low, value_low, preferred_element_type=jnp.float32)
    attended_low = attended.reshape(slot_count, model_width).astype(jnp.bfloat16)
    branch_one = jnp.dot(attended_low, out_weight, preferred_element_type=jnp.float32)
    residual = token_values + live_mask[:, None] * branch_one
    ffn_norm, norm_two_back = jax.vjp(layer_norm, residual, gain_two.astype(jnp.float32))
    ffn_low = ffn_norm.astype(jnp.bfloat16)
    ffn_hidden = jnp.dot(ffn_low, in_weight, preferred_element_type=jnp.float32)
    gated_out, gate_back = jax.vjp(gated_gelu, ffn_hidden)
    gated_low = gated_out.astype(jnp.bfloat16)
    branch_two = jnp.dot(gated_low, down_weight, preferred_element_type=jnp.float32)
    mixed_rows = (residual + live_mask[:, None] * branch_two).astype(jnp.bfloat16)
    saved_state = (
        norm_one_back,
        normed_low,
        rope_back,
        query_low,
        key_low,
        value_low,
        row_lse,
        attended_low,
        norm_two_back,
        ffn_low,
        gate_back,
        gated_low,
        scale_factor,
    )
    return (mixed_rows, saved_state)


def backward_pass(params, saved_state, grad_rows, live_mask):
    gain_one, qkv_weight, out_weight, gain_two, in_weight, down_weight = params
    (
        norm_one_back,
        normed_low,
        rope_back,
        query_low,
        key_low,
        value_low,
        row_lse,
        attended_low,
        norm_two_back,
        ffn_low,
        gate_back,
        gated_low,
        scale_factor,
    ) = saved_state
    slot_count, head_count, head_size = query_low.shape
    upstream = grad_rows.astype(jnp.float32)
    branch_two_grad = (live_mask[:, None] * upstream).astype(jnp.bfloat16)
    down_grad = jnp.einsum(
        "sf,sd->fd", gated_low, branch_two_grad, preferred_element_type=jnp.float32
    )
    gated_grad = jnp.einsum(
        "sd,fd->sf", branch_two_grad, down_weight, preferred_element_type=jnp.float32
    )
    (hidden_grad,) = gate_back(gated_grad)
    hidden_low = hidden_grad.astype(jnp.bfloat16)
    in_grad = jnp.einsum("sd,sf->df", ffn_low, hidden_low, preferred_element_type=jnp.float32)
    ffn_norm_grad = jnp.einsum(
        "sf,df->sd", hidden_low, in_weight, preferred_element_type=jnp.float32
    )
    residual_part, gain_two_grad = norm_two_back(ffn_norm_grad)
    residual_grad = upstream + residual_part
    branch_one_grad = (live_mask[:, None] * residual_grad).astype(jnp.bfloat16)
    out_grad = jnp.einsum(
        "se,sd->ed", attended_low, branch_one_grad, preferred_element_type=jnp.float32
    )
    attended_grad = jnp.einsum(
        "sd,ed->se", branch_one_grad, out_weight, preferred_element_type=jnp.float32
    )
    attended_grad = attended_grad.astype(jnp.bfloat16).reshape(slot_count, head_count, head_size)
    scores = masked_scores(query_low, key_low, live_mask, scale_factor)
    attn_prob = jnp.exp(scores - row_lse)
    prob_grad = jnp.einsum(
        "qhd,khd->hqk", attended_grad, value_low, preferred_element_type=jnp.float32
    )
    score_grad = attn_prob * (prob_grad - jnp.sum(prob_grad * attn_prob, axis=-1, keepdims=True))
    score_low = score_grad.astype(jnp.bfloat16)
    query_grad = (
        jnp.einsum("hqk,khd->qhd", score_low, key_low, preferred_element_type=jnp.float32)
        * scale_factor
    )
    key_grad = (
        jnp.einsum("hqk,qhd->khd", score_low, query_low, preferred_element_type=jnp.float32)
        * scale_factor
    )
    value_grad = jnp.einsum(
        "hqk,qhd->khd",
        attn_prob.astype(jnp.bfloat16),
        attended_grad,
        preferred_element_type=jnp.float32,
    )
    query_pre, key_pre = rope_back((query_grad, key_grad))
    packed_grad = jnp.stack([query_pre, key_pre, value_grad], axis=1)
    packed_low = packed_grad.reshape(slot_count, 3 * head_count * head_size).astype(jnp.bfloat16)
    qkv_grad = jnp.einsum("sd,se->de", normed_low, packed_low, preferred_element_type=jnp.float32)
    normed_grad = jnp.einsum(
        "se,de->sd", packed_low, qkv_weight, preferred_element_type=jnp.float32
    )
    token_part, gain_one_grad = norm_one_back(normed_grad)
    input_grad = (residual_grad + token_part).astype(jnp.bfloat16)
    return (input_grad, (gain_one_grad, qkv_grad, out_grad, gain_two_grad, in_grad, down_grad))


def on_device(tokens, cotangent, deal, lengths, ln1_gain, w_qkv, w_out, ln2_gain, w_in, w_down):
    fsdp_count = lax.axis_size("fsdp")
    micro_count = tokens.shape[0]
    destination = deal[:, 0, :]
    indices = jnp.arange(fsdp_count, dtype=jnp.int32)
    matches = (destination[:, :, None] == indices[None, None, :]).astype(jnp.int32)
    source = jnp.sum(matches * indices[None, :, None], axis=1)
    pick_rows = jax.vmap(lambda stacked, ordering: jnp.take(stacked, ordering, axis=0))
    sent_tokens = pick_rows(tokens, source)
    sent_grads = pick_rows(cotangent, source)
    dealt_tokens, dealt_grads = (
        lax.all_to_all(sent_tokens, "fsdp", split_axis=1, concat_axis=2, tiled=True),
        lax.all_to_all(sent_grads, "fsdp", split_axis=1, concat_axis=2, tiled=True),
    )
    slot_count = dealt_tokens.shape[2]
    positions = jnp.arange(slot_count, dtype=jnp.int32)
    shards = (
        ln1_gain.astype(jnp.bfloat16),
        w_qkv.astype(jnp.bfloat16),
        w_out.astype(jnp.bfloat16),
        ln2_gain.astype(jnp.bfloat16),
        w_in.astype(jnp.bfloat16),
        w_down.astype(jnp.bfloat16),
    )
    totals = None
    mixed_list = []
    grad_list = []
    for micro_index in range(micro_count):
        live_mask = (positions < lengths[micro_index, 0, 0]).astype(jnp.float32)
        forward_params = (
            lax.all_gather(shards[0], "fsdp", axis=0, tiled=True),
            lax.all_gather(shards[1], "fsdp", axis=0, tiled=True),
            lax.all_gather(shards[2], "fsdp", axis=0, tiled=True),
            lax.all_gather(shards[3], "fsdp", axis=0, tiled=True),
            lax.all_gather(shards[4], "fsdp", axis=0, tiled=True),
            lax.all_gather(shards[5], "fsdp", axis=0, tiled=True),
        )
        mixed_rows, saved_state = forward_pass(
            forward_params, dealt_tokens[micro_index, 0], live_mask
        )
        backward_params = (
            lax.all_gather(shards[0], "fsdp", axis=0, tiled=True),
            lax.all_gather(shards[1], "fsdp", axis=0, tiled=True),
            lax.all_gather(shards[2], "fsdp", axis=0, tiled=True),
            lax.all_gather(shards[3], "fsdp", axis=0, tiled=True),
            lax.all_gather(shards[4], "fsdp", axis=0, tiled=True),
            lax.all_gather(shards[5], "fsdp", axis=0, tiled=True),
        )
        input_grad, param_grads = backward_pass(
            backward_params, saved_state, dealt_grads[micro_index, 0], live_mask
        )
        totals = param_grads if totals is None else jax.tree.map(jnp.add, totals, param_grads)
        mixed_list.append(mixed_rows)
        grad_list.append(input_grad)
    owned_total = lax.psum_scatter(totals, "fsdp", scatter_dimension=0, tiled=True)
    replica_total = jax.tree.map(
        lambda part: part.astype(jnp.float32), lax.psum(shortened(owned_total), "rep")
    )
    mixed_all = jnp.stack(mixed_list)[:, None]
    grads_all = jnp.stack(grad_list)[:, None]
    back_mixed, back_grads = (
        lax.all_to_all(mixed_all, "fsdp", split_axis=2, concat_axis=1, tiled=True),
        lax.all_to_all(grads_all, "fsdp", split_axis=2, concat_axis=1, tiled=True),
    )
    mixed_out = pick_rows(back_mixed, destination)
    grad_tokens = pick_rows(back_grads, destination)
    return (mixed_out, grad_tokens) + tuple(replica_total)


def solution(mesh):
    return jax.shard_map(
        on_device,
        mesh=mesh,
        in_specs=(
            P(None, "rep", "fsdp", None),
            P(None, "rep", "fsdp", None),
            P(None, "rep", None),
            P(None, "rep", "fsdp"),
            P("fsdp"),
            P("fsdp", None),
            P("fsdp", None),
            P("fsdp"),
            P("fsdp", None),
            P("fsdp", None),
        ),
        out_specs=(
            P(None, "rep", "fsdp", None),
            P(None, "rep", "fsdp", None),
            P("fsdp"),
            P("fsdp", None),
            P("fsdp", None),
            P("fsdp"),
            P("fsdp", None),
            P("fsdp", None),
        ),
        check_vma=False,
    )
```

profile of v0, /device:TPU:17, one launch (start us, length us, event | category | flops | bytes accessed | tf_op | source)
XLA Modules:
  0.0 1408.5 jit_solution(16934930058948958268)
XLA Ops:
  7.2 2.5 convert_element_type.275
  9.9 1.8 convert_element_type.281
  11.7 1.2 convert_element_type.285
  13.0 1.2 copy-done.52
  17.7 5.6 all-to-all-start
  23.3 34.4 %all-gather.1 = bf16[8,1,128]{2,1,0:T(2,128)(2,1)S(1)} all-gather(bf16[1,1,128]{2,1,0:T(2,128)(2,1)S(1)} %convert_bitcast_fusion), channel_id=1, replica_groups=mesh['fsdp'=8,'rep'=4] {'fsdp'}, dimensions={0}, use_global_device_ids=true | all-gather | bytes 2304 | tf_op jit(solution)/shard_map/all_gather | solution.py:226
  57.7 10.7 all-gather
  70.5 1.2 broadcast_compare_fusion.1
  73.2 9.0 all-to-all-start.2
  82.6 21.1 %all-to-all-done.2 = bf16[2,8,16,1024]{3,2,0,1:T(8,128)(2,1)S(1)} async-done(((bf16[2,8,16,1024]{3,2,0,1:T(8,128)(2,1)}), bf16[2,8,16,1024]{3,2,0,1:T(8,128)(2,1)S(1)}, u32[]{:S(2)}, u32[]{:S(2)}) %all-to-all-start.2) | async-done | bytes 524320 | tf_op jit(solution)/shard_map/all_to_all | solution.py:205
  107.4 20.5 %all-gather.7.cloned.1.call-done = bf16[1024,3072]{1,0:T(8,128)(2,1)} async-done(((bf16[128,3072]{1,0:T(8,128)(2,1)}), bf16[1024,3072]{1,0:T(8,128)(2,1)}) %all-gather.7.cloned.1.call-update) | async-done | bytes 6291472 | tf_op jit(solution)/shard_map/all_gather | solution.py:224
  127.9 8.6 copy.93
  136.5 4.6 fusion.83
  143.1 37.9 %all-gather.9.cloned.1.call-done = bf16[1024,1024]{1,0:T(8,128)(2,1)} async-done(((bf16[128,1024]{1,0:T(8,128)(2,1)}), bf16[1024,1024]{1,0:T(8,128)(2,1)}) %all-gather.9.cloned.1.call-update) | async-done | bytes 2097168 | tf_op jit(solution)/shard_map/all_gather | solution.py:225
  181.0 2.1 fusion.79
  183.4 4.6 fusion.82
  190.2 145.9 %all-gather.11.cloned.1.call-done = bf16[1024,5248]{1,0:T(8,128)(2,1)} async-done(((bf16[128,5248]{1,0:T(8,128)(2,1)}), bf16[1024,5248]{1,0:T(8,128)(2,1)}) %all-gather.11.cloned.1.call-update) | async-done | bytes 10747920 | tf_op jit(solution)/shard_map/all_gather | solution.py:227
  336.1 5.7 fusion.70
  341.8 82.4 %all-gather.13.cloned.1.call-done = bf16[2624,1024]{1,0:T(8,128)(2,1)} async-done(((bf16[328,1024]{1,0:T(8,128)(2,1)}), bf16[2624,1024]{1,0:T(8,128)(2,1)}) %all-gather.13.cloned.1.call-update) | async-done | bytes 5373968 | tf_op jit(solution)/shard_map/all_gather | solution.py:228
  424.2 6.6 fusion.32
  430.8 1.7 multiply_add_fusion
  432.5 3.7 multiply_reduce_fusion.2
  438.0 1.6 convolution_convert_fusion
  440.7 1.9 multiply_reduce_fusion
  444.3 1.2 multiply_add_fusion.5
  446.3 1.8 convolution_convert_fusion.3
  449.0 1.7 fusion.69
  450.8 13.8 fusion.33
  464.6 1.7 multiply_add_fusion.1
  466.3 3.7 multiply_reduce_fusion.3
  472.3 2.7 convolution_add_fusion.3
  476.1 1.6 fusion.87
  477.7 5.5 convolution_add_fusion.1
  483.3 1.5 copy-done.5
  484.8 1.5 convolution_convert_fusion.1
  486.3 1.2 copy.101
  489.8 1.4 multiply_reduce_fusion.1
  496.2 1.8 fusion.85
  498.0 6.4 convolution_add_fusion.2
  504.7 11.0 fusion.38
  515.7 13.7 convolution_add_fusion
  530.5 3.5 fusion.27
  534.1 3.5 fusion.26
  537.7 1.3 copy.96
  539.0 4.8 all-to-all-start.1
  543.8 5.1 fusion.84
  549.0 5.1 multiply_reduce_fusion.8
  554.7 17.3 %reduce-scatter.7.cloned.1.call-done = f32[128,1024]{1,0:T(8,128)} async-done(((f32[1024,1024]{1,0:T(8,128)}), f32[128,1024]{1,0:T(8,128)}) %reduce-scatter.7.cloned.1.call-update) | async-done | bytes 524304 | tf_op jit(solution)/shard_map/reduce_scatter | solution.py:247
  572.0 1.8 convert_element_type.327
  573.8 184.7 %reduce-scatter.11.cloned.1.call-done = f32[328,1024]{1,0:T(8,128)} async-done(((f32[2624,1024]{1,0:T(8,128)}), f32[328,1024]{1,0:T(8,128)}) %reduce-scatter.11.cloned.1.call-update) | async-done | bytes 1343504 | tf_op jit(solution)/shard_map/reduce_scatter | solution.py:247
  758.5 2.3 convert_element_type.333
  760.8 207.8 %reduce-scatter.5.cloned.1.call-done = f32[128,3072]{1,0:T(8,128)} async-done(((f32[1024,3072]{1,0:T(8,128)}), f32[128,3072]{1,0:T(8,128)}) %reduce-scatter.5.cloned.1.call-update) | async-done | bytes 1572880 | tf_op jit(solution)/shard_map/reduce_scatter | solution.py:247
  968.5 2.4 convert_element_type.325
  970.9 351.8 %reduce-scatter.9.cloned.1.call-done = f32[128,5248]{1,0:T(8,128)} async-done(((f32[1024,5248]{1,0:T(8,128)}), f32[128,5248]{1,0:T(8,128)}) %reduce-scatter.9.cloned.1.call-update) | async-done | bytes 2686992 | tf_op jit(solution)/shard_map/reduce_scatter | solution.py:247
  1322.7 3.0 convert_element_type.331
  1327.6 1.3 copy.111
  1328.9 4.6 all-to-all-start.3
  1334.9 18.1 %all-reduce.14 = (bf16[1024]{0:T(1024)(128)(2,1)S(1)}, bf16[1024]{0:T(1024)(128)(2,1)S(1)}) all-reduce(f32[1024]{0:T(1024)S(1)} %add.189, f32[1024]{0:T(1024)S(1)} %add.192), channel_id=2, replica_groups=mesh['fsdp'=8,'rep'=4] {'fsdp'}, use_global_device_ids=true, to_apply=%region_25.27.clone | all-reduce | flops 2048 | bytes 12288
  1353.2 9.3 all-reduce.15
  1367.2 26.6 %all-reduce.19.cloned.1.call-done = (bf16[128,3072]{1,0:T(8,128)(2,1)}, bf16[128,1024]{1,0:T(8,128)(2,1)}, bf16[128,5248]{1,0:T(8,128)(2,1)}, bf16[328,1024]{1,0:T(8,128)(2,1)}) async-done(((bf16[128,3072]{1,0:T(8,128)(2,1)}, bf16[128,1024]{1,0:T(8,128)(2,1)}, bf16[128,5248]{1,0:T(8,128)(2,1)}, bf16[328,1024]{1,0:T(8,128)(2,1)}), (bf16[128,3072]{1,0:T(8,128)(2,1)}, bf16[128,1024]{1,0:T(8,128)(2,1)}, ...) | async-done | bytes 3063824 | tf_op jit(solution)/shard_map/psum | solution.py:249
  1393.8 1.8 convert_element_type.328
  1395.6 2.5 convert_element_type.326
  1398.1 1.2 convert_element_type.334
  1399.9 1.7 convert_element_type.332
  (308 shorter events, 41.9 us)
Async XLA Ops:
  7.2 8.3 copy-start
  7.2 120.7 %all-gather.7.cloned.1.call-start = ((), (), s32[]{:S(2)}) async-start(), calls=%async_computation.8 | async-start | bytes 7077888 | tf_op jit(solution)/shard_map/all_gather | solution.py:224
  7.2 4.5 copy-start.38
  9.8 171.2 %all-gather.9.cloned.1.call-start = ((), (), s32[]{:S(2)}) async-start(), calls=%async_computation.9 | async-start | bytes 2359296 | tf_op jit(solution)/shard_map/all_gather | solution.py:225
  11.7 324.4 %all-gather.11.cloned.1.call-start = ((), (), s32[]{:S(2)}) async-start(), calls=%async_computation.10 | async-start | bytes 12091392 | tf_op jit(solution)/shard_map/all_gather | solution.py:227
  13.0 2.3 copy-start.78
  13.0 3.0 copy-start.75
  13.0 411.2 %all-gather.13.cloned.1.call-start = ((), (), s32[]{:S(2)}) async-start(), calls=%async_computation.11 | async-start | bytes 6045696 | tf_op jit(solution)/shard_map/all_gather | solution.py:228
  16.8 6.5 copy-start.85
  16.8 6.5 copy-start.86
  16.8 52.5 %copy-start.82 = (s32[2,1,1]{0,2,1:T(1,128)S(1)}, s32[2,1,1]{0,2,1:T(1,128)}, u32[]{:S(2)}) copy-start(s32[2,1,1]{0,2,1:T(1,128)} %param.15) | copy-start | bytes 28
  17.7 55.5 %all-to-all-start = ((bf16[2,8,16,1024]{3,2,0,1:T(8,128)(2,1)}), bf16[2,8,16,1024]{3,2,0,1:T(8,128)(2,1)S(1)}, u32[]{:S(2)}, u32[]{:S(2)}) async-start(bf16[2,8,16,1024]{3,2,0,1:T(8,128)(2,1)} %copy.92), calls=%async_computation | async-start | bytes 1048576 | tf_op jit(solution)/shard_map/all_to_all | solution.py:204
  68.4 37.7 %copy-start.76 = (f32[8,1,128]{2,1,0:T(1,128)}, f32[8,1,128]{2,1,0:T(1,128)S(1)}, u32[]{:S(2)}) copy-start(f32[8,1,128]{2,1,0:T(1,128)S(1)} %convert_element_type.339) | copy-start | bytes 12292
  73.2 33.2 %copy-start.6 = (bf16[2,8,16,1024]{3,2,0,1:T(8,128)(2,1)}, bf16[2,8,16,1024]{3,2,0,1:T(8,128)(2,1)S(1)}, u32[]{:S(2)}) copy-start(bf16[2,8,16,1024]{3,2,0,1:T(8,128)(2,1)S(1)} %all-to-all-done) | copy-start | bytes 1572868
  73.2 30.5 %all-to-all-start.2 = ((bf16[2,8,16,1024]{3,2,0,1:T(8,128)(2,1)}), bf16[2,8,16,1024]{3,2,0,1:T(8,128)(2,1)S(1)}, u32[]{:S(2)}, u32[]{:S(2)}) async-start(bf16[2,8,16,1024]{3,2,0,1:T(8,128)(2,1)} %copy.98), calls=%async_computation.2 | async-start | bytes 1048576 | tf_op jit(solution)/shard_map/all_to_all | solution.py:205
  82.2 489.8 %reduce-scatter.7.cloned.1.call-start = ((), (), s32[]{:S(2)}) async-start(), calls=%async_computation.13 | async-start | bytes 4718592 | tf_op jit(solution)/shard_map/reduce_scatter | solution.py:247
  103.8 332.7 %copy-start.34 = (bf16[1,8,16,1024]{3,2,0,1:T(8,128)(2,1)}, bf16[1,8,16,1024]{3,2,0,1:T(8,128)(2,1)S(1)}, u32[]{:S(2)}) copy-start(bf16[1,8,16,1024]{3,2,0,1:T(8,128)(2,1)S(1)} %get-tuple-element.70) | copy-start | bytes 786436
  106.4 30.1 %copy-start.39 = (bf16[1,8,16,1024]{3,2,0,1:T(8,128)(2,1)}, bf16[1,8,16,1024]{3,2,0,1:T(8,128)(2,1)S(1)}, u32[]{:S(2)}) copy-start(bf16[1,8,16,1024]{3,2,0,1:T(8,128)(2,1)S(1)} %get-tuple-element.68) | copy-start | bytes 786436
  106.5 76.9 %copy-start.36 = (bf16[1,8,16,1024]{3,2,0,1:T(8,128)(2,1)}, bf16[1,8,16,1024]{3,2,0,1:T(8,128)(2,1)S(1)}, u32[]{:S(2)}) copy-start(bf16[1,8,16,1024]{3,2,0,1:T(8,128)(2,1)S(1)} %get-tuple-element.67) | copy-start | bytes 786436
  143.1 40.0 %copy-start.41 = (bf16[16,64,128]{2,1,0:T(8,128)(2,1)}, bf16[16,64,128]{2,1,0:T(8,128)(2,1)S(1)}, u32[]{:S(2)}) copy-start(bf16[16,64,128]{2,1,0:T(8,128)(2,1)S(1)} %convolution_convert_fusion.2) | copy-start | bytes 786436
  183.3 4.6 copy-start.83
  424.2 8.3 copy-start.2
  432.5 3.7 copy-start.15
  432.5 3.7 copy-start.84
  436.2 1.8 copy-start.3
  438.0 2.7 copy-start.43
  438.0 10.9 slice-start
  440.7 2.0 copy-start.45
  440.7 2.0 copy-start.9
  440.7 2.2 copy-start.72
  440.7 2.2 copy-start.74
  440.7 2.7 copy-start.68
  440.7 2.7 copy-start.70
  442.6 6.3 slice-start.1
  444.3 3.9 copy-start.4
  445.5 3.5 slice-start.2
  445.9 2.3 copy-start.11
  445.9 2.3 copy-start.49
  448.1 2.5 slice-start.3
  449.0 1.8 slice-start.4
  449.0 1.8 copy-start.55
  466.3 3.7 copy-start.17
  474.9 283.5 %reduce-scatter.11.cloned.1.call-start = ((), (), s32[]{:S(2)}) async-start(), calls=%async_computation.15 | async-start | bytes 12091392 | tf_op jit(solution)/shard_map/reduce_scatter | solution.py:247
  483.2 485.3 %reduce-scatter.5.cloned.1.call-start = ((), (), s32[]{:S(2)}) async-start(), calls=%async_computation.12 | async-start | bytes 14155776 | tf_op jit(solution)/shard_map/reduce_scatter | solution.py:247
  486.3 2.4 copy-start.57
  486.3 3.4 copy-start.12
  487.6 3.6 copy-start.47
  495.8 2.2 copy-start.20
  496.2 1.8 copy-start.40
  504.4 11.3 copy-start.16
  504.4 818.3 %reduce-scatter.9.cloned.1.call-start = ((), (), s32[]{:S(2)}) async-start(), calls=%async_computation.14 | async-start | bytes 24182784 | tf_op jit(solution)/shard_map/reduce_scatter | solution.py:247
  504.7 11.0 copy-start.25
  530.5 3.5 copy-start.19
  539.0 789.9 %all-to-all-start.1 = ((bf16[2,1,128,1024]{3,0,1,2:T(2,128)(2,1)}), bf16[2,1,128,1024]{3,0,1,2:T(2,128)(2,1)}, u32[]{:S(2)}, u32[]{:S(2)}) async-start(bf16[2,1,128,1024]{3,0,1,2:T(2,128)(2,1)} %copy.96), calls=%async_computation.1 | async-start | bytes 1048576 | tf_op jit(solution)/shard_map/all_to_all | solution.py:254
  543.8 5.2 copy-start.7
  543.8 5.2 copy-start.21
  543.8 5.2 copy-start.77
  543.8 850.0 %all-reduce.19.cloned.1.call-start = ((), (), s32[]{:S(2)}) async-start(), calls=%async_computation.16 | async-start | bytes 6127616 | tf_op jit(solution)/shard_map/psum | solution.py:249
  1327.5 6.1 copy-start.79
  1327.5 6.1 copy-start.87
  1328.9 36.4 %all-to-all-start.3 = ((bf16[2,1,128,1024]{3,0,1,2:T(2,128)(2,1)}), bf16[2,1,128,1024]{3,0,1,2:T(2,128)(2,1)S(1)}, u32[]{:S(2)}, u32[]{:S(2)}) async-start(bf16[2,1,128,1024]{3,0,1,2:T(2,128)(2,1)} %copy.111), calls=%async_computation.3 | async-start | bytes 1048576 | tf_op jit(solution)/shard_map/all_to_all | solution.py:255
  1395.6 2.5 copy-start.58
  1398.1 1.8 copy-start.53
  1399.3 2.3 copy-start.1
  (43 other events, 48.5 us)
Sparse Core Ops, SparseCore 0:
  10.8 117.0 all-gather.6
  130.6 50.3 all-gather.8
  183.7 152.3 all-gather.10
  338.1 86.0 all-gather.12
  475.1 96.8 reduce-scatter.6
  575.9 182.5 reduce-scatter.10
  762.1 206.4 reduce-scatter.4
  972.4 350.2 reduce-scatter.8
  1326.1 67.6 all-reduce.18
where the time goes:
time: 1420 us; the launch traced here: 1410 us
  waiting for transfers between devices  1100 us (77%)
  matrix products  119 us (8%)
  blocking collectives  72.5 us (5%)
  other arithmetic  42.7 us (3%)
  local copies, waits for them, and re-layouts  37 us (3%)
  starting transfers between devices  24.5 us (2%)
  between operations  16.2 us (1%)
    reduce_scatter x4, waiting for transfers between devices, on_device(): lax.psum_scatter(totals, 'fsdp', scatter_dimension=0, tiled=True)  762 us
    all_gather x1, waiting for transfers between devices, on_device(): lax.all_gather(shards[4], 'fsdp', axis=0, tiled=True)  146 us
    all_gather x1, waiting for transfers between devices, on_device(): lax.all_gather(shards[5], 'fsdp', axis=0, tiled=True)  82.4 us
    all_gather x1, waiting for transfers between devices, on_device(): lax.all_gather(shards[2], 'fsdp', axis=0, tiled=True)  37.9 us
    all_gather x1, blocking collectives, on_device(): lax.all_gather(shards[3], 'fsdp', axis=0, tiled=True)  34.4 us
  transfers between devices with their start and end apart: 13, of which 10 were waited for; matrix products, arithmetic and copies ran while one was open for 9% of the time, Pallas kernels for 0%

commit v1 on v0

v1 whole, which is shorter than its diff:
```python
import functools

import jax
import jax.numpy as jnp
from jax import lax
from jax.experimental import pallas as pl
from jax.experimental.pallas import tpu as pltpu
from jax.sharding import PartitionSpec as P

HEADS = 16
ROPE_BASE = 160000.0
NORM_EPS = 1e-05
MESH = pl.DeviceIdType.MESH
MIB = 1 << 20
BF16 = jnp.bfloat16
F32 = jnp.float32


def rope_tables(slot_count, head_size):
    half_size = head_size // 2
    frequency = ROPE_BASE ** (-(jnp.arange(half_size, dtype=F32) * 2.0 / head_size))
    angles = jnp.arange(slot_count, dtype=F32)[:, None] * frequency[None, :]
    return jnp.cos(angles), jnp.sin(angles)


def rotate(values, cosine, sine):
    front, back = jnp.split(values, 2, axis=-1)
    cosine, sine = cosine[:, None, :], sine[:, None, :]
    return jnp.concatenate([front * cosine - back * sine, back * cosine + front * sine], axis=-1)


def normed(values, gain):
    center = values - jnp.mean(values, axis=-1, keepdims=True)
    root = lax.rsqrt(jnp.mean(center * center, axis=-1, keepdims=True) + NORM_EPS)
    vhat = center * root
    return vhat * gain, vhat, root


def norm_back(dy, gain, vhat, root):
    dgain = jnp.sum(dy * vhat, axis=tuple(range(dy.ndim - 1)))
    e = dy * gain
    dz = root * (
        e
        - jnp.mean(e, axis=-1, keepdims=True)
        - vhat * jnp.mean(e * vhat, axis=-1, keepdims=True)
    )
    return dgain, dz


def mm(spec, a, b):
    return jnp.einsum(spec, a, b, preferred_element_type=F32)


def layer(g1, wqkv, wo, g2, win, wdown, tokens, dout, live):
    m, slot, d = tokens.shape
    heads, size = HEADS, d // HEADS
    scale = size ** (-0.5)
    w1, w2 = win
    lv = live[:, :, None]
    x = tokens.astype(F32)
    y, vhat1, root1 = normed(x, g1)
    a = y.astype(BF16)
    qkv = mm("mtd,de->mte", a, wqkv).reshape(m, slot, 3, heads, size)
    cosine, sine = rope_tables(slot, size)
    q = rotate(qkv[:, :, 0], cosine, sine).astype(BF16)
    k = rotate(qkv[:, :, 1], cosine, sine).astype(BF16)
    v = qkv[:, :, 2].astype(BF16)
    s = mm("mqhd,mkhd->mhqk", q, k) * scale
    s = jnp.where(live[:, None, None, :] > 0, s, -1e30)
    p = jax.nn.softmax(s, axis=-1)
    pb = p.astype(BF16)
    o = mm("mhqk,mkhd->mqhd", pb, v).astype(BF16).reshape(m, slot, d)
    h = x + lv * mm("mte,ed->mtd", o, wo)
    y, vhat2, root2 = normed(h, g2)
    hn = y.astype(BF16)
    z1 = mm("mtd,df->mtf", hn, w1)
    z2 = mm("mtd,df->mtf", hn, w2)
    cdf = 0.5 * (1.0 + lax.erf(z1 * (0.5**0.5)))
    pdf = jnp.exp(-0.5 * z1 * z1) * 0.3989422804014327
    act = z1 * cdf
    gg = (act * z2).astype(BF16)
    mixed = (h + lv * mm("mtf,fd->mtd", gg, wdown)).astype(BF16)

    up = dout.astype(F32)
    dy2 = (lv * up).astype(BF16)
    g_down = mm("mtf,mtd->fd", gg, dy2)
    dgg = mm("mtd,fd->mtf", dy2, wdown)
    dw1 = (dgg * z2 * (cdf + z1 * pdf)).astype(BF16)
    dw2 = (dgg * act).astype(BF16)
    g_in = (mm("mtd,mtf->df", hn, dw1), mm("mtd,mtf->df", hn, dw2))
    dhn = mm("mtf,df->mtd", dw1, w1) + mm("mtf,df->mtd", dw2, w2)
    g_g2, dhv = norm_back(dhn, g2, vhat2, root2)
    dh = up + dhv
    dy1 = (lv * dh).astype(BF16)
    g_out = mm("mte,mtd->ed", o, dy1)
    do = mm("mtd,ed->mte", dy1, wo).astype(BF16).reshape(m, slot, heads, size)
    dp = mm("mqhd,mkhd->mhqk", do, v)
    ds = (p * (dp - jnp.sum(dp * p, axis=-1, keepdims=True))).astype(BF16)
    dq = mm("mhqk,mkhd->mqhd", ds, k) * scale
    dk = mm("mhqk,mqhd->mkhd", ds, q) * scale
    dv = mm("mhqk,mqhd->mkhd", pb, do)
    dqkv = jnp.stack([rotate(dq, cosine, -sine), rotate(dk, cosine, -sine), dv], axis=2)
    dqkv = dqkv.reshape(m, slot, 3 * d).astype(BF16)
    g_qkv = mm("mtd,mte->de", a, dqkv)
    da = mm("mte,de->mtd", dqkv, wqkv)
    g_g1, dxv = norm_back(da, g1, vhat1, root1)
    gtok = (dh + dxv).astype(BF16)
    return mixed, gtok, (g_g1, g_qkv, g_out, g_g2, g_in, g_down)


def plain(tokens, cotangent, deal, lengths, ln1_gain, w_qkv, w_out, ln2_gain, w_in, w_down):
    slot = tokens.shape[2] * lax.axis_size("fsdp")
    me = lax.axis_index("fsdp")

    def spread(rows):
        return lax.all_to_all(rows, "fsdp", split_axis=1, concat_axis=2, tiled=True)[:, 0]

    def back(rows):
        return lax.all_to_all(rows[:, None], "fsdp", split_axis=2, concat_axis=1, tiled=True)

    def whole(shard):
        return lax.all_gather(shard.astype(BF16), "fsdp", axis=0, tiled=True)

    table = lax.all_gather(lengths[:, 0], "fsdp", axis=1, tiled=True)
    mine = lax.dynamic_slice_in_dim(deal[:, 0], me, 1, axis=1)
    pick = jnp.arange(table.shape[1], dtype=jnp.int32)[None, :] == mine
    length = jnp.sum(jnp.where(pick, table, 0), axis=1, keepdims=True)
    live = (jnp.arange(slot, dtype=jnp.int32)[None, :] < length).astype(F32)
    win = jnp.split(whole(w_in), 2, axis=1)
    mixed, gtok, grads = layer(
        whole(ln1_gain).astype(F32), whole(w_qkv), whole(w_out), whole(ln2_gain).astype(F32), win, whole(w_down),
        spread(tokens), spread(cotangent), live,
    )
    g_g1, g_qkv, g_out, g_g2, g_in, g_down = grads

    def owned(part):
        part = lax.psum_scatter(part, "fsdp", scatter_dimension=0, tiled=True)
        return lax.psum(part, "rep")

    g_in = jnp.concatenate(g_in, axis=1)
    return (back(mixed), back(gtok)) + tuple(owned(g) for g in (g_g1, g_qkv, g_out, g_g2, g_in, g_down))


class Unit:
    def __init__(self, mat, rows, real, col, width):
        self.mat, self.rows, self.real, self.col, self.width = mat, rows, real, col, width


def split_rows(rows, share):
    a = max(16, round(rows * share / 16) * 16)
    return a, rows - 2 * a


def make_units(d, ffs, n, widths):
    units = []
    pad = -(-ffs // 16) * 16
    totals = {"qkv": 3 * d // 2, "o": d // 2, "i": n * pad, "d": d // 2}
    for mat, parts in widths:
        rows, real = (pad, ffs) if mat == "d" else (d // n, d // n)
        width = totals[mat] // parts
        units += [Unit(mat, rows, real, i * width, width) for i in range(parts)]
    return units


class Place:
    def __init__(self):
        self.f = lax.axis_index("fsdp")
        self.r = lax.axis_index("rep")
        self.z, self.y = lax.div(self.f, 2), lax.rem(self.f, 2)
        self.x, self.c = lax.div(self.r, 2), lax.rem(self.r, 2)
        z = self.z
        self.zs = [z + 1 - 2 * lax.rem(z, 2), lax.rem(z + 2, 4), 3 - z]
        self.yn = self.f + 1 - 2 * self.y
        self.xn = lax.rem(self.r + 2, 4)
        self.cn = self.r + 1 - 2 * self.c

    def others(self):
        return [lax.rem(self.f + k, 8) for k in range(1, 8)]


def at(offset, size, unit=16):
    return pl.ds(pl.multiple_of(offset, unit), size)


def remote(src, dst, send, recv, f, r):
    return pltpu.make_async_remote_copy(
        src_ref=src, dst_ref=dst, send_sem=send, recv_sem=recv,
        device_id={"fsdp": f, "rep": r}, device_id_type=MESH,
    )


def meet(me):
    barrier = pltpu.get_barrier_semaphore()
    friends = [(f, me.r) for f in me.others()] + [(me.f, lax.rem(me.r + k, 4)) for k in (1, 2, 3)]
    for f, r in friends:
        pl.semaphore_signal(barrier, inc=1, device_id={"fsdp": f, "rep": r}, device_id_type=MESH)
    pl.semaphore_wait(barrier, len(friends))


class Gather:
    SHARE = 0.375

    def __init__(self, me, units, shards, whole, recv, send, zsend, local):
        self.me, self.units, self.shards, self.whole = me, units, shards, whole
        self.recv, self.send, self.zsend, self.local = recv, send, zsend, local
        self.pending = []

    def piece(self, u, ref, j, c, part, own=False):
        unit, x = self.units[u], self.me.x
        a, b = split_rows(unit.rows, self.SHARE)
        off = [x * a, x * (unit.rows - a), (1 - x) * (unit.rows - a)][part]
        size = [a + b, a, a][part]
        return ref.at[c, at((0 if own else j * unit.rows) + off, size)]

    def copy(self, u, j, kind, part, f, r, src=None):
        me = self.me
        dst = self.piece(u, self.whole[u], j, me.c, part)
        cp = remote(dst if src is None else src, dst, self.send.at[u, j, kind], self.recv.at[u, j, kind], f, r)
        cp.start()
        self.pending.append(cp)

    def start(self, u):
        me, unit = self.me, self.units[u]
        own = self.piece(u, self.shards[u], me.f, me.c, 0, own=True)
        for k, z in enumerate(me.zs):
            cp = remote(
                own, self.piece(u, self.whole[u], me.f, me.c, 0), self.zsend.at[u, k], self.recv.at[u, me.f, 0],
                2 * z + me.y, me.r,
            )
            cp.start()
            self.pending.append(cp)
            if k == 0:
                self.copy(u, me.f, 0, 0, me.yn, me.r, src=own)
        cp = pltpu.make_async_copy(
            self.shards[u], self.whole[u].at[:, at(me.f * unit.rows, unit.rows)], self.local.at[u]
        )
        cp.start()
        self.pending.append(cp)

    def arrived(self, u, j, kind, part, c):
        ref = self.piece(u, self.whole[u], j, c, part)
        remote(ref, ref, self.send.at[u, j, kind], self.recv.at[u, j, kind], self.me.f, self.me.r).wait_recv()

    def inplane(self, u, k, over_y):
        me = self.me
        z = me.zs[k] if k < 3 else me.z
        j = 2 * z + (1 - me.y if over_y else me.y)
        self.arrived(u, j, 0, 0, me.c)
        if not over_y:
            self.copy(u, j, 0, 0, me.yn, me.r)
        self.copy(u, j, 1, 1, me.f, me.xn)
        self.copy(u, j, 2, 0, me.f, me.cn)

    def over_x(self, u, k):
        me = self.me
        j = lax.rem(me.f + k, 8)
        self.arrived(u, j, 1, 2, me.c)
        self.copy(u, j, 3, 2, me.f, me.cn)

    def complete(self, u):
        me = self.me
        for k in range(1, 8):
            j = lax.rem(me.f + k, 8)
            self.arrived(u, j, 2, 0, 1 - me.c)
            self.arrived(u, j, 3, 2, 1 - me.c)

    ROUTE = ((0, False), (3, True), (1, False), (2, False), (0, True), (1, True), (2, True))

    def finish(self):
        for cp in self.pending:
            cp.wait_send() if cp.is_remote else cp.wait()


def gather_kernel(units, tok, cot, small, *refs):
    n = len(units)
    shards, refs = refs[:n], refs[n:]
    dealt_tok, dealt_cot, smalls = refs[:3]
    whole, refs = refs[3 : 3 + n], refs[3 + n :]
    recv, send, zsend, local, asend, arecv, alocal, ssend, srecv = refs
    me = Place()
    meet(me)
    g = Gather(me, units, shards, whole, recv, send, zsend, local)
    micro, _, rows, _ = tok.shape
    sends, locals_ = [], []
    for k, f in enumerate(me.others()):
        cp = remote(small, smalls.at[me.f], ssend.at[k], srecv.at[k], f, me.r)
        cp.start()
        sends.append(cp)
    cp = pltpu.make_async_copy(small, smalls.at[me.f], alocal.at[4])
    cp.start()
    locals_.append(cp)

    def deal(which, src, dst):
        for m in range(micro):
            cp = pltpu.make_async_copy(src.at[m, me.f], dst.at[m, at(me.f * rows, rows)], alocal.at[which * 2 + m])
            cp.start()
            locals_.append(cp)
            for k, f in enumerate(me.others()):
                cp = remote(
                    src.at[m, f], dst.at[m, at(me.f * rows, rows)], asend.at[which, m, k], arecv.at[which, m, k], f, me.r
                )
                cp.start()
                sends.append(cp)

    deal(0, tok, dealt_tok)
    g.start(0)
    g.start(1)
    for u in range(n):
        for i, (k, over_y) in enumerate(g.ROUTE):
            g.inplane(u, k, over_y)
            if i == 3 and u + 2 < n:
                g.start(u + 2)
        if u == 1:
            deal(1, cot, dealt_cot)
        for k in range(1, 8):
            g.over_x(u, k)
    for u in range(n):
        g.complete(u)
    for cp in sends:
        cp.wait_send()
    for k in range(7):
        src = lax.rem(me.f + 7 - k, 8)
        remote(small, smalls.at[src], ssend.at[k], srecv.at[k], me.f, me.r).wait_recv()
        for which, (s, dst) in enumerate(((tok, dealt_tok), (cot, dealt_cot))):
            for m in range(micro):
                remote(
                    s.at[m, 0], dst.at[m, at(src * rows, rows)], asend.at[which, m, k], arecv.at[which, m, k], me.f, me.r
                ).wait_recv()
    for cp in locals_:
        cp.wait()
    g.finish()


def gather_call(units, tok, cot, small, shards):
    micro, n, rows, d = tok.shape
    u = len(units)
    any_ = pl.BlockSpec(memory_space=pl.ANY)
    return pl.pallas_call(
        functools.partial(gather_kernel, units),
        out_shape=[
            jax.ShapeDtypeStruct((micro, n * rows, d), BF16),
            jax.ShapeDtypeStruct((micro, n * rows, d), BF16),
            jax.ShapeDtypeStruct((n, 8, 128), F32),
        ]
        + [jax.ShapeDtypeStruct((2, n * t.rows, t.width), BF16) for t in units],
        in_specs=[any_] * (3 + u),
        out_specs=[any_] * (3 + u),
        scratch_shapes=[
            pltpu.SemaphoreType.DMA((u, 8, 4)),
            pltpu.SemaphoreType.DMA((u, 8, 4)),
            pltpu.SemaphoreType.DMA((u, 3)),
            pltpu.SemaphoreType.DMA((u,)),
            pltpu.SemaphoreType.DMA((2, micro, 7)),
            pltpu.SemaphoreType.DMA((2, micro, 7)),
            pltpu.SemaphoreType.DMA((5,)),
            pltpu.SemaphoreType.DMA((7,)),
            pltpu.SemaphoreType.DMA((7,)),
        ],
        compiler_params=pltpu.CompilerParams(collective_id=0, has_side_effects=True, vmem_limit_bytes=32 * MIB),
    )(tok, cot, small, *shards)


def add_rows(dst, doff, src, soff, rows):
    def step(i, _):
        d = at(doff + i * 16, 16)
        dst[d, :] = (dst[d, :].astype(F32) + src[at(soff + i * 16, 16), :].astype(F32)).astype(BF16)
        return 0

    lax.fori_loop(0, rows // 16, step, 0)


class Reduce:
    SHARE = 0.25

    def __init__(self, me, units, bufs, outs, sems):
        self.me, self.units, self.bufs, self.outs, self.sems = me, units, bufs, outs, sems
        z, y = me.z, me.y
        zs = list(me.zs) + [z]
        self.order = [2 * k + 1 - y for k in zs] + [2 * k + y for k in zs]
        self.waits = []

    def parts(self, u):
        unit = self.units[u]
        a, b = split_rows(unit.rows, self.SHARE)
        return unit.rows, a, b

    def send(self, src, dst, kind, u, k, f, r, recv_k=None):
        s, r_ = self.sems[kind]
        cp = remote(src, dst, s.at[u, k], r_.at[u, k if recv_k is None else recv_k], f, r)
        cp.start()
        self.waits.append(cp)

    def wait(self, ref, kind, u, k):
        s, r_ = self.sems[kind]
        remote(ref, ref, s.at[u, k], r_.at[u, k], self.me.f, self.me.r).wait_recv()

    def to_sibling(self, u, i, src):
        rows, a, b = self.parts(u)
        me, j = self.me, self.order[i]
        self.send(src, self.bufs["sib"][u].at[at(j * rows, rows)], "core", u, i, me.f, me.cn)

    def chip_sum(self, u, i):
        rows, a, b = self.parts(u)
        me, j = self.me, self.order[i]
        own, sib = self.bufs["own"][u], self.bufs["sib"][u]
        self.wait(sib.at[at(j * rows, rows)], "core", u, i)
        add_rows(own, j * rows, sib, j * rows, rows)
        self.send(
            own.at[at(j * rows + (1 - me.x) * (rows - a), a)], self.bufs["xr"][u].at[i], "x", u, i, me.f, me.xn
        )

    def x_sum(self, u, i):
        rows, a, b = self.parts(u)
        me, j = self.me, self.order[i]
        own, xr = self.bufs["own"][u], self.bufs["xr"][u]
        self.wait(xr.at[i], "x", u, i)
        add_rows(own, j * rows + me.x * (rows - a), xr.at[i], 0, a)
        if i < 4:
            self.send(
                own.at[at(j * rows + me.x * a, a + b)], self.bufs["yr"][u].at[i], "y", u, i, me.yn, me.r
            )

    def y_sum(self, u, i):
        rows, a, b = self.parts(u)
        me, j = self.me, self.order[i]
        own, yr = self.bufs["own"][u], self.bufs["yr"][u]
        self.wait(yr.at[i - 4], "y", u, i - 4)
        add_rows(own, j * rows + me.x * a, yr.at[i - 4], 0, a + b)
        if i < 7:
            self.send(own.at[at(j * rows + me.x * a, a + b)], self.bufs["zr"][u].at[i - 4], "z", u, i - 4, j, me.r)

    def owner_sum(self, u):
        rows, a, b = self.parts(u)
        me = self.me
        own, zr, xs = self.bufs["own"][u], self.bufs["zr"][u], self.bufs["xs"][u]
        for k in range(3):
            self.wait(zr.at[k], "z", u, k)
        base = me.f * rows + me.x * a

        def step(i, _):
            t = at(i * 16, 16)
            total = own[at(base + i * 16, 16), :].astype(F32)
            for k in range(3):
                total = total + zr[k, t, :].astype(F32)
            xs[t, :] = total.astype(BF16)
            return 0

        lax.fori_loop(0, (a + b) // 16, step, 0)
        self.send(xs, self.bufs["xf"][u], "xf", u, 0, me.f, me.xn)

    def final(self, u):
        rows, a, b = self.parts(u)
        me, unit = self.me, self.units[u]
        xs, xf, fin = self.bufs["xs"][u], self.bufs["xf"][u], self.bufs["fin"][u]
        x = me.x
        self.wait(xf, "xf", u, 0)

        def mine(i, _):
            fin[at(x * (rows - a) + i * 16, 16), :] = xs[at(x * b + i * 16, 16), :].astype(F32)
            fin[at((1 - x) * (rows - a) + i * 16, 16), :] = xf[at((1 - x) * b + i * 16, 16), :].astype(F32)
            return 0

        def both(i, _):
            fin[at(a + i * 16, 16), :] = (
                xs[at((1 - x) * a + i * 16, 16), :].astype(F32) + xf[at(x * a + i * 16, 16), :].astype(F32)
            )
            return 0

        lax.fori_loop(0, a // 16, mine, 0)
        lax.fori_loop(0, b // 16, both, 0)
        src, dst = self.out_place(u, me.c)
        self.send(src, dst, "out", u, 0, me.f, me.cn)
        cp = pltpu.make_async_copy(src, dst, self.sems["local"].at[u])
        cp.start()
        self.waits.append(cp)

    def out_place(self, u, c):
        unit = self.units[u]
        half = self.outs[unit.mat].shape[1] // 2
        src = self.bufs["fin"][u].at[pl.ds(0, unit.real)]
        return src, self.outs[unit.mat].at[:, at(c * half + unit.col, unit.width, 128)]

    def drain(self):
        me = self.me
        for u in range(len(self.units)):
            src, dst = self.out_place(u, 1 - me.c)
            s, r_ = self.sems["out"]
            remote(src, dst, s.at[u, 0], r_.at[u, 0], me.f, me.r).wait_recv()
        for cp in self.waits:
            cp.wait_send() if cp.is_remote else cp.wait()


KINDS = ("core", "x", "y", "z", "xf", "out")


def reduce_kernel(units, mixed, gtok, gsmall, *refs):
    n = len(units)
    partial, refs = refs[:n], refs[n:]
    out_mixed, out_gtok, out_small, out_qkv, out_o, out_i, out_d = refs[:7]
    refs = refs[7:]
    bufs = {}
    for name in ("own", "sib", "xr", "yr", "zr", "xs", "xf", "fin"):
        bufs[name], refs = refs[:n], refs[n:]
    slots, reps, svm = refs[:3]
    refs = refs[3:]
    sems = {}
    for kind in KINDS:
        sems[kind], refs = (refs[0], refs[1]), refs[2:]
    sems["local"] = refs[0]
    load, asend, arecv, alocal, ssend, srecv, rsend, rrecv, slocal = refs[1:]
    me = Place()
    meet(me)
    red = Reduce(me, units, bufs, dict(qkv=out_qkv, o=out_o, i=out_i, d=out_d), sems)
    micro, rows = mixed.shape[0], out_mixed.shape[2]
    loads = []
    for u, unit in enumerate(units):
        cp = pltpu.make_async_copy(partial[u].at[me.c], bufs["own"][u], load.at[u])
        cp.start()
        loads.append(cp)
    for u, unit in enumerate(units):
        for i in range(8):
            j = red.order[i]
            red.to_sibling(u, i, partial[u].at[1 - me.c, at(j * unit.rows, unit.rows)])
    sends = []
    for k, f in enumerate(me.others()):
        cp = remote(gsmall.at[f], slots.at[me.f], ssend.at[k], srecv.at[k], f, me.r)
        cp.start()
        sends.append(cp)
    own_small = pltpu.make_async_copy(gsmall.at[me.f], slots.at[me.f], slocal.at[0])
    own_small.start()
    locals_ = []
    for which, (src, dst) in enumerate(((mixed, out_mixed), (gtok, out_gtok))):
        for m in range(micro):
            cp = pltpu.make_async_copy(src.at[m, at(me.f * rows, rows)], dst.at[m, me.f], alocal.at[which * 2 + m])
            cp.start()
            locals_.append(cp)
            for k, f in enumerate(me.others()):
                cp = remote(
                    src.at[m, at(f * rows, rows)], dst.at[m, me.f], asend.at[which, m, k], arecv.at[which, m, k], f, me.r
                )
                cp.start()
                sends.append(cp)

    def small_reduce():
        own_small.wait()
        for k in range(7):
            remote(slots.at[0], slots.at[0], ssend.at[k], srecv.at[k], me.f, me.r).wait_recv()
        total = slots[0]
        for j in range(1, 8):
            total = total + slots[j]
        svm[...] = total
        reps[me.r] = total
        for k in range(3):
            cp = remote(svm, reps.at[me.r], rsend.at[k], rrecv.at[k], me.f, lax.rem(me.r + k + 1, 4))
            cp.start()
            sends.append(cp)

    def small_final():
        for k in range(3):
            remote(svm, reps.at[0], rsend.at[k], rrecv.at[k], me.f, me.r).wait_recv()
        svm2 = reps[0] + reps[1] + reps[2] + reps[3]
        slots[0] = svm2
        cp = pltpu.make_async_copy(slots.at[0], out_small, slocal.at[1])
        cp.start()
        locals_.append(cp)

    def stage(s, u):
        if s == 0:
            loads[u].wait()
            for i in range(8):
                red.chip_sum(u, i)
        elif s == 1:
            for i in range(8):
                red.x_sum(u, i)
                if i >= 4:
                    red.y_sum(u, i)
        elif s == 2:
            red.owner_sum(u)
        else:
            red.final(u)

    for t in range(n + 3):
        for s in range(4):
            u = t - s
            if 0 <= u < n:
                stage(s, u)
        if t == 1:
            small_reduce()
        if t == 3:
            small_final()
    red.drain()
    for cp in sends:
        cp.wait_send()
    for k in range(7):
        for which, dst in enumerate((out_mixed, out_gtok)):
            for m in range(micro):
                remote(dst.at[m, 0], dst.at[m, 0], asend.at[which, m, k], arecv.at[which, m, k], me.f, me.r).wait_recv()
    for cp in locals_:
        cp.wait()


def reduce_call(units, d, ffs, mixed, gtok, gsmall, partial):
    n = 8
    micro, slot, _ = mixed.shape
    rows = slot // n
    u = len(units)
    any_ = pl.BlockSpec(memory_space=pl.ANY)
    ab = [split_rows(t.rows, Reduce.SHARE) for t in units]
    pad = n * (-(-ffs // 16) * 16)
    scratch = (
        [pltpu.VMEM((n * t.rows, t.width), BF16) for t in units]
        + [pltpu.VMEM((n * t.rows, t.width), BF16) for t in units]
        + [pltpu.VMEM((8, a, t.width), BF16) for t, (a, b) in zip(units, ab)]
        + [pltpu.VMEM((4, a + b, t.width), BF16) for t, (a, b) in zip(units, ab)]
        + [pltpu.VMEM((3, a + b, t.width), BF16) for t, (a, b) in zip(units, ab)]
        + [pltpu.VMEM((a + b, t.width), BF16) for t, (a, b) in zip(units, ab)]
        + [pltpu.VMEM((a + b, t.width), BF16) for t, (a, b) in zip(units, ab)]
        + [pltpu.VMEM((t.rows, t.width), F32) for t in units]
        + [pltpu.VMEM((8, 8, 128), F32), pltpu.VMEM((4, 8, 128), F32), pltpu.VMEM((8, 128), F32)]
        + [
            pltpu.SemaphoreType.DMA((u, size))
            for size in (8, 8, 4, 3, 1, 1)
            for _ in range(2)
        ]
        + [
            pltpu.SemaphoreType.DMA((u,)),
            pltpu.SemaphoreType.DMA((u,)),
            pltpu.SemaphoreType.DMA((2, micro, 7)),
            pltpu.SemaphoreType.DMA((2, micro, 7)),
            pltpu.SemaphoreType.DMA((4,)),
            pltpu.SemaphoreType.DMA((7,)),
            pltpu.SemaphoreType.DMA((7,)),
            pltpu.SemaphoreType.DMA((3,)),
            pltpu.SemaphoreType.DMA((3,)),
            pltpu.SemaphoreType.DMA((2,)),
        ]
    )
    return pl.pallas_call(
        functools.partial(reduce_kernel, units),
        out_shape=[
            jax.ShapeDtypeStruct((micro, n, rows, d), BF16),
            jax.ShapeDtypeStruct((micro, n, rows, d), BF16),
            jax.ShapeDtypeStruct((8, 128), F32),
            jax.ShapeDtypeStruct((d // n, 3 * d), F32),
            jax.ShapeDtypeStruct((d // n, d), F32),
            jax.ShapeDtypeStruct((d // n, 2 * pad), F32),
            jax.ShapeDtypeStruct((ffs, d), F32),
        ],
        in_specs=[any_] * (3 + u),
        out_specs=[any_] * 7,
        scratch_shapes=scratch,
        compiler_params=pltpu.CompilerParams(collective_id=1, has_side_effects=True, vmem_limit_bytes=60 * MIB),
    )(mixed, gtok, gsmall, *partial)


def padded(columns, n, pad):
    size = columns.shape[-1] // n
    blocks = columns.reshape(columns.shape[:-1] + (n, size))
    blocks = jnp.pad(blocks, [(0, 0)] * (blocks.ndim - 1) + [(0, pad - size)])
    return blocks.reshape(columns.shape[:-1] + (n * pad,))


def unpadded(columns, n, size):
    blocks = columns.reshape(columns.shape[:-1] + (n, columns.shape[-1] // n))
    return blocks[..., :size].reshape(columns.shape[:-1] + (n * size,))


GATHER_WIDTHS = (("qkv", 2), ("o", 1), ("i", 3), ("d", 1))
REDUCE_WIDTHS = (("d", 1), ("i", 3), ("o", 1), ("qkv", 2))


def routed(tokens, cotangent, deal, lengths, ln1_gain, w_qkv, w_out, ln2_gain, w_in, w_down):
    n = 8
    micro, _, part, d = tokens.shape
    slot = part * n
    ffs = w_down.shape[0]
    pad = -(-ffs // 16) * 16
    units = make_units(d, ffs, n, GATHER_WIDTHS)
    shard = {
        "qkv": jnp.stack(jnp.split(w_qkv.astype(BF16), 2, axis=1)),
        "o": jnp.stack(jnp.split(w_out.astype(BF16), 2, axis=1)),
        "i": padded(jnp.stack(jnp.split(w_in.astype(BF16), 2, axis=1)), n, pad),
        "d": jnp.pad(jnp.stack(jnp.split(w_down.astype(BF16), 2, axis=1)), ((0, 0), (0, pad - ffs), (0, 0))),
    }
    shards = [shard[t.mat][:, :, t.col : t.col + t.width] for t in units]
    gain = [g.astype(BF16).astype(F32)[None] for g in (ln1_gain, ln2_gain)]
    len_row = jnp.pad(lengths[:, 0, 0].astype(F32), (0, 128 - micro))[None]
    small = jnp.concatenate(gain + [len_row, jnp.zeros((5, 128), F32)])
    outs = gather_call(units, tokens, cotangent, small, shards)
    tok, dout, smalls, whole = outs[0], outs[1], outs[2], outs[3:]
    full = {}
    for t, w in zip(units, whole):
        full.setdefault(t.mat, []).append(w)
    full = {k: jnp.concatenate(v, axis=2) for k, v in full.items()}
    flat = lambda w: jnp.concatenate([w[0], w[1]], axis=1)
    g1, g2 = smalls[:, 0].reshape(d), smalls[:, 1].reshape(d)
    me = lax.axis_index("fsdp")
    mine = lax.dynamic_slice_in_dim(deal[:, 0], me, 1, axis=1)
    pick = jnp.arange(n, dtype=jnp.int32)[None, :] == mine
    length = jnp.sum(jnp.where(pick, smalls[:, 2, :micro].T, 0.0), axis=1, keepdims=True)
    live = (jnp.arange(slot, dtype=jnp.int32).astype(F32)[None, :] < length).astype(F32)
    mixed, gtok, grads = layer(
        g1, flat(full["qkv"]), flat(full["o"]), g2, (full["i"][0], full["i"][1]), flat(full["d"]), tok, dout, live
    )
    g_g1, g_qkv, g_out, g_g2, g_in, g_down = grads
    halves = lambda g: jnp.stack(jnp.split(g.astype(BF16), 2, axis=1))
    grad = {"qkv": halves(g_qkv), "o": halves(g_out), "i": jnp.stack([g.astype(BF16) for g in g_in]), "d": halves(g_down)}
    runits = make_units(d, ffs, n, REDUCE_WIDTHS)
    partial = [grad[t.mat][:, :, t.col : t.col + t.width] for t in runits]
    gsmall = jnp.pad(jnp.stack([g_g1.reshape(n, 128), g_g2.reshape(n, 128)], axis=1), ((0, 0), (0, 6), (0, 0)))
    o_mixed, o_gtok, o_small, o_qkv, o_out, o_in, o_down = reduce_call(runits, d, ffs, mixed, gtok, gsmall, partial)
    o_in = jnp.concatenate([unpadded(h, n, ffs) for h in jnp.split(o_in, 2, axis=1)], axis=1)
    return o_mixed, o_gtok, o_small[0], o_qkv, o_out, o_small[1], o_in, o_down


def solution(mesh):
    small = mesh.shape["fsdp"] == 8 and mesh.shape["rep"] == 4
    rows = P(None, "rep", "fsdp", None)
    return jax.shard_map(
        routed if small else plain,
        mesh=mesh,
        in_specs=(
            rows, rows, P(None, "rep", None), P(None, "rep", "fsdp"),
            P("fsdp"), P("fsdp", None), P("fsdp", None), P("fsdp"), P("fsdp", None), P("fsdp", None),
        ),
        out_specs=(rows, rows, P("fsdp"), P("fsdp", None), P("fsdp", None), P("fsdp"), P("fsdp", None), P("fsdp", None)),
        check_vma=False,
    )
```

time: 1420 us -> 426 us (0.30)
  waiting for transfers between devices: 1100 us -> 0 us
  Pallas kernels: 0 us -> 285 us
  matrix products: 119 us -> 46 us
  blocking collectives: 72.5 us -> 0 us
  local copies, waits for them, and re-layouts: 37 us -> 64.6 us
  starting transfers between devices: 24.5 us -> 0 us
  other arithmetic: 42.7 us -> 24.4 us
  between operations: 16.2 us -> 1.64 us
    reduce_scatter x4 -> x0, waiting for transfers between devices: 762 us -> none  [on_device(): lax.psum_scatter(totals, 'fsdp', scatter_dimension=0, tiled=True)]
    all_gather x4 -> x0, waiting for transfers between devices: 287 us -> none  [the longest x1 146 us: on_device(): lax.all_gather(shards[4], 'fsdp', axis=0, tiled=True)]
    pallas_call x0 -> x2, Pallas kernels: none -> 285 us  [the longest x1 145 us: reduce_call(): pl.pallas_call(functools.partial(reduce_kernel, units), out_shape=[jax.Sh...]
    dot_general x36 -> x20, matrix products: 119 us -> 43.9 us  [mm(): return jnp.einsum(spec, a, b, preferred_element_type=F32)]
    all_gather x2 -> x0, blocking collectives: 45.1 us -> none  [the longest x1 34.4 us: on_device(): lax.all_gather(shards[3], 'fsdp', axis=0, tiled=True)]
    psum x1 -> x0, waiting for transfers between devices: 26.6 us -> none  [on_device(): lax.psum(shortened(owned_total), 'rep')]
    unnamed x191 -> x113, local copies, waits for them, and re-layouts: 15.9 us -> 42 us
    convert_element_type x28 -> x9, other arithmetic: 29.2 us -> 4 us  [the longest x1 1.22 us: layer(): gtok = (dh + dxv).astype(BF16)]
  transfers between devices with their start and end apart: 13 -> 0, of which waited for: 10 -> 0; matrix products, arithmetic and copies ran while one was open for 9% -> 0% of each run, Pallas kernels for 0% -> 0%
where the time goes in v1:
time: 426 us; the launch traced here: 421 us
  Pallas kernels  285 us (67%)
  local copies, waits for them, and re-layouts  64.6 us (15%)
  matrix products  46 us (11%)
  other arithmetic  24.4 us (6%)
    pallas_call x1, Pallas kernels, reduce_call(): pl.pallas_call(functools.partial(reduce_kernel, units), out_shape=[jax.Sh...  145 us
    pallas_call x1, Pallas kernels, gather_call(): pl.pallas_call(functools.partial(gather_kernel, units), out_shape=[jax.Sh...  140 us
    dot_general x20, matrix products, mm(): return jnp.einsum(spec, a, b, preferred_element_type=F32)  43.9 us
    unnamed x113, local copies, waits for them, and re-layouts  42 us

profile of v1, /device:TPU:17, one launch (start us, length us, event | category | flops | bytes accessed | tf_op | source)
XLA Modules:
  0.0 421.3 jit_solution(9054379601675049072)
XLA Ops:
  3.8 1.1 convert_element_type.130
  6.5 0.8 pad_maximum_fusion.8
  7.3 2.3 copy.33
  10.7 1.0 copy-done.11
  11.7 0.9 copy-done.12
  12.7 1.0 copy-done.13
  13.7 1.0 copy-done.14
  14.7 139.8 %shard_map.161 = (bf16[2,128,1024]{2,1,0:T(8,128)(2,1)S(1)}, bf16[2,128,1024]{2,1,0:T(8,128)(2,1)S(1)}, f32[8,8,128]{2,1,0:T(8,128)S(1)}, bf16[2,1024,768]{2,1,0...) custom-call(bf16[2,8,16,1024]{3,2,1,0:T(8,128)(2,1)S(1)} %copy-done., ...), custom_call_target="tpu_custom_call" | custom-call | tf_op jit(solution)/shard_map/pallas_call | solution.py:338
  154.5 1.8 copy-done.2
  156.3 1.9 copy-done.4
  158.2 1.7 copy-done.6
  159.9 1.7 copy-done.8
  161.5 1.3 copy-done.10
  163.7 3.1 slice_bitcast_fusion.19
  167.1 1.6 copy-done.7
  169.4 2.8 fusion.8
  172.5 1.5 copy-done.27
  174.1 1.1 subtract_convert_fusion.3
  175.2 2.1 fusion.88
  177.4 2.4 convolution_convert_fusion.1
  180.0 0.8 fusion.89
  182.1 1.7 copy-done.5
  183.8 2.3 constant_dynamic-update-slice_fusion.4
  186.1 1.1 copy-done.3
  187.2 2.2 constant_dynamic-update-slice_fusion.3
  189.4 1.2 copy-done.16
  190.6 2.3 constant_dynamic-update-slice_fusion.2
  192.9 4.6 %fusion.6 = f32[2,128,2688]{2,1,0:T(8,128)S(1)} fusion(bf16[2,128,1024]{2,1,0:T(8,128)(2,1)S(1)} %multiply_convert_fusion.4, bf16[2,1024,2688]{2,1,0:T(8,128)(2,1)} %constant_dynamic-update-slice_fusion.2), kind=kOutput, calls=%fused_computation.21 | convolution fusion | flops 1409286144 | bytes 8781824 | tf_op jit(solution)/shard_map/mtd,df->mtf/dot_general | solution.py:51
  197.5 4.2 %fusion.4 = f32[2,128,2688]{2,1,0:T(8,128)S(1)} fusion(bf16[2,128,1024]{2,1,0:T(8,128)(2,1)S(1)} %multiply_convert_fusion.4, bf16[2,1024,2688]{2,1,0:T(8,128)(2,1)} %constant_dynamic-update-slice_fusion.2), kind=kOutput, calls=%fused_computation.19 | convolution fusion | flops 1409286144 | bytes 8781824 | tf_op jit(solution)/shard_map/mtd,df->mtf/dot_general | solution.py:51
  201.7 3.2 multiply_convert_fusion
  204.9 2.4 fusion.32.mixed
  207.4 5.0 %fusion.3 = f32[2,128,1024]{2,1,0:T(8,128)S(1)} fusion(bf16[2,128,2688]{2,1,0:T(8,128)(2,1)S(1)} %get-tuple-element.68, bf16[2,1024,2688]{2,1,0:T(8,128)(2,1)} %constant_dynamic-update-slice_fusion.2), kind=kOutput, calls=%fused_computation.18 | convolution fusion | flops 1409286144 | bytes 7929856 | tf_op jit(solution)/shard_map/mtf,df->mtd/dot_general | solution.py:51
  212.6 1.9 multiply_reduce_fusion.1
  215.0 1.6 fusion.33
  216.5 1.3 copy.44
  217.9 2.6 multiply_reduce_fusion
  220.5 0.8 fusion.40
  222.4 0.8 fusion.26
  224.4 1.5 copy-done.20
  225.9 1.0 copy-done.22
  226.9 2.1 fusion.47
  229.0 1.2 fusion.46.gtok
  231.8 1.5 pad_maximum_fusion.4.refs_4_
  233.7 1.9 bitcast_convert_fusion.3
  236.0 2.9 pad_maximum_fusion.refs_0_
  238.9 1.7 fusion.2
  240.7 1.7 fusion.1
  242.4 4.7 %pad_maximum_fusion.1 = (bf16[2,1024,896]{2,1,0:T(8,128)(2,1)}, bf16[2,1024,896]{2,1,0:T(8,128)(2,1)}, bf16[2,1024,896]{2,1,0:T(8,128)(2,1)}) fusion(bf16[1,1024,2688]{2,1,0:T(8,128)(2,1)S(1)} %fusion.2, bf16[1,1024,2688]{2,1,0:T(8,128)(2,1)S(1)} %fusion.1), kind=kLoop, calls=%fused_computation.28 | loop fusion | flops 22020096 | bytes 22020096 | tf_op jit(solution)/shard_map/stack | solution.py:707
  247.1 2.0 bitcast_convert_fusion
  249.6 2.8 pad_maximum_fusion.2
  252.5 144.8 %shard_map.162 = (bf16[2,8,16,1024]{3,2,1,0:T(8,128)(2,1)}, bf16[2,8,16,1024]{3,2,1,0:T(8,128)(2,1)}, f32[8,128]{1,0:T(8,128)}, f32[128,3072]{1,0:T(8,128)}, f32...) custom-call(bf16[2,128,1024]{2,1,0:T(8,128)(2,1)} %fusion.32.mixed, ...), custom_call_target="tpu_custom_call" | custom-call | tf_op jit(solution)/shard_map/pallas_call | solution.py:638
  397.3 1.3 slice_bitcast_fusion.26
  398.6 3.0 fusion.84
  401.6 2.9 copy.55
  404.5 2.5 slice.131
  406.9 1.5 copy.56
  408.5 1.5 slice.132
  410.2 1.7 pad_maximum_fusion.3
  411.8 3.4 copy.57
  415.3 1.9 copy.95
  417.2 0.8 copy.96
  418.0 1.1 copy.97
  419.2 0.8 copy.98
  420.0 1.1 copy.99
  (144 shorter events, 15.3 us)
Async XLA Ops:
  0.6 0.7 copy-start
  0.6 5.0 %copy-start.32 = (f32[328,1024]{1,0:T(8,128)S(1)}, f32[328,1024]{1,0:T(8,128)}, u32[]{:S(2)}) copy-start(f32[328,1024]{1,0:T(8,128)} %param.19) | copy-start | bytes 4030468
  4.9 1.5 copy-start.25
  10.7 1.0 copy-start.11
  11.7 0.9 copy-start.12
  12.7 1.0 copy-start.13
  13.7 1.0 copy-start.14
  154.5 1.8 copy-start.2
  156.3 1.9 copy-start.4
  158.2 1.7 copy-start.6
  159.9 1.7 copy-start.8
  161.5 1.3 copy-start.10
  163.4 3.4 copy-start.9
  166.8 1.9 copy-start.7
  169.4 2.8 copy-start.19
  169.4 2.8 copy-start.21
  172.2 1.7 copy-start.27
  172.4 1.7 copy-start.43
  177.3 2.5 copy-start.23
  177.3 4.1 slice-start
  177.3 2.5 copy-start.37
  177.3 2.6 copy-start.38
  177.3 4.4 %slice-start.1 = ((s8[5505024]{0:T(1024)(128)(4,1)}), s8[1310720]{0:T(1024)(128)(4,1)S(1)}, s32[]{:S(2)}) async-start(s8[5505024]{0:T(1024)(128)(4,1)} %bitcast.173), calls=%async_computation.1 | async-start | bytes 2621440
  179.8 1.3 copy-start.41
  181.8 2.0 copy-start.5
  183.8 3.4 copy-start.3
  187.2 3.4 copy-start.16
  204.9 2.5 copy-start.17
  204.9 2.5 copy-start.28
  204.9 7.5 %copy-start.30 = (bf16[2,128,2688]{2,1,0:T(8,128)(2,1)}, bf16[2,128,2688]{2,1,0:T(8,128)(2,1)S(1)}, u32[]{:S(2)}) copy-start(bf16[2,128,2688]{2,1,0:T(8,128)(2,1)S(1)} %get-tuple-element.67) | copy-start | bytes 4128772
  204.9 7.5 %slice-start.2 = ((s8[11010048]{0:T(1024)(128)(4,1)}), s8[2621440]{0:T(1024)(128)(4,1)S(1)}, s32[]{:S(2)}) async-start(s8[11010048]{0:T(1024)(128)(4,1)} %bitcast.187), calls=%async_computation.2 | async-start | bytes 5242880
  204.9 7.5 %slice-start.3 = ((s8[11010048]{0:T(1024)(128)(4,1)}), s8[4194304]{0:T(1024)(128)(4,1)S(1)}, s32[]{:S(2)}) async-start(s8[11010048]{0:T(1024)(128)(4,1)} %bitcast.187), calls=%async_computation.3 | async-start | bytes 8388608
  207.4 5.2 %slice-start.4 = ((s8[11010048]{0:T(1024)(128)(4,1)}), s8[4194304]{0:T(1024)(128)(4,1)S(1)}, s32[]{:S(2)}) async-start(s8[11010048]{0:T(1024)(128)(4,1)} %bitcast.187), calls=%async_computation.4 | async-start | bytes 8388608
  217.8 2.6 copy-start.24
  221.3 1.0 copy-start.35
  221.3 1.0 copy-start.36
  221.3 1.8 copy-start.34
  224.0 1.9 copy-start.20
  224.0 2.8 copy-start.22
  229.0 1.9 copy-start.42
  231.8 1.9 copy-start.18
  236.0 2.9 copy-start.31
  238.9 1.7 copy-start.29
  408.4 1.7 copy-start.15
  411.8 5.4 %copy-start.40 = (bf16[2,8,16,1024]{3,2,1,0:T(8,128)(2,1)S(1)}, bf16[2,8,16,1024]{3,2,1,0:T(8,128)(2,1)}, u32[]{:S(2)}) copy-start(bf16[2,8,16,1024]{3,2,1,0:T(8,128)(2,1)} %get-tuple-element.133) | copy-start | bytes 1572868
  411.8 6.2 %copy-start.26 = (f32[128,3072]{1,0:T(8,128)S(1)}, f32[128,3072]{1,0:T(8,128)}, u32[]{:S(2)}) copy-start(f32[128,3072]{1,0:T(8,128)} %get-tuple-element.135) | copy-start | bytes 4718596
  415.3 3.9 copy-start.39
  417.2 2.7 copy-start.33
  417.2 3.8 copy-start.1

commit v2 on v0

v2 whole, which is shorter than its diff:
```python
import functools

import jax
import jax.numpy as jnp
from jax import lax
from jax.experimental import pallas as pl
from jax.experimental.pallas import tpu as pltpu
from jax.sharding import PartitionSpec as P

HEADS = 16
ROPE_BASE = 160000.0
NORM_EPS = 1e-05
MESH = pl.DeviceIdType.MESH
MIB = 1 << 20
BF16 = jnp.bfloat16
F32 = jnp.float32


def rope_tables(slot_count, head_size):
    half_size = head_size // 2
    frequency = ROPE_BASE ** (-(jnp.arange(half_size, dtype=F32) * 2.0 / head_size))
    angles = jnp.arange(slot_count, dtype=F32)[:, None] * frequency[None, :]
    return jnp.cos(angles), jnp.sin(angles)


def rotate(values, cosine, sine):
    front, back = jnp.split(values, 2, axis=-1)
    cosine, sine = cosine[:, None, :], sine[:, None, :]
    return jnp.concatenate([front * cosine - back * sine, back * cosine + front * sine], axis=-1)


def normed(values, gain):
    center = values - jnp.mean(values, axis=-1, keepdims=True)
    root = lax.rsqrt(jnp.mean(center * center, axis=-1, keepdims=True) + NORM_EPS)
    vhat = center * root
    return vhat * gain, vhat, root


def norm_back(dy, gain, vhat, root):
    dgain = jnp.sum(dy * vhat, axis=tuple(range(dy.ndim - 1)))
    e = dy * gain
    dz = root * (
        e
        - jnp.mean(e, axis=-1, keepdims=True)
        - vhat * jnp.mean(e * vhat, axis=-1, keepdims=True)
    )
    return dgain, dz


def mm(spec, a, b):
    return jnp.einsum(spec, a, b, preferred_element_type=F32)


def layer(g1, wqkv, wo, g2, win, wdown, tokens, dout, live):
    m, slot, d = tokens.shape
    heads, size = HEADS, d // HEADS
    scale = size ** (-0.5)
    w1, w2 = win
    lv = live[:, :, None]
    x = tokens.astype(F32)
    y, vhat1, root1 = normed(x, g1)
    a = y.astype(BF16)
    qkv = mm("mtd,de->mte", a, wqkv).reshape(m, slot, 3, heads, size)
    cosine, sine = rope_tables(slot, size)
    q = rotate(qkv[:, :, 0], cosine, sine).astype(BF16)
    k = rotate(qkv[:, :, 1], cosine, sine).astype(BF16)
    v = qkv[:, :, 2].astype(BF16)
    s = mm("mqhd,mkhd->mhqk", q, k) * scale
    s = jnp.where(live[:, None, None, :] > 0, s, -1e30)
    p = jax.nn.softmax(s, axis=-1)
    pb = p.astype(BF16)
    o = mm("mhqk,mkhd->mqhd", pb, v).astype(BF16).reshape(m, slot, d)
    h = x + lv * mm("mte,ed->mtd", o, wo)
    y, vhat2, root2 = normed(h, g2)
    hn = y.astype(BF16)
    z1 = mm("mtd,df->mtf", hn, w1)
    z2 = mm("mtd,df->mtf", hn, w2)
    cdf = 0.5 * (1.0 + lax.erf(z1 * (0.5**0.5)))
    pdf = jnp.exp(-0.5 * z1 * z1) * 0.3989422804014327
    act = z1 * cdf
    gg = (act * z2).astype(BF16)
    mixed = (h + lv * mm("mtf,fd->mtd", gg, wdown)).astype(BF16)

    up = dout.astype(F32)
    dy2 = (lv * up).astype(BF16)
    g_down = mm("mtf,mtd->fd", gg, dy2)
    dgg = mm("mtd,fd->mtf", dy2, wdown)
    dw1 = (dgg * z2 * (cdf + z1 * pdf)).astype(BF16)
    dw2 = (dgg * act).astype(BF16)
    g_in = (mm("mtd,mtf->df", hn, dw1), mm("mtd,mtf->df", hn, dw2))
    dhn = mm("mtf,df->mtd", dw1, w1) + mm("mtf,df->mtd", dw2, w2)
    g_g2, dhv = norm_back(dhn, g2, vhat2, root2)
    dh = up + dhv
    dy1 = (lv * dh).astype(BF16)
    g_out = mm("mte,mtd->ed", o, dy1)
    do = mm("mtd,ed->mte", dy1, wo).astype(BF16).reshape(m, slot, heads, size)
    dp = mm("mqhd,mkhd->mhqk", do, v)
    ds = (p * (dp - jnp.sum(dp * p, axis=-1, keepdims=True))).astype(BF16)
    dq = mm("mhqk,mkhd->mqhd", ds, k) * scale
    dk = mm("mhqk,mqhd->mkhd", ds, q) * scale
    dv = mm("mhqk,mqhd->mkhd", pb, do)
    dqkv = jnp.stack([rotate(dq, cosine, -sine), rotate(dk, cosine, -sine), dv], axis=2)
    dqkv = dqkv.reshape(m, slot, 3 * d).astype(BF16)
    g_qkv = mm("mtd,mte->de", a, dqkv)
    da = mm("mte,de->mtd", dqkv, wqkv)
    g_g1, dxv = norm_back(da, g1, vhat1, root1)
    gtok = (dh + dxv).astype(BF16)
    return mixed, gtok, (g_g1, g_qkv, g_out, g_g2, g_in, g_down)


def plain(tokens, cotangent, deal, lengths, ln1_gain, w_qkv, w_out, ln2_gain, w_in, w_down):
    slot = tokens.shape[2] * lax.axis_size("fsdp")
    me = lax.axis_index("fsdp")

    def spread(rows):
        return lax.all_to_all(rows, "fsdp", split_axis=1, concat_axis=2, tiled=True)[:, 0]

    def back(rows):
        return lax.all_to_all(rows[:, None], "fsdp", split_axis=2, concat_axis=1, tiled=True)

    def whole(shard):
        return lax.all_gather(shard.astype(BF16), "fsdp", axis=0, tiled=True)

    table = lax.all_gather(lengths[:, 0], "fsdp", axis=1, tiled=True)
    mine = lax.dynamic_slice_in_dim(deal[:, 0], me, 1, axis=1)
    pick = jnp.arange(table.shape[1], dtype=jnp.int32)[None, :] == mine
    length = jnp.sum(jnp.where(pick, table, 0), axis=1, keepdims=True)
    live = (jnp.arange(slot, dtype=jnp.int32)[None, :] < length).astype(F32)
    win = jnp.split(whole(w_in), 2, axis=1)
    mixed, gtok, grads = layer(
        whole(ln1_gain).astype(F32), whole(w_qkv), whole(w_out), whole(ln2_gain).astype(F32), win, whole(w_down),
        spread(tokens), spread(cotangent), live,
    )
    g_g1, g_qkv, g_out, g_g2, g_in, g_down = grads

    def owned(part):
        part = lax.psum_scatter(part, "fsdp", scatter_dimension=0, tiled=True)
        return lax.psum(part, "rep")

    g_in = jnp.concatenate(g_in, axis=1)
    return (back(mixed), back(gtok)) + tuple(owned(g) for g in (g_g1, g_qkv, g_out, g_g2, g_in, g_down))


NF, NR, NZ = 8, 4, 4


def at(offset, size, unit=16):
    return pl.ds(pl.multiple_of(offset, unit), size)


def nn(a, b):
    return lax.dot_general(a, b, (((1,), (0,)), ((), ())), preferred_element_type=F32)


def nt(a, b):
    return lax.dot_general(a, b, (((1,), (1,)), ((), ())), preferred_element_type=F32)


def tn(a, b):
    return lax.dot_general(a, b, (((0,), (0,)), ((), ())), preferred_element_type=F32)


def loop(n, body):
    def step(i, carry):
        body(i)
        return carry

    lax.fori_loop(0, n, step, 0)


class Sizes:
    def __init__(self, micro, part, d, ffs):
        self.micro, self.part, self.d, self.ffs = micro, part, d, ffs
        self.slot = part * NF
        self.rows = micro * self.slot
        self.all = NR * self.rows
        self.shard = d // NF
        self.hq = d // NR
        self.ffp = -(-ffs // 16) * 16
        self.tile = 256
        self.ntile = -(-(2 * self.ffp) // self.tile)
        self.fq = self.ntile * self.tile


class Copies:
    def __init__(self, sends, recvs):
        self.sends, self.recvs, self.next = sends, recvs, 0
        self.pending = []

    def take(self, n=1):
        base, self.next = self.next, self.next + n
        return base

    def make(self, src, dst, send, recv, f, r):
        return pltpu.make_async_remote_copy(
            src_ref=src, dst_ref=dst, send_sem=self.sends.at[send], recv_sem=self.recvs.at[recv],
            device_id={"fsdp": f, "rep": r}, device_id_type=MESH,
        )

    def start(self, build, cond=None):
        def go():
            self.make(*build()).start()

        if cond is None:
            go()
        else:
            pl.when(cond)(go)
        self.pending.append((build, cond))

    def arrived(self, ref, recv, f, r):
        self.make(ref, ref, recv, recv, f, r).wait_recv()

    def drain(self, pending=None):
        for build, cond in self.pending if pending is None else pending:

            def go():
                self.make(*build()).wait_send()

            if cond is None:
                go()
            else:
                pl.when(cond)(go)
        if pending is None:
            self.pending = []


def kernel(sz, names, *refs):
    k = dict(zip(names, refs))
    d, rows, slot, micro, part = sz.d, sz.rows, sz.slot, sz.micro, sz.part
    f, r = lax.axis_index("fsdp"), lax.axis_index("rep")
    z, y = lax.div(f, 2), lax.rem(f, 2)
    c = lax.rem(r, 2)
    yn = f + 1 - 2 * y
    cn = r + 1 - 2 * c
    xn = lax.rem(r + 2, 4)
    dn = lax.rem(cn + 2, 4)
    others = [lax.rem(f + i, NF) for i in range(1, NF)]
    cp = Copies(k["sends"], k["recvs"])
    local_pending = []

    def local(src, dst, i):
        copy = pltpu.make_async_copy(src, dst, k["locals"].at[i])
        copy.start()
        return copy

    def block(i):
        return at(i * rows, rows)

    barrier = pltpu.get_barrier_semaphore()
    friends = [(o, r) for o in others] + [(f, o) for o in (cn, xn, dn)]
    for ff, rr in friends:
        pl.semaphore_signal(barrier, inc=1, device_id={"fsdp": ff, "rep": rr}, device_id_type=MESH)

    wq, wo, wi, wd = k["wq"], k["wo"], k["wi"], k["wd"]
    sq, so, si, sd = k["sq"], k["so"], k["si"], k["sd"]
    sh = sz.shard

    class ColumnGather:
        def __init__(self, src, whole, col, width):
            self.src, self.whole, self.cols = src, whole, at(col, width, 128)
            self.recv, self.ysend, self.zsend, self.own = cp.take(NF), cp.take(NF), cp.take(NF), cp.take(3)

        def dst(self, j):
            return self.whole.at[at(j * sh, sh), self.cols]

        def start(self, i):
            src = self.src.at[:, self.cols]
            cp.start(lambda: (src, self.dst(f), self.own, self.recv + f, f + 2, r), z < NZ - 1)
            cp.start(lambda: (src, self.dst(f), self.own + 1, self.recv + f, f - 2, r), z > 0)
            cp.start(lambda: (src, self.dst(f), self.own + 2, self.recv + f, yn, r))
            local_pending.append(local(src, self.dst(f), i))

        def column(self):
            for dist in (1, 2, 3):
                for sign in (-1, 1):
                    j = f + 2 * sign * dist
                    here = (z >= dist) if sign < 0 else (z + dist < NZ)
                    onward = (z < NZ - 1) if sign < 0 else (z > 0)

                    @pl.when(here)
                    def _(j=j):
                        cp.arrived(self.dst(j), self.recv + j, f, r)

                    cp.start(
                        lambda j=j, sign=sign: (self.dst(j), self.dst(j), self.zsend + j, self.recv + j, f - 2 * sign, r),
                        jnp.logical_and(here, onward),
                    )
                    cp.start(lambda j=j: (self.dst(j), self.dst(j), self.ysend + j, self.recv + j, yn, r), here)

        def over_y(self):
            for i in range(NZ):
                j = 2 * i + 1 - y
                cp.arrived(self.dst(j), self.recv + j, f, r)

    class RowGather:
        def __init__(self, src, whole, row, height, pitch):
            self.src, self.whole, self.row, self.height, self.pitch = src, whole, row, height, pitch
            self.recv, self.send, self.own = cp.take(2), cp.take(3), cp.take(3)

        def dst(self, yy):
            return self.whole.at[at(yy * self.pitch + self.row, self.height)]

        def start(self, i):
            src = self.src.at[at(self.row, self.height)]
            mine = z == r
            cp.start(
                lambda: (src, self.dst(y), self.own, self.recv + y, f + 2, r), jnp.logical_and(mine, z < NZ - 1)
            )
            cp.start(lambda: (src, self.dst(y), self.own + 1, self.recv + y, f - 2, r), jnp.logical_and(mine, z > 0))
            cp.start(lambda: (src, self.dst(y), self.own + 2, self.recv + y, yn, r), mine)

            @pl.when(mine)
            def _():
                local(src, self.dst(y), i).wait()

        def column(self):
            @pl.when(z != r)
            def _():
                cp.arrived(self.dst(y), self.recv + y, f, r)

            dst = self.dst(y)
            up = jnp.logical_and(z > r, z < NZ - 1)
            down = jnp.logical_and(z < r, z > 0)
            cp.start(lambda: (dst, dst, self.send, self.recv + y, f + 2, r), up)
            cp.start(lambda: (dst, dst, self.send + 1, self.recv + y, f - 2, r), down)
            cp.start(lambda: (dst, dst, self.send + 2, self.recv + y, yn, r), z != r)

        def over_y(self):
            cp.arrived(self.dst(1 - y), self.recv + 1 - y, f, r)

    t2 = 2 * sz.tile
    g_q = ColumnGather(sq, wq, 0, 3 * sz.hq)
    g_o = [RowGather(so, wo, i * (sh // 2), sh // 2, sh) for i in range(2)]
    g_i = [ColumnGather(si, wi, i * t2, t2) for i in range(sz.ntile)]
    third = sz.ffp // 3
    g_d = [RowGather(sd, wd, i * third, third, sz.ffp) for i in range(3)]

    class Spread:
        def __init__(self, buf):
            self.buf = buf
            self.ids = cp.take(4)
            self.mine = []

        def _start(self, build):
            cp.start(build)
            self.mine.append(cp.pending.pop())

        def start(self):
            own = self.buf.at[block(r)]
            self._start(lambda: (own, own, self.ids + 1, self.ids + 1, f, xn))
            self._start(lambda: (own, own, self.ids, self.ids, f, cn))

        def forward(self):
            got = self.buf.at[block(xn)]
            cp.arrived(got, self.ids + 1, f, r)
            self._start(lambda: (got, got, self.ids + 2, self.ids + 2, f, cn))

        def free(self):
            cp.drain(self.mine)
            self.mine = []

        def done(self):
            cp.arrived(self.buf.at[block(cn)], self.ids, f, r)
            cp.arrived(self.buf.at[block(dn)], self.ids + 2, f, r)

    class Sum:
        def __init__(self, part, sib, xsend, xrecv):
            self.part, self.sib, self.xsend, self.xrecv = part, sib, xsend, xrecv
            self.ids = cp.take(3)
            self.order = (dn, xn, cn, r)
            self.mine = []

        def _start(self, build):
            cp.start(build)
            self.mine.append(cp.pending.pop())

        def ready(self, i):
            if i == 0:
                src = self.part.at[block(dn)]
                self._start(lambda: (src, self.sib.at[0], self.ids, self.ids, f, cn))
            elif i == 1:
                cp.arrived(self.sib.at[0], self.ids, f, r)

                def add(t):
                    s = at(t * 32, 32)
                    self.xsend[s, :] = (self.part[at(xn * rows + t * 32, 32), :] + self.sib[0, s, :]).astype(BF16)

                loop(rows // 32, add)
                self._start(lambda: (self.xsend, self.xrecv, self.ids + 1, self.ids + 1, f, xn))
            elif i == 2:
                src2 = self.part.at[block(cn)]
                self._start(lambda: (src2, self.sib.at[1], self.ids + 2, self.ids + 2, f, cn))

        def done(self):
            cp.arrived(self.sib.at[1], self.ids + 2, f, r)
            cp.arrived(self.xrecv, self.ids + 1, f, r)

        def value(self, t, n):
            s = at(t * n, n)
            return self.part[at(r * rows + t * n, n), :] + self.sib[1, s, :] + self.xrecv[s, :].astype(F32)

        def free(self):
            cp.drain(self.mine)
            self.mine = []

    def add_into(dst, doff, src, n):
        def step(t):
            s = at(doff + t * 16, 16)
            dst[s, :] = (dst[s, :].astype(F32) + src[at(t * 16, 16), :].astype(F32)).astype(BF16)

        loop(n // 16, step)

    class ColumnReduce:
        def __init__(self, grad, yr, zr, fin, out, col, width):
            self.grad, self.yr, self.zr, self.fin, self.out, self.col, self.width = grad, yr, zr, fin, out, col, width
            self.ids, self.zsend, self.zrecv, self.oid = cp.take(NZ), cp.take(NZ), cp.take(NZ + 1), cp.take(4)

        def send(self, j):
            zz = lax.div(j, 2)
            cp.start(lambda: (self.grad.at[at(j * sh, sh)], self.yr.at[zz], self.ids + zz, self.ids + zz, yn, r))

        def add_y(self, j):
            zz = lax.div(j, 2)
            cp.arrived(self.yr.at[zz], self.ids + zz, f, r)
            add_into(self.grad, j * sh, self.yr.at[zz], sh)

        def chain(self, sign, dist):
            j = f + 2 * sign * dist
            here = (z + dist < NZ) if sign > 0 else (z >= dist)
            behind = (z > 0) if sign > 0 else (z < NZ - 1)
            zz = z + sign * dist

            @pl.when(here)
            def _():
                self.add_y(j)

                @pl.when(behind)
                def _():
                    cp.arrived(self.zr.at[zz], self.zrecv + zz, f, r)
                    add_into(self.grad, j * sh, self.zr.at[zz], sh)

            there = NZ if (sign < 0 and dist == 1) else zz
            cp.start(
                lambda: (
                    self.grad.at[at(j * sh, sh)], self.zr.at[there], self.zsend + zz, self.zrecv + there, f + 2 * sign, r
                ),
                here,
            )

        def middle(self):
            for dist in (3, 2, 1):
                for sign in (1, -1):
                    self.chain(sign, dist)

        def final(self, lid):
            self.add_y(f)
            for slot_, cond in ((z, z > 0), (NZ, z < NZ - 1)):

                @pl.when(cond)
                def _(slot_=slot_):
                    cp.arrived(self.zr.at[slot_], self.zrecv + slot_, f, r)
                    add_into(self.grad, f * sh, self.zr.at[slot_], sh)

            src = self.grad.at[at(f * sh, sh)]
            for i, to in enumerate((xn, dn, cn)):
                cp.start(lambda i=i, to=to: (src, self.dst(r), self.oid + i, self.oid + i, f, to))
            local_pending.append(local(src, self.dst(r), lid))

        def dst(self, q):
            return self.out.at[q, :, at(self.col, self.width, 128)]

        def done(self):
            for i, source in enumerate((xn, dn, cn)):
                cp.arrived(self.dst(source), self.oid + i, f, r)

    class RowReduce:
        def __init__(self, grad, yr, zr, out, row, height, pitch):
            self.grad, self.yr, self.zr, self.out = grad, yr, zr, out
            self.row, self.height, self.pitch = row, height, pitch
            self.ids, self.zid, self.oid = cp.take(1), cp.take(4), cp.take(3)

        def rows(self, yy):
            return at(yy * self.pitch + self.row, self.height)

        def send(self):
            src = self.grad.at[self.rows(1 - y)]
            cp.start(lambda: (src, self.yr, self.ids, self.ids, yn, r))

        def middle(self):
            cp.arrived(self.yr, self.ids, f, r)
            mine = y * self.pitch + self.row
            add_into(self.grad, mine, self.yr, self.height)
            src = self.grad.at[self.rows(y)]
            for i, (cond, behind, step) in enumerate(((z < r, z > 0, 2), (z > r, z < NZ - 1, -2))):

                @pl.when(jnp.logical_and(cond, behind))
                def _(i=i):
                    cp.arrived(self.zr.at[i], self.zid + i, f, r)
                    add_into(self.grad, mine, self.zr.at[i], self.height)

                cp.start(
                    lambda i=i, step=step: (src, self.zr.at[i], self.zid + 2 + i, self.zid + i, f + step, r), cond
                )

        def dst(self):
            return self.out.at[at(self.row, self.height)]

        def final(self, lid):
            mine = y * self.pitch + self.row
            owner = z == r
            for i, cond in enumerate((z > 0, z < NZ - 1)):

                @pl.when(jnp.logical_and(owner, cond))
                def _(i=i):
                    cp.arrived(self.zr.at[i], self.zid + i, f, r)
                    add_into(self.grad, mine, self.zr.at[i], self.height)

            src = self.grad.at[self.rows(y)]
            for i, to in enumerate((xn, dn, cn)):
                cp.start(lambda i=i, to=to: (src, self.dst(), self.oid + i, self.oid + i, f, to), owner)

            @pl.when(owner)
            def _():
                local(src, self.dst(), lid).wait()

        def done(self):
            for i, source in enumerate((xn, dn, cn)):

                @pl.when(z == source)
                def _(i=i):
                    cp.arrived(self.dst(), self.oid + i, f, r)

    class Deal:
        def __init__(self, src, dst, lid):
            self.src, self.dst, self.lid, self.ids = src, dst, lid, cp.take(micro * NF)

        def start(self):
            for m in range(micro):
                for i, o in enumerate(others):
                    n = self.ids + m * NF + i
                    cp.start(
                        lambda m=m, o=o, n=n: (
                            self.src.at[m, o], self.dst.at[at(m * slot + f * part, part)], n, n, o, r
                        )
                    )
                local_pending.append(local(self.src.at[m, f], self.dst.at[at(m * slot + f * part, part)], self.lid + m))

        def done(self):
            for m in range(micro):
                for i in range(NF - 1):
                    source = lax.rem(f + NF - 1 - i, NF)
                    cp.arrived(self.dst.at[at(m * slot + source * part, part)], self.ids + m * NF + i, f, r)

    class Back:
        def __init__(self, src, dst, lid):
            self.src, self.dst, self.lid, self.ids = src, dst, lid, cp.take(micro * NF)

        def start(self):
            for m in range(micro):
                for i, o in enumerate(others):
                    n = self.ids + m * NF + i
                    cp.start(
                        lambda m=m, o=o, n=n: (
                            self.src.at[at(m * slot + o * part, part)], self.dst.at[m, f], n, n, o, r
                        )
                    )
                local_pending.append(local(self.src.at[at(m * slot + f * part, part)], self.dst.at[m, f], self.lid + m))

        def done(self):
            for m in range(micro):
                for i in range(NF - 1):
                    source = lax.rem(f + NF - 1 - i, NF)
                    cp.arrived(self.dst.at[m, source], self.ids + m * NF + i, f, r)

    L = iter(range(k["locals"].shape[0]))

    def lid(n=1):
        first = next(L)
        for _ in range(n - 1):
            next(L)
        return first

    smalls, lens = k["smalls"], k["lens"]
    small_ids, len_ids = cp.take(NF), cp.take(3)
    deal_x = Deal(k["tok"], k["xs"], lid(micro))
    deal_c = Deal(k["cot"], k["cs"], lid(micro))
    aall, hall, call = k["aall"], k["hall"], k["call"]
    e_a, e_c, e_h, e_y = Spread(aall), Spread(call), Spread(hall), Spread(hall)
    part_ = k["part"]
    s_1 = Sum(part_, k["sib0"], k["xsend"], k["xrecv0"])
    s_m = Sum(part_, k["sib1"], k["xsend"], k["xrecv1"])
    s_h = Sum(part_, k["sib0"], k["xsend"], k["xrecv0"])
    s_a = Sum(part_, k["sib0"], k["xsend"], k["xrecv0"])

    own_small = local(k["small"], smalls.at[f], lid())
    pl.semaphore_wait(barrier, len(friends))
    for i, o in enumerate(others):
        n = small_ids + i
        cp.start(lambda n=n, o=o: (k["small"], smalls.at[f], n, n, o, r))
    g_q.start(lid())
    deal_x.start()
    lo_ids = [lid() for _ in g_o]
    for g, i in zip(g_o, lo_ids):
        g.start(i)
    g_i[0].start(lid())

    wd[pl.ds(2 * sz.ffp, sz.fq - 2 * sz.ffp), :] = jnp.zeros((sz.fq - 2 * sz.ffp, d), BF16)

    g_q.column()

    own_small.wait()
    for i in range(NF - 1):
        source = lax.rem(f + NF - 1 - i, NF)
        cp.arrived(smalls.at[source], small_ids + i, f, r)
    gains = k["gains"]
    for j in range(NF):
        gains[0:2, j * sh : (j + 1) * sh] = smalls[j, 0:2, :]
    lane = lax.broadcasted_iota(jnp.int32, (1, 128), 1)
    sub = lax.broadcasted_iota(jnp.int32, (NF, 128), 0)
    ownrow = smalls[f]
    len_tab = smalls[:, 2, :]
    table = jnp.zeros((8, 128), F32)
    row8 = lax.broadcasted_iota(jnp.int32, (8, 128), 0)
    for m in range(micro):
        dealt = jnp.sum(jnp.where(lane == f, ownrow[3 + m : 4 + m, :], 0.0), axis=1, keepdims=True)
        hit = jnp.where(sub.astype(F32) == dealt, len_tab, 0.0)
        col = jnp.sum(hit, axis=0, keepdims=True)
        length = jnp.sum(jnp.where(lane == m, col, 0.0), axis=1, keepdims=True)
        table = jnp.where(row8 == m, length, table)
    lens[r] = table
    for i, to in enumerate((xn, dn, cn)):
        cp.start(lambda i=i, to=to: (lens.at[r], lens.at[r], len_ids + i, len_ids + i, f, to))

    def live_rows(m, t, n):
        pos = lax.broadcasted_iota(jnp.int32, (n, 1), 0).astype(F32) + (t * n).astype(F32)
        return pos < lens[r, m : m + 1, 0:1]

    def live_at(t, n):
        per = slot // n
        m = lax.div(t, per)
        pos = lax.broadcasted_iota(jnp.int32, (n, 1), 0) + lax.rem(t, per) * n
        length = lens[r, pl.ds(m, 1), :][:, 0:1]
        return pos.astype(F32) < length

    def normed(v):
        center = v - jnp.mean(v, axis=-1, keepdims=True)
        root = lax.rsqrt(jnp.mean(center * center, axis=-1, keepdims=True) + NORM_EPS)
        return center * root, root

    def norm_back(dy, gain, vhat, root):
        e = dy * gain
        return root * (e - jnp.mean(e, axis=-1, keepdims=True) - vhat * jnp.mean(e * vhat, axis=-1, keepdims=True))

    NL = 32
    xs, cs, hbuf, dhbuf = k["xs"], k["cs"], k["hbuf"], k["dhbuf"]

    deal_x.done()
    for pending in local_pending:
        pending.wait()
    local_pending.clear()

    def norm1(t):
        vhat, _ = normed(xs[at(t * NL, NL), :].astype(F32))
        aall[at(r * rows + t * NL, NL), :] = (vhat * gains[0:1, :]).astype(BF16)

    loop(rows // NL, norm1)
    e_a.start()
    deal_c.start()
    g_i[1].start(lid())
    for g in g_o:
        g.column()
    g_i[0].column()
    g_q.over_y()
    e_a.forward()
    if sz.ntile > 2:
        g_i[2].start(lid())
    for i, to in enumerate((xn, dn, cn)):
        cp.arrived(lens.at[to], len_ids + i, f, r)
    for g in g_o:
        g.over_y()
    e_a.done()
    g_i[1].column()

    qkv, pbuf, obuf = k["qkv"], k["pbuf"], k["obuf"]
    lane128 = lax.broadcasted_iota(jnp.int32, (1, 128), 1)
    front = lax.rem(lane128, 64) < 32
    low = lane128 < 64
    low_b = low.astype(F32).astype(BF16)
    high_b = (1.0 - low.astype(F32)).astype(BF16)
    hq = sz.hq
    npair = hq // 128
    scale = 64 ** (-0.5)

    def swap(v):
        return jnp.where(front, pltpu.roll(v, 96, 1), pltpu.roll(v, 32, 1))

    def both(v):
        return jnp.concatenate([v * low_b, v * high_b], axis=0)

    def joined(v):
        return jnp.where(low, v[:slot], v[slot:])

    def project(b):
        a = aall[block(b), :]
        for which in range(3):
            t = nn(a, wq[:, which * hq : (which + 1) * hq])
            for p in range(npair):
                v = t[:, p * 128 : (p + 1) * 128]
                if which < 2:
                    v = v * k["cos"][...] + swap(v) * k["sin"][...]
                qkv[block(b), which * hq + p * 128 : which * hq + (p + 1) * 128] = v.astype(BF16)

    def triple(s, p):
        return [qkv[at(s * slot, slot), which * hq + p * 128 : which * hq + (p + 1) * 128] for which in range(3)]

    def attend(b):
        def one(m):
            s = b * micro + m
            length = lens[b, pl.ds(m, 1), :]
            for p in range(npair):
                q_, k_, v_ = triple(s, p)
                scores = nt(both(q_), k_) * scale
                scores = jnp.where(lane128.astype(F32) < length, scores, -1e30)
                e = jnp.exp(scores - jnp.max(scores, axis=-1, keepdims=True))
                prob = e / jnp.sum(e, axis=-1, keepdims=True)
                pbuf[s, p] = prob
                out = nn(prob.astype(BF16), v_)
                obuf[at(s * slot, slot), p * 128 : (p + 1) * 128] = joined(out).astype(BF16)

        loop(micro, one)

    def branch_one(b):
        def tile(n):
            cols = at(n * 256, 256, 128)
            part_[block(b), cols] = nn(obuf[block(b), :], wo[:, cols])

        loop(d // 256, tile)

    for i, b in enumerate(s_1.order):
        project(b)
        attend(b)
        branch_one(b)
        s_1.ready(i)
        if i == 0:
            g_i[0].over_y()
            g_i[1].over_y()
        if i == 1 and sz.ntile > 2:
            g_i[2].column()
        if i == 1:
            for g in g_d:
                g.start(lid())

    deal_c.done()
    for pending in local_pending:
        pending.wait()
    local_pending.clear()

    def mask_c(t):
        lv = live_at(t, NL)
        call[at(r * rows + t * NL, NL), :] = jnp.where(lv, cs[at(t * NL, NL), :].astype(F32), 0.0).astype(BF16)

    loop(rows // NL, mask_c)

    s_1.done()

    def norm2(t):
        s = at(t * NL, NL)
        h = xs[s, :].astype(F32) + jnp.where(live_at(t, NL), s_1.value(t, NL), 0.0)
        hbuf[s, :] = h
        vhat, _ = normed(h)
        hall[at(r * rows + t * NL, NL), :] = (vhat * gains[1:2, :]).astype(BF16)

    loop(rows // NL, norm2)
    e_h.start()
    e_c.start()
    for g in g_d:
        g.column()
    for g in g_i[2:]:
        g.over_y()
    s_1.free()
    e_h.forward()
    e_h.done()

    gg, slope = k["gg"], k["slope"]
    tile_ = sz.tile

    def feed(i):
        b = lax.div(i, sz.ntile)
        n = lax.rem(i, sz.ntile)
        rs = at(b * rows, rows)
        w = nn(hall[rs, :], wi[:, at(n * 2 * tile_, 2 * tile_, 128)])
        w1, w2 = w[:, :tile_], w[:, tile_:]
        cdf = 0.5 * (1.0 + lax.erf(w1 * (0.5**0.5)))
        act = w1 * cdf
        pdf = jnp.exp(-0.5 * w1 * w1) * 0.3989422804014327
        cols = at(n * tile_, tile_, 128)
        gg[rs, cols] = (act * w2).astype(BF16)
        part_[rs, cols] = act
        slope[rs, cols] = w2 * (cdf + w1 * pdf)

    loop(NR * sz.ntile, feed)
    e_h.free()
    e_c.forward()
    e_c.done()
    for g in g_d:
        g.over_y()

    gd, gi, go, gq = k["gd"], k["gi"], k["go"], k["gq"]
    r_d = [RowReduce(gd, k["yrd"].at[i], k["zrd"].at[i], k["rd"], i * third, third, sz.ffp) for i in range(3)]
    r_i = [
        ColumnReduce(gi.at[n], k["yri"].at[n], k["zri"].at[n], None, k["ri"], n * t2, t2) for n in range(sz.ntile)
    ]
    r_o = [
        RowReduce(go, k["yro"].at[i], k["zro"].at[i], k["ro"], i * (sh // 2), sh // 2, sh) for i in range(2)
    ]
    r_q = ColumnReduce(gq, k["yrq"], k["zrq"], None, k["rq"], 0, 3 * hq)

    def grad_down(i):
        m = lax.div(i, 2)
        n = lax.rem(i, 2)
        cols = at(n * (d // 2), d // 2, 128)
        gd[at(m * 256, 256), cols] = tn(gg[:, at(m * 256, 256, 128)], call[:, cols]).astype(BF16)

    loop(sz.fq // 256 * 2, grad_down)
    for u in r_d:
        u.send()

    dw = k["dw"]

    def hidden(i):
        b = lax.div(i, sz.ntile)
        n = lax.rem(i, sz.ntile)
        rs = at(b * rows, rows)
        cols = at(n * tile_, tile_, 128)
        dgg = nt(call[rs, :], wd[at(n * tile_, tile_), :])
        dw[rs, at(n * 2 * tile_, tile_, 128)] = (dgg * slope[rs, cols]).astype(BF16)
        dw[rs, at(n * 2 * tile_ + tile_, tile_, 128)] = (dgg * part_[rs, cols]).astype(BF16)

    loop(NR * sz.ntile, hidden)
    for u in r_d:
        u.middle()

    def grad_in(n, j):
        gi[n, at(j * sh, sh), :] = tn(
            hall[:, at(j * sh, sh, 128)], dw[:, at(n * 2 * tile_, 2 * tile_, 128)]
        ).astype(BF16)

    def gin(other):
        for n in range(sz.ntile):

            def one(i, n=n):
                grad_in(n, 2 * i + (1 - y if other else y))

            loop(NZ, one)
            if other:
                for i in range(NZ):
                    r_i[n].send(2 * i + 1 - y)

    gin(True)
    gin(False)

    for i, b in enumerate(s_h.order):

        def tile(n, b=b):
            cols = at(n * 256, 256, 128)
            part_[block(b), cols] = nt(dw[block(b), :], wi[at(n * 256, 256), :])

        loop(d // 256, tile)
        s_h.ready(i)
    for u in r_d:
        u.final(lid())
    r_i[0].middle()
    dg = k["dg"]
    dg[...] = jnp.zeros_like(dg)
    s_h.done()

    def fold(v):
        return jnp.sum(v.reshape(NL // 8, 8, d), axis=0)

    def back2(t):
        s = at(t * NL, NL)
        dy = s_h.value(t, NL)
        vhat, root = normed(hbuf[s, :])
        dg[1] += fold(dy * vhat)
        dh = cs[s, :].astype(F32) + norm_back(dy, gains[1:2, :], vhat, root)
        dhbuf[s, :] = dh
        hall[at(r * rows + t * NL, NL), :] = jnp.where(live_at(t, NL), dh, 0.0).astype(BF16)

    loop(rows // NL, back2)
    e_y.start()
    s_h.free()

    mx = k["mx"]
    for i, b in enumerate(s_m.order):

        def tile(n, b=b):
            cols = at(n * 256, 256, 128)
            part_[block(b), cols] = nn(gg[block(b), :], wd[:, cols])

        loop(d // 256, tile)
        s_m.ready(i)
    r_i[1].middle()
    e_y.forward()
    e_y.done()

    def grad_out(i):
        cols = at(i * 256, 256, 128)
        go[:, cols] = tn(obuf[...], hall[:, cols]).astype(BF16)

    loop(d // 256, grad_out)
    for u in r_o:
        u.send()

    def attend_back(s):
        do_all = nt(hall[at(s * slot, slot), :], wo[...]).astype(BF16)
        for p in range(npair):
            q_, k_, v_ = triple(s, p)
            q2, do2 = both(q_), both(do_all[:, p * 128 : (p + 1) * 128])
            prob = pbuf[s, p]
            dp = nt(do2, v_)
            ds = (prob * (dp - jnp.sum(dp * prob, axis=-1, keepdims=True))).astype(BF16)
            dq = joined(nn(ds, k_)) * scale
            dk = tn(ds, q2) * scale
            dv = tn(prob.astype(BF16), do2)
            cosine, sine = k["cos"][0:slot, :], k["sin"][0:slot, :]
            dq = dq * cosine - swap(dq) * sine
            dk = dk * cosine - swap(dk) * sine
            for which, v in enumerate((dq, dk, dv)):
                dw[at(s * slot, slot), which * hq + p * 128 : which * hq + (p + 1) * 128] = v.astype(BF16)

    loop(NR * micro, attend_back)

    def grad_qkv(j):
        gq[at(j * sh, sh), :] = tn(aall[:, at(j * sh, sh, 128)], dw[:, 0 : 3 * hq]).astype(BF16)

    loop(NZ, lambda i: grad_qkv(2 * i + 1 - y))
    for i in range(NZ):
        r_q.send(2 * i + 1 - y)
    s_m.done()

    def mix(t):
        s = at(t * NL, NL)
        mx[s, :] = (hbuf[s, :] + jnp.where(live_at(t, NL), s_m.value(t, NL), 0.0)).astype(BF16)

    loop(rows // NL, mix)
    back_m = Back(mx, k["o_mixed"], lid(micro))
    back_m.start()
    s_m.free()
    for i, b in enumerate(s_a.order):

        def tile(n, b=b):
            cols = at(n * 256, 256, 128)
            part_[block(b), cols] = nt(dw[block(b), 0 : 3 * hq], wq[at(n * 256, 256), :])

        loop(d // 256, tile)
        s_a.ready(i)
    loop(NZ, lambda i: grad_qkv(2 * i + y))
    for u in r_o:
        u.middle()
    for u in r_i[2:]:
        u.middle()
    r_q.middle()
    s_a.done()
    gt = k["gt"]

    def back1(t):
        s = at(t * NL, NL)
        dy = s_a.value(t, NL)
        vhat, root = normed(xs[s, :].astype(F32))
        dg[0] += fold(dy * vhat)
        gt[s, :] = (dhbuf[s, :] + norm_back(dy, gains[0:1, :], vhat, root)).astype(BF16)

    loop(rows // NL, back1)
    back_t = Back(gt, k["o_gtok"], lid(micro))
    back_t.start()

    gsend, gslots, greps = k["gsend"], k["gslots"], k["greps"]
    for which in range(2):
        total = jnp.sum(dg[which], axis=0, keepdims=True)
        for j in range(NF):
            gsend[j, which : which + 1, :] = total[:, j * sh : (j + 1) * sh]
    gs_ids, gr_ids = cp.take(NF), cp.take(3)
    for i, o in enumerate(others):
        n = gs_ids + i
        cp.start(lambda n=n, o=o: (gsend.at[o], gslots.at[f], n, n, o, r))
    gslots[f] = gsend[f]
    for u in r_i:
        u.final(lid())
    for u in r_o:
        u.final(lid())
    for i in range(NF - 1):
        source = lax.rem(f + NF - 1 - i, NF)
        cp.arrived(gslots.at[source], gs_ids + i, f, r)
    total = gslots[0]
    for j in range(1, NF):
        total = total + gslots[j]
    greps[r] = total
    for i, to in enumerate((xn, dn, cn)):
        cp.start(lambda i=i, to=to: (greps.at[r], greps.at[r], gr_ids + i, gr_ids + i, f, to))
    r_q.final(lid())
    for i, source in enumerate((xn, dn, cn)):
        cp.arrived(greps.at[source], gr_ids + i, f, r)
    gout = k["gout"]
    gout[...] = greps[0] + greps[1] + greps[2] + greps[3]
    local_pending.append(local(gout, k["o_small"], lid()))

    for u in r_d + r_i + r_o + [r_q, back_m, back_t]:
        u.done()
    s_a.free()
    for e in (e_a, e_c, e_y):
        e.free()
    cp.drain()
    for pending in local_pending:
        pending.wait()


def fused(sz, tok, cot, small, cos, sin, sq, so, si, sd):
    d, sh, all_, rows = sz.d, sz.shard, sz.all, sz.rows
    t2 = 2 * sz.tile
    third, half = sz.ffp // 3, sh // 2
    hq3 = 3 * sz.hq
    bf = lambda *s: pltpu.VMEM(s, BF16)
    fl = lambda *s: pltpu.VMEM(s, F32)
    ins = ("tok", "cot", "small", "cos", "sin", "sq", "so", "si", "sd")
    outs = {
        "o_mixed": jax.ShapeDtypeStruct((sz.micro, NF, sz.part, d), BF16),
        "o_gtok": jax.ShapeDtypeStruct((sz.micro, NF, sz.part, d), BF16),
        "o_small": jax.ShapeDtypeStruct((8, 128), F32),
        "rq": jax.ShapeDtypeStruct((NR, sh, hq3), BF16),
        "ro": jax.ShapeDtypeStruct((sh, d), BF16),
        "ri": jax.ShapeDtypeStruct((NR, sh, sz.ntile * t2), BF16),
        "rd": jax.ShapeDtypeStruct((sz.ffp, d), BF16),
    }
    scratch = {
        "wq": bf(d, hq3), "wo": bf(2 * sh, d), "wi": bf(d, sz.ntile * t2), "wd": bf(sz.fq, d),
        "xs": bf(rows, d), "cs": bf(rows, d), "mx": bf(rows, d), "gt": bf(rows, d),
        "aall": bf(all_, d), "hall": bf(all_, d), "call": bf(all_, d),
        "smalls": fl(NF, 8, 128), "lens": fl(NR, 8, 128), "gains": fl(8, d),
        "qkv": bf(all_, hq3), "pbuf": fl(NR * sz.micro, sz.hq // 128, 2 * sz.slot, 128), "obuf": bf(all_, sz.hq),
        "part": fl(all_, d), "sib0": fl(2, rows, d), "sib1": fl(2, rows, d),
        "xsend": bf(rows, d), "xrecv0": bf(rows, d), "xrecv1": bf(rows, d),
        "hbuf": fl(rows, d), "dhbuf": fl(rows, d), "dg": fl(2, 8, d),
        "gg": bf(all_, sz.fq), "slope": fl(all_, sz.fq), "dw": bf(all_, sz.ntile * t2),
        "gd": bf(sz.fq, d), "gi": bf(sz.ntile, d, t2), "go": bf(2 * sh, d), "gq": bf(d, hq3),
        "yrd": bf(3, third, d), "zrd": bf(3, 2, third, d),
        "yri": bf(sz.ntile, NZ, sh, t2), "zri": bf(sz.ntile, NZ + 1, sh, t2),
        "yro": bf(2, half, d), "zro": bf(2, 2, half, d),
        "yrq": bf(NZ, sh, hq3), "zrq": bf(NZ + 1, sh, hq3),
        "gsend": fl(NF, 8, 128), "gslots": fl(NF, 8, 128), "greps": fl(NR, 8, 128), "gout": fl(8, 128),
        "sends": pltpu.SemaphoreType.DMA((384,)), "recvs": pltpu.SemaphoreType.DMA((384,)),
        "locals": pltpu.SemaphoreType.DMA((48,)),
    }
    any_ = pl.BlockSpec(memory_space=pl.ANY)
    vmem = pl.BlockSpec(memory_space=pltpu.VMEM)
    names = ins + tuple(outs) + tuple(scratch)
    return pl.pallas_call(
        functools.partial(kernel, sz, names),
        out_shape=list(outs.values()),
        in_specs=[any_] * 3 + [vmem] * 2 + [any_] * 4,
        out_specs=[any_] * len(outs),
        scratch_shapes=list(scratch.values()),
        compiler_params=pltpu.CompilerParams(collective_id=0, has_side_effects=True, vmem_limit_bytes=64 * MIB),
    )(tok, cot, small, cos, sin, sq, so, si, sd)


def routed(tokens, cotangent, deal, lengths, ln1_gain, w_qkv, w_out, ln2_gain, w_in, w_down):
    micro, _, part, d = tokens.shape
    ffs = w_down.shape[0]
    sz = Sizes(micro, part, d, ffs)
    r = lax.axis_index("rep")
    hq, sh = sz.hq, sz.shard
    quarter = lambda w, start: lax.dynamic_slice_in_dim(w, start, hq, axis=1)
    sq = jnp.concatenate([quarter(w_qkv, i * d + r * hq) for i in range(3)], axis=1).astype(BF16)
    so = w_out.astype(BF16)
    sd = jnp.pad(w_down.astype(BF16), ((0, sz.ffp - ffs), (0, 0)))
    halves = []
    for i in range(2):
        w = lax.dynamic_slice_in_dim(w_in, i * NF * ffs + r * 2 * ffs, 2 * ffs, axis=1).astype(BF16)
        gap = jnp.zeros((sh, sz.ffp - ffs), BF16)
        end = jnp.zeros((sh, sz.fq - 2 * sz.ffp), BF16)
        halves.append(jnp.concatenate([w[:, :ffs], gap, w[:, ffs:], gap, end], axis=1))
    t = sz.tile
    si = jnp.concatenate([h[:, n * t : (n + 1) * t] for n in range(sz.ntile) for h in halves], axis=1)
    gain = [lax.reduce_precision(g, 8, 7)[None] for g in (ln1_gain, ln2_gain)]
    wide = lambda v: jnp.pad(v.astype(F32), ((0, 0), (0, 128 - v.shape[1])))
    small = jnp.concatenate(gain + [wide(lengths[:, 0, 0][None]), wide(deal[:, 0]), jnp.zeros((5 - micro, 128), F32)])
    half = 32
    freq = ROPE_BASE ** (-(jnp.arange(half, dtype=F32) * 2.0 / (2 * half)))
    angles = jnp.arange(sz.slot, dtype=F32)[:, None] * freq[None, :]
    cos = jnp.tile(jnp.cos(angles), (micro, 4))
    sin = jnp.tile(jnp.concatenate([-jnp.sin(angles), jnp.sin(angles)], axis=1), (micro, 2))
    mixed, gtok, osmall, rq, ro, ri, rd = fused(sz, tokens, cotangent, small, cos, sin, sq, so, si, sd)
    grad_qkv = jnp.concatenate(
        [rq[q, :, i * hq : (i + 1) * hq] for i in range(3) for q in range(NR)], axis=1
    ).astype(F32)
    pieces = []
    for i in range(2):
        for q in range(NR):
            w = jnp.concatenate([ri[q, :, (2 * n + i) * t : (2 * n + i + 1) * t] for n in range(sz.ntile)], axis=1)
            pieces += [w[:, :ffs], w[:, sz.ffp : sz.ffp + ffs]]
    grad_in = jnp.concatenate(pieces, axis=1).astype(F32)
    return mixed, gtok, osmall[0], grad_qkv, ro.astype(F32), osmall[1], grad_in, rd[:ffs].astype(F32)


def solution(mesh):
    small = mesh.shape["fsdp"] == NF and mesh.shape["rep"] == NR
    rows = P(None, "rep", "fsdp", None)
    return jax.shard_map(
        routed if small else plain,
        mesh=mesh,
        in_specs=(
            rows, rows, P(None, "rep", None), P(None, "rep", "fsdp"),
            P("fsdp"), P("fsdp", None), P("fsdp", None), P("fsdp"), P("fsdp", None), P("fsdp", None),
        ),
        out_specs=(rows, rows, P("fsdp"), P("fsdp", None), P("fsdp", None), P("fsdp"), P("fsdp", None), P("fsdp", None)),
        check_vma=False,
    )
```

time: 1420 us -> 326 us (0.23)
  waiting for transfers between devices: 1100 us -> 0 us
  Pallas kernels: 0 us -> 300 us
  matrix products: 119 us -> 0 us
  blocking collectives: 72.5 us -> 0 us
  other arithmetic: 42.7 us -> 10.5 us
  starting transfers between devices: 24.5 us -> 0 us
  local copies, waits for them, and re-layouts: 37 us -> 13.7 us
  between operations: 16.2 us -> 0.99 us
    reduce_scatter x4 -> x0, waiting for transfers between devices: 762 us -> none  [on_device(): lax.psum_scatter(totals, 'fsdp', scatter_dimension=0, tiled=True)]
    pallas_call x0 -> x1, Pallas kernels: none -> 300 us  [fused(): pl.pallas_call(functools.partial(kernel, sz, names), out_shape=list(outs....]
    all_gather x4 -> x0, waiting for transfers between devices: 287 us -> none  [the longest x1 146 us: on_device(): lax.all_gather(shards[4], 'fsdp', axis=0, tiled=True)]
    dot_general x36 -> x0, matrix products: 119 us -> none  [the longest x2 24.8 us: backward_pass(): jnp.einsum('sd,sf->df', ffn_low, hidden_low, preferred_element_type=jnp.f...]
    all_gather x2 -> x0, blocking collectives: 45.1 us -> none  [the longest x1 34.4 us: on_device(): lax.all_gather(shards[3], 'fsdp', axis=0, tiled=True)]
    psum x1 -> x0, waiting for transfers between devices: 26.6 us -> none  [on_device(): lax.psum(shortened(owned_total), 'rep')]
    all_to_all x4 -> x0, starting transfers between devices: 24 us -> none  [the longest x1 8.99 us: on_device(): lax.all_to_all(sent_grads, 'fsdp', split_axis=1, concat_axis=2, tiled=True)]
    convert_element_type x28 -> x8, other arithmetic: 29.2 us -> 5.89 us  [the longest x1 1.69 us: routed(): grad_in = jnp.concatenate(pieces, axis=1).astype(F32)]
  transfers between devices with their start and end apart: 13 -> 0, of which waited for: 10 -> 0; matrix products, arithmetic and copies ran while one was open for 9% -> 0% of each run, Pallas kernels for 0% -> 0%
where the time goes in v2:
time: 326 us; the launch traced here: 325 us
  Pallas kernels  300 us (92%)
  local copies, waits for them, and re-layouts  13.7 us (4%)
  other arithmetic  10.5 us (3%)
    pallas_call x1, Pallas kernels, fused(): pl.pallas_call(functools.partial(kernel, sz, names), out_shape=list(outs....  300 us

profile of v2, /device:TPU:17, one launch (start us, length us, event | category | flops | bytes accessed | tf_op | source)
XLA Modules:
  0.0 325.1 jit_solution(17779309794017351272)
XLA Ops:
  0.6 1.3 dynamic-slice_convert_fusion
  2.0 0.1 fusion.11
  2.1 0.6 slice_dynamic-update-slice_fusion.1
  2.8 0.6 slice_dynamic-update-slice_fusion
  3.4 0.7 fusion.1
  4.1 0.0 copy-start.8
  4.1 0.0 copy-start.9
  4.1 0.0 copy-start.7
  4.1 0.0 copy-start.10
  4.1 0.0 copy-start
  4.2 0.7 fusion.3
  4.9 0.1 pad_slice_fusion
  5.0 0.7 fusion.5
  5.7 0.7 fusion.7.refs_7_
  6.4 1.1 dynamic-slice_convert_fusion.4
  7.5 0.7 pad_maximum_fusion.refs_5_
  8.2 0.1 fusion.10
  8.4 0.8 copy.19.refs_4_
  9.2 0.8 copy.18.refs_3_
  10.0 0.0 copy-done.8
  10.0 0.0 copy-done.9
  10.0 0.0 copy-done.7
  10.0 0.0 copy-done.10
  10.1 0.6 concatenate.89.refs_2_
  10.7 0.0 copy-done
  10.7 0.0 copy-start.3
  10.7 0.1 convert_element_type.58
  10.8 0.9 pad.14.refs_8_
  11.7 0.0 copy-done.3
  11.7 0.7 convert_element_type.55.refs_6_
  12.5 299.9 %shard_map.161 = (bf16[2,8,16,1024]{3,2,1,0:T(8,128)(2,1)}, bf16[2,8,16,1024]{3,2,1,0:T(8,128)(2,1)}, f32[8,128]{1,0:T(8,128)}, bf16[4,128,768]{2,1,0:T(8,128)(2...) custom-call(bf16[2,8,16,1024]{3,2,1,0:T(8,128)(2,1)} %refs_0_.1, ...), custom_call_target="tpu_custom_call" | custom-call | tf_op jit(solution)/shard_map/pallas_call | solution.py:1056
  312.4 1.4 slice_bitcast_fusion
  313.8 0.1 pad_maximum_fusion.1
  313.9 0.1 pad_maximum_fusion.3
  314.0 0.1 pad_maximum_fusion.5
  314.1 0.1 pad_maximum_fusion.7
  314.2 0.1 pad_maximum_fusion.9
  314.4 0.1 pad_maximum_fusion.11
  314.5 1.0 slice_bitcast_fusion.20
  315.5 0.1 pad_maximum_fusion.13
  315.6 0.1 pad_maximum_fusion.15
  315.7 1.2 concatenate.114
  316.9 0.0 copy-start.1
  316.9 1.7 convert_element_type.61
  318.6 0.0 copy-done.1
  318.7 0.0 copy-start.2
  318.8 1.3 convert_element_type.59
  320.1 0.0 copy-start.6
  320.1 0.0 copy-start.5
  320.1 0.0 copy-done.2
  320.1 0.0 copy-start.4
  320.1 1.2 slice_convert_fusion
  321.3 0.0 copy-done.6
  321.3 0.8 convert_element_type.60
  322.2 1.3 slice_bitcast_fusion.24
  323.5 0.0 copy-done.5
  323.5 0.8 copy.44
  324.3 0.0 copy-done.4
  324.3 0.8 copy.45
  (26 shorter events, 0.2 us)
Async XLA Ops:
  4.1 5.9 %copy-start.8 = (f32[128]{0:T(128)S(1)}, f32[128]{0:T(128)}, u32[]{:S(2)}) copy-start(f32[128]{0:T(128)} %param.17) | copy-start | bytes 1540
  4.1 5.9 %copy-start.9 = (f32[128]{0:T(128)S(1)}, f32[128]{0:T(128)}, u32[]{:S(2)}) copy-start(f32[128]{0:T(128)} %param.14) | copy-start | bytes 1540
  4.1 5.9 %copy-start.7 = (s32[2,1,8]{2,1,0:T(1,128)S(1)}, s32[2,1,8]{2,1,0:T(1,128)}, u32[]{:S(2)}) copy-start(s32[2,1,8]{2,1,0:T(1,128)} %param.12) | copy-start | bytes 196
  4.1 5.9 %copy-start.10 = (s32[2,1,1]{0,2,1:T(1,128)S(1)}, s32[2,1,1]{0,2,1:T(1,128)}, u32[]{:S(2)}) copy-start(s32[2,1,1]{0,2,1:T(1,128)} %param.13) | copy-start | bytes 28
  4.1 6.5 %copy-start = (f32[328,1024]{1,0:T(8,128)S(1)}, f32[328,1024]{1,0:T(8,128)}, u32[]{:S(2)}) copy-start(f32[328,1024]{1,0:T(8,128)} %param.19) | copy-start | bytes 4030468
  10.7 1.0 copy-start.3
  316.9 1.7 copy-start.1
  318.7 1.4 copy-start.2
  320.1 1.2 copy-start.6
  320.1 3.4 %copy-start.5 = (bf16[2,8,16,1024]{3,2,1,0:T(8,128)(2,1)S(1)}, bf16[2,8,16,1024]{3,2,1,0:T(8,128)(2,1)}, u32[]{:S(2)}) copy-start(bf16[2,8,16,1024]{3,2,1,0:T(8,128)(2,1)} %get-tuple-element.88) | copy-start | bytes 1572868
  320.1 4.1 %copy-start.4 = (bf16[2,8,16,1024]{3,2,1,0:T(8,128)(2,1)S(1)}, bf16[2,8,16,1024]{3,2,1,0:T(8,128)(2,1)}, u32[]{:S(2)}) copy-start(bf16[2,8,16,1024]{3,2,1,0:T(8,128)(2,1)} %get-tuple-element.89) | copy-start | bytes 1572868

commit v3 on v0

v3 whole, which is shorter than its diff:
```python
import functools
import types

import jax
import jax.numpy as jnp
import numpy as np
from jax import lax
from jax.experimental import pallas as pl
from jax.experimental.pallas import tpu as pltpu
from jax.sharding import PartitionSpec as P

HEADS = 16
ROPE_BASE = 160000.0
NORM_EPS = 1e-05
MESH = pl.DeviceIdType.MESH
MIB = 1 << 20
BF16 = jnp.bfloat16
F32 = jnp.float32


def rope_tables(slot_count, head_size):
    half_size = head_size // 2
    frequency = ROPE_BASE ** (-(jnp.arange(half_size, dtype=F32) * 2.0 / head_size))
    angles = jnp.arange(slot_count, dtype=F32)[:, None] * frequency[None, :]
    return jnp.cos(angles), jnp.sin(angles)


def rotate(values, cosine, sine):
    front, back = jnp.split(values, 2, axis=-1)
    cosine, sine = cosine[:, None, :], sine[:, None, :]
    return jnp.concatenate([front * cosine - back * sine, back * cosine + front * sine], axis=-1)


def normed(values, gain):
    center = values - jnp.mean(values, axis=-1, keepdims=True)
    root = lax.rsqrt(jnp.mean(center * center, axis=-1, keepdims=True) + NORM_EPS)
    vhat = center * root
    return vhat * gain, vhat, root


def norm_back(dy, gain, vhat, root):
    dgain = jnp.sum(dy * vhat, axis=tuple(range(dy.ndim - 1)))
    e = dy * gain
    dz = root * (
        e
        - jnp.mean(e, axis=-1, keepdims=True)
        - vhat * jnp.mean(e * vhat, axis=-1, keepdims=True)
    )
    return dgain, dz


def mm(spec, a, b):
    return jnp.einsum(spec, a, b, preferred_element_type=F32)


def layer(g1, wqkv, wo, g2, win, wdown, tokens, dout, live):
    m, slot, d = tokens.shape
    heads, size = HEADS, d // HEADS
    scale = size ** (-0.5)
    w1, w2 = win
    lv = live[:, :, None]
    x = tokens.astype(F32)
    y, vhat1, root1 = normed(x, g1)
    a = y.astype(BF16)
    qkv = mm("mtd,de->mte", a, wqkv).reshape(m, slot, 3, heads, size)
    cosine, sine = rope_tables(slot, size)
    q = rotate(qkv[:, :, 0], cosine, sine).astype(BF16)
    k = rotate(qkv[:, :, 1], cosine, sine).astype(BF16)
    v = qkv[:, :, 2].astype(BF16)
    s = mm("mqhd,mkhd->mhqk", q, k) * scale
    s = jnp.where(live[:, None, None, :] > 0, s, -1e30)
    p = jax.nn.softmax(s, axis=-1)
    pb = p.astype(BF16)
    o = mm("mhqk,mkhd->mqhd", pb, v).astype(BF16).reshape(m, slot, d)
    h = x + lv * mm("mte,ed->mtd", o, wo)
    y, vhat2, root2 = normed(h, g2)
    hn = y.astype(BF16)
    z1 = mm("mtd,df->mtf", hn, w1)
    z2 = mm("mtd,df->mtf", hn, w2)
    cdf = 0.5 * (1.0 + lax.erf(z1 * (0.5**0.5)))
    pdf = jnp.exp(-0.5 * z1 * z1) * 0.3989422804014327
    act = z1 * cdf
    gg = (act * z2).astype(BF16)
    mixed = (h + lv * mm("mtf,fd->mtd", gg, wdown)).astype(BF16)

    up = dout.astype(F32)
    dy2 = (lv * up).astype(BF16)
    g_down = mm("mtf,mtd->fd", gg, dy2)
    dgg = mm("mtd,fd->mtf", dy2, wdown)
    dw1 = (dgg * z2 * (cdf + z1 * pdf)).astype(BF16)
    dw2 = (dgg * act).astype(BF16)
    g_in = (mm("mtd,mtf->df", hn, dw1), mm("mtd,mtf->df", hn, dw2))
    dhn = mm("mtf,df->mtd", dw1, w1) + mm("mtf,df->mtd", dw2, w2)
    g_g2, dhv = norm_back(dhn, g2, vhat2, root2)
    dh = up + dhv
    dy1 = (lv * dh).astype(BF16)
    g_out = mm("mte,mtd->ed", o, dy1)
    do = mm("mtd,ed->mte", dy1, wo).astype(BF16).reshape(m, slot, heads, size)
    dp = mm("mqhd,mkhd->mhqk", do, v)
    ds = (p * (dp - jnp.sum(dp * p, axis=-1, keepdims=True))).astype(BF16)
    dq = mm("mhqk,mkhd->mqhd", ds, k) * scale
    dk = mm("mhqk,mqhd->mkhd", ds, q) * scale
    dv = mm("mhqk,mqhd->mkhd", pb, do)
    dqkv = jnp.stack([rotate(dq, cosine, -sine), rotate(dk, cosine, -sine), dv], axis=2)
    dqkv = dqkv.reshape(m, slot, 3 * d).astype(BF16)
    g_qkv = mm("mtd,mte->de", a, dqkv)
    da = mm("mte,de->mtd", dqkv, wqkv)
    g_g1, dxv = norm_back(da, g1, vhat1, root1)
    gtok = (dh + dxv).astype(BF16)
    return mixed, gtok, (g_g1, g_qkv, g_out, g_g2, g_in, g_down)


def plain(tokens, cotangent, deal, lengths, ln1_gain, w_qkv, w_out, ln2_gain, w_in, w_down):
    slot = tokens.shape[2] * lax.axis_size("fsdp")
    me = lax.axis_index("fsdp")

    def spread(rows):
        return lax.all_to_all(rows, "fsdp", split_axis=1, concat_axis=2, tiled=True)[:, 0]

    def back(rows):
        return lax.all_to_all(rows[:, None], "fsdp", split_axis=2, concat_axis=1, tiled=True)

    def whole(shard):
        return lax.all_gather(shard.astype(BF16), "fsdp", axis=0, tiled=True)

    table = lax.all_gather(lengths[:, 0], "fsdp", axis=1, tiled=True)
    mine = lax.dynamic_slice_in_dim(deal[:, 0], me, 1, axis=1)
    pick = jnp.arange(table.shape[1], dtype=jnp.int32)[None, :] == mine
    length = jnp.sum(jnp.where(pick, table, 0), axis=1, keepdims=True)
    live = (jnp.arange(slot, dtype=jnp.int32)[None, :] < length).astype(F32)
    win = jnp.split(whole(w_in), 2, axis=1)
    mixed, gtok, grads = layer(
        whole(ln1_gain).astype(F32), whole(w_qkv), whole(w_out), whole(ln2_gain).astype(F32), win, whole(w_down),
        spread(tokens), spread(cotangent), live,
    )
    g_g1, g_qkv, g_out, g_g2, g_in, g_down = grads

    def owned(part):
        part = lax.psum_scatter(part, "fsdp", scatter_dimension=0, tiled=True)
        return lax.psum(part, "rep")

    g_in = jnp.concatenate(g_in, axis=1)
    return (back(mixed), back(gtok)) + tuple(owned(g) for g in (g_g1, g_qkv, g_out, g_g2, g_in, g_down))


NF, NR, NZ = 8, 4, 4
DN, XN, CN = 0, 1, 2


def at(offset, size, unit=16):
    return pl.ds(pl.multiple_of(offset, unit), size)


def nn(a, b):
    return lax.dot_general(a, b, (((1,), (0,)), ((), ())), preferred_element_type=F32)


def nt(a, b):
    return lax.dot_general(a, b, (((1,), (1,)), ((), ())), preferred_element_type=F32)


def tn(a, b):
    return lax.dot_general(a, b, (((0,), (0,)), ((), ())), preferred_element_type=F32)


def loop(n, body):
    def step(i, carry):
        body(i)
        return carry

    lax.fori_loop(0, n, step, 0)


ORDER = (
    2, 0, 14, 15, 62, 1, 10, 43, 4, 44, 5, 6, 3, 7, 45, 47, 23, 64, 48, 49, 63, 8, 12, 16, 50, 42, 11, 17, 65, 25,
    52, 13, 9, 59, 24, 66, 28, 33, 51, 39, 36, 18, 57, 55, 46, 53, 54, 56, 19, 30, 61, 60, 20, 69, 21, 29, 58, 67,
    31, 71, 22, 26, 34, 72, 68, 76, 70, 40, 75, 32, 73, 74, 27, 80, 79, 37, 81, 41, 77, 78, 82, 38, 35, 86, 83, 93,
    85, 84, 94, 97, 132, 95, 90, 87, 138, 88, 89, 96, 135, 98, 99, 119, 141, 100, 105, 142, 103, 118, 146, 92, 136,
    133, 101, 106, 102, 147, 143, 91, 104, 115, 162, 109, 116, 161, 107, 156, 148, 117, 157, 137, 120, 144, 152,
    121, 108, 110, 111, 166, 139, 167, 112, 114, 122, 123, 171, 149, 163, 113, 176, 124, 126, 168, 151, 172, 173,
    134, 177, 169, 178, 140, 145, 125, 158, 153, 127, 128, 150, 174, 179, 129, 159, 170, 160, 164, 154, 130, 155,
    175, 180, 131, 165, 181,
)


def run_tasks(tasks):
    done = set()
    for i in ORDER or range(len(tasks)):
        deps, fn = tasks[i]
        assert done.issuperset(deps)
        fn()
        done.add(i)
    assert len(done) == len(tasks)


SOURCES = ((1, 0, 3, 2), (2, 2, 1, 1), (3, 3, 0, 0))
SOURCE_BELOW = ((0, 1, 0, 1), (0, 0, 1, 1), (0, 0, 1, 1))
OWNERS = ((3, 3, 0, 0), (2, 2, 1, 1), (1, 0, 3, 2))
OWNER_ABOVE = ((1, 1, 0, 0), (1, 1, 0, 0), (1, 0, 1, 0))
OWNER_SLOT = ((3, 3, 0, 0), (2, 2, 4, 1), (1, 4, 3, 4))


class Sizes:
    def __init__(self, micro, part, d, ffs):
        self.micro, self.part, self.d, self.ffs = micro, part, d, ffs
        self.slot = part * NF
        self.rows = micro * self.slot
        self.all = NR * self.rows
        self.shard = d // NF
        self.hq = d // NR
        self.ffp = -(-ffs // 16) * 16
        self.tile = 256
        self.ntile = -(-(2 * self.ffp) // self.tile)
        self.fq = self.ntile * self.tile


class Copies:
    def __init__(self, sends, recvs):
        self.sends, self.recvs, self.nsend, self.nrecv = sends, recvs, 0, 0
        self.left = []

    def send(self, n=1):
        base, self.nsend = self.nsend, self.nsend + n
        assert self.nsend <= self.sends.shape[0]
        return base

    def recv(self, n=1):
        base, self.nrecv = self.nrecv, self.nrecv + n
        assert self.nrecv <= self.recvs.shape[0]
        return base

    def make(self, src, dst, send, recv, f, r):
        return pltpu.make_async_remote_copy(
            src_ref=src, dst_ref=dst, send_sem=self.sends.at[send], recv_sem=self.recvs.at[recv],
            device_id={"fsdp": f, "rep": r}, device_id_type=MESH,
        )

    def start(self, build, cond=None):
        def go():
            self.make(*build()).start()

        go() if cond is None else pl.when(cond)(go)

    def arrived(self, ref, recv, f, r):
        self.make(ref, ref, 0, recv, f, r).wait_recv()

    def gone(self, ref, send, f, r, cond=None):
        def go():
            self.make(ref, ref, send, 0, f, r).wait_send()

        go() if cond is None else pl.when(cond)(go)

    def at_end(self, ref, send, cond=None):
        self.left.append((ref, send, cond))


def kernel(sz, names, *refs):
    k = types.SimpleNamespace(**dict(zip(names, refs)))
    d, rows, slot, micro, part = sz.d, sz.rows, sz.slot, sz.micro, sz.part
    f, r = lax.axis_index("fsdp"), lax.axis_index("rep")
    z, y = lax.div(f, 2), lax.rem(f, 2)
    c = lax.rem(r, 2)
    yn = f + 1 - 2 * y
    cn = r + 1 - 2 * c
    xn = lax.rem(r + 2, 4)
    dn = lax.rem(cn + 2, 4)
    others = [lax.rem(f + i, NF) for i in range(1, NF)]
    cp = Copies(k.sends, k.recvs)

    def local(src, dst, i):
        copy = pltpu.make_async_copy(src, dst, k.locals.at[i])
        copy.start()
        return copy

    def block(i):
        return at(i * rows, rows)

    barrier = pltpu.get_barrier_semaphore()
    friends = [(o, r) for o in others] + [(f, o) for o in (cn, xn, dn)]
    for ff, rr in friends:
        pl.semaphore_signal(barrier, inc=1, device_id={"fsdp": ff, "rep": rr}, device_id_type=MESH)

    tasks = []

    def task(*deps):
        def register(fn):
            tasks.append((deps, fn))
            return len(tasks) - 1

        return register

    wq, wo, wi, wd = k.wq, k.wo, k.wi, k.wd
    sh = sz.shard
    micros = range(micro)
    ends = []

    eights = (1 + 7 * lax.rem(z, 2)) * (1 + 63 * lax.div(z, 2))

    def by_z(*values):
        code = sum(v << (3 * i) for i, v in enumerate(values))
        return lax.rem(lax.div(jnp.int32(code), eights), 8)

    inner = jnp.logical_and(z > 0, z < NZ - 1)
    order_z = [by_z(*o) for o in OWNERS] + [z]

    class ColumnGather:
        def __init__(self, whole, col, width):
            self.whole, self.cols = whole, at(col, width, 128)
            self.zrecv, self.yrecv, self.zsend, self.ysend = cp.recv(NZ), cp.recv(), cp.send(), cp.send()
            cp.at_end(self.shards(NZ), self.ysend)
            cp.at_end(self.shards(NZ + 1), self.zsend, inner)
            cp.at_end(self.shards(1), self.zsend, jnp.logical_not(inner))

        def shards(self, n):
            return self.whole.at[pl.ds(0, n * sh), self.cols]

        def dst(self, j):
            return self.whole.at[at(j * sh, sh), self.cols]

        def over(self, j):
            dst = self.dst(j)
            cp.start(lambda: (dst, dst, self.ysend, self.yrecv, yn, r))

        def start(self):
            src = self.dst(f)
            cp.start(lambda: (src, src, self.zsend, self.zrecv + z, f + 2, r), z < NZ - 1)
            cp.start(lambda: (src, src, self.zsend, self.zrecv + z, f - 2, r), z > 0)
            self.over(f)

        def along_z(self, i):
            source, up = by_z(*SOURCES[i]), by_z(*SOURCE_BELOW[i])
            j = 2 * source + y
            dst = self.dst(j)
            cp.arrived(dst, self.zrecv + source, f, r)
            cp.start(lambda: (dst, dst, self.zsend, self.zrecv + source, f + 2 * (2 * up - 1), r), inner)
            self.over(j)

        def over_y(self):
            cp.arrived(self.shards(NZ), self.yrecv, f, r)

        def register(self, *deps):
            start = task(*deps)(self.start)
            steps = [task(start)(lambda i=i: self.along_z(i)) for i in range(NZ - 1)]
            self.needs = [start, *steps, task(start)(self.over_y)]

    class LongRowGather:
        def __init__(self, whole, row, height, pitch):
            self.whole, self.row, self.height, self.pitch = whole, row, height, pitch
            self.recv, self.send = cp.recv(2), cp.send(3)
            for n, cond in ((0, z < NZ - 1), (1, z > 0)):
                cp.at_end(self.dst(y), self.send + n, jnp.logical_and((z >= r) if n == 0 else (z <= r), cond))
            cp.at_end(self.dst(y), self.send + 2)

        def dst(self, yy):
            return self.whole.at[at(yy * self.pitch + self.row, self.height)]

        def onward(self):
            dst = self.dst(y)
            up = jnp.logical_and(z >= r, z < NZ - 1)
            down = jnp.logical_and(z <= r, z > 0)
            cp.start(lambda: (dst, dst, self.send, self.recv + y, f + 2, r), up)
            cp.start(lambda: (dst, dst, self.send + 1, self.recv + y, f - 2, r), down)
            cp.start(lambda: (dst, dst, self.send + 2, self.recv + y, yn, r))

        def start(self):
            @pl.when(z == r)
            def _():
                self.onward()

        def pass_on(self):
            @pl.when(z != r)
            def _():
                cp.arrived(self.dst(y), self.recv + y, f, r)
                self.onward()

        def rest(self):
            cp.arrived(self.dst(1 - y), self.recv + 1 - y, f, r)

        def register(self, *deps):
            start = task(*deps)(self.start)
            self.needs = [start, task(start)(self.pass_on), task(start)(self.rest)]

    class RowGather:
        def __init__(self, whole, row, height, pitch):
            self.whole, self.row, self.height, self.pitch = whole, row, height, pitch
            self.recv, self.send = cp.recv(2), cp.send(5)
            for yy, send in ((y, self.send), (1 - y, self.send + 2)):
                cp.at_end(self.dst(yy), send, self.up)
                cp.at_end(self.dst(yy), send + 1, self.down)
            cp.at_end(self.dst(y), self.send + 4, z == r)

        up = jnp.logical_and(z >= r, z < NZ - 1)
        down = jnp.logical_and(z <= r, z > 0)

        def dst(self, yy):
            return self.whole.at[at(yy * self.pitch + self.row, self.height)]

        def onward(self, yy, send):
            dst = self.dst(yy)
            cp.start(lambda: (dst, dst, send, self.recv + yy, f + 2, r), self.up)
            cp.start(lambda: (dst, dst, send + 1, self.recv + yy, f - 2, r), self.down)

        def start(self):
            dst = self.dst(y)
            cp.start(lambda: (dst, dst, self.send + 4, self.recv + y, yn, r), z == r)

        last = jnp.logical_and(z != r, jnp.logical_or(z == 0, z == NZ - 1))

        def pass_on(self, near):
            yy, send = (y, self.send) if near else (1 - y, self.send + 2)
            waits = jnp.logical_not(self.last)

            @pl.when(jnp.logical_and(waits, z != r) if near else waits)
            def _():
                cp.arrived(self.dst(yy), self.recv + yy, f, r)

            self.onward(yy, send)

        def rest(self):
            @pl.when(self.last)
            def _():
                for yy in (y, 1 - y):
                    cp.arrived(self.dst(yy), self.recv + yy, f, r)

        def register(self, *deps):
            start = task(*deps)(self.start)
            self.needs = [task(start)(lambda near=near: self.pass_on(near)) for near in (1, 0)]
            self.needs += [start, task(start)(self.rest)]

    class Spread:
        def __init__(self, buf):
            self.buf = buf
            self.ids, self.out = [cp.recv(3) for _ in micros], cp.send()

        def ref(self, b, m):
            return self.buf.at[at(b * rows + m * slot, slot)]

        def start(self, m):
            own, n = self.ref(r, m), self.ids[m]
            cp.start(lambda: (own, own, self.out, n + 1, f, xn))
            cp.start(lambda: (own, own, self.out, n, f, cn))

        def forward(self, m):
            got, n = self.ref(xn, m), self.ids[m]
            cp.arrived(got, n + 1, f, r)
            cp.start(lambda: (got, got, self.out, n + 2, f, cn))

        def got(self, b):
            for m in micros:
                if b is cn:
                    cp.arrived(self.ref(cn, m), self.ids[m], f, r)
                elif b is dn:
                    cp.arrived(self.ref(dn, m), self.ids[m] + 2, f, r)

        def register(self, deps):
            forward = [task(*deps)(lambda m=m: self.forward(m)) for m in micros]
            got = [task(*deps)(lambda b=b: self.got(b)) for b in (cn, dn)]
            self.need = [[got[1]], forward, [got[0]], list(deps)]
            self.all = [*forward, *got, *deps]

        def free(self):
            cp.gone(self.buf.at[pl.ds(0, 3 * rows)], self.out, f, r)

    class Sum:
        def __init__(self, part, sib, xsend, xrecv):
            self.part, self.sib, self.xsend, self.xrecv = part, sib, xsend, xrecv
            self.ids, self.xids, self.out, self.xout = cp.recv(2), cp.recv(micro), cp.send(), cp.send()

        def ready(self, w):
            if w not in (DN, CN):
                return
            b, i = (dn, 0) if w == DN else (cn, 1)
            src = self.part.at[block(b)]
            cp.start(lambda: (src, self.sib.at[i], self.out, self.ids + i, f, cn))

        def over_x(self):
            cp.arrived(self.sib.at[0], self.ids, f, r)
            for m in micros:

                def add(t, m=m):
                    s = at(m * slot + t * 32, 32)
                    self.xsend[s, :] = (
                        self.part[at(xn * rows + m * slot + t * 32, 32), :] + self.sib[0, s, :]
                    ).astype(BF16)

                loop(slot // 32, add)
                mm = at(m * slot, slot)
                cp.start(lambda m=m, mm=mm: (self.xsend.at[mm], self.xrecv.at[mm], self.xout, self.xids + m, f, xn))

        def done(self, m):
            if m == 0:
                cp.arrived(self.sib.at[1], self.ids + 1, f, r)
            cp.arrived(self.xrecv.at[at(m * slot, slot)], self.xids + m, f, r)

        def value(self, row, n):
            s = at(row, n)
            return self.part[at(r * rows + row, n), :] + self.sib[1, s, :] + self.xrecv[s, :].astype(F32)

        def free(self):
            cp.gone(self.part.at[pl.ds(0, 2 * rows)], self.out, f, r)
            cp.gone(self.xsend, self.xout, f, r)

    def add_into(dst, doff, src, n):
        def step(t):
            s = at(doff + t * 16, 16)
            dst[s, :] = (dst[s, :].astype(F32) + src[at(t * 16, 16), :].astype(F32)).astype(BF16)

        loop(n // 16, step)

    class ColumnReduce:
        def __init__(self, grad, yr, zr, out, col, width):
            self.grad, self.yr, self.zr, self.out = grad, yr, zr, out
            self.col, self.width = col, width
            self.yrecv, self.zrecv, self.orecv = cp.recv(NZ), cp.recv(NZ + 1), cp.recv(2)
            self.ysend, self.zsend, self.osend = cp.send(), cp.send(), cp.send()
            self.lid = lid()
            for n, send in ((NZ, self.ysend), (NZ - 1, self.zsend), (3, self.osend)):
                cp.at_end(grad.at[pl.ds(0, n * sh)], send)

        def send(self, j):
            zz = lax.div(j, 2)
            cp.start(lambda: (self.grad.at[at(j * sh, sh)], self.yr.at[zz], self.ysend, self.yrecv + zz, yn, r))

        def add_y(self, j):
            zz = lax.div(j, 2)
            cp.arrived(self.yr.at[zz], self.yrecv + zz, f, r)
            add_into(self.grad, j * sh, self.yr.at[zz], sh)

        def chain(self, i):
            owner, up, there = by_z(*OWNERS[i]), by_z(*OWNER_ABOVE[i]), by_z(*OWNER_SLOT[i])
            j = 2 * owner + y
            self.add_y(j)

            @pl.when(inner)
            def _():
                cp.arrived(self.zr.at[owner], self.zrecv + owner, f, r)
                add_into(self.grad, j * sh, self.zr.at[owner], sh)

            cp.start(
                lambda: (
                    self.grad.at[at(j * sh, sh)], self.zr.at[there], self.zsend, self.zrecv + there,
                    f + 2 * (2 * up - 1), r,
                )
            )

        def final(self):
            self.add_y(f)
            for slot_, cond in ((z, z > 0), (NZ, z < NZ - 1)):

                @pl.when(cond)
                def _(slot_=slot_):
                    cp.arrived(self.zr.at[slot_], self.zrecv + slot_, f, r)
                    add_into(self.grad, f * sh, self.zr.at[slot_], sh)

            src = self.grad.at[at(f * sh, sh)]
            for i, to in enumerate((xn, cn)):
                cp.start(lambda i=i, to=to: (src, self.dst(r), self.osend, self.orecv + i, f, to))
            ends.append(local(src, self.dst(r), self.lid))

        def dst(self, q):
            return self.out.at[q, :, at(self.col, self.width, 128)]

        def relay(self):
            got = self.dst(xn)
            cp.arrived(got, self.orecv, f, r)
            cp.start(lambda: (got, got, self.osend, self.orecv + 1, f, cn))

        def done(self):
            cp.arrived(self.out.at[pl.ds(0, 2), :, at(self.col, self.width, 128)], self.orecv + 1, f, r)

        def register(self, *deps):
            steps = [task(*deps)(lambda i=i: self.chain(i)) for i in range(NZ - 1)]
            final = task(*deps)(self.final)
            task(final)(self.relay)

    class LongRowReduce:
        def __init__(self, grad, yr, zr, out, row, height, pitch):
            self.grad, self.yr, self.zr, self.out = grad, yr, zr, out
            self.row, self.height, self.pitch = row, height, pitch
            self.yrecv, self.zrecv, self.orecv = cp.recv(), cp.recv(2), cp.recv(2)
            self.ysend, self.zsend, self.osend = cp.send(), cp.send(), cp.send()
            self.lid = lid()
            one = self.grad.at[self.rows(y)]
            cp.at_end(one, self.ysend)
            cp.at_end(one, self.zsend, z != r)
            cp.at_end(self.grad.at[pl.ds(0, 2 * height)], self.osend, z == r)
            cp.at_end(one, self.osend, z == xn)

        def rows(self, yy):
            return at(yy * self.pitch + self.row, self.height)

        def send(self):
            cp.start(lambda: (self.grad.at[self.rows(1 - y)], self.yr, self.ysend, self.yrecv, yn, r))

        def add(self, way):
            cp.arrived(self.zr.at[way], self.zrecv + way, f, r)
            add_into(self.grad, y * self.pitch + self.row, self.zr.at[way], self.height)

        def chain(self):
            cp.arrived(self.yr, self.yrecv, f, r)
            add_into(self.grad, y * self.pitch + self.row, self.yr, self.height)
            src = self.grad.at[self.rows(y)]
            for way, (toward, behind, step) in enumerate(((z < r, z > 0, 2), (z > r, z < NZ - 1, -2))):

                @pl.when(jnp.logical_and(toward, behind))
                def _(way=way):
                    self.add(way)

                cp.start(
                    lambda way=way, step=step: (src, self.zr.at[way], self.zsend, self.zrecv + way, f + step, r), toward
                )

        def dst(self):
            return self.out.at[at(self.row, self.height)]

        def final(self):
            for way, cond in enumerate((z > 0, z < NZ - 1)):

                @pl.when(jnp.logical_and(z == r, cond))
                def _(way=way):
                    self.add(way)

            src = self.grad.at[self.rows(y)]
            for i, to in enumerate((xn, cn)):
                cp.start(lambda i=i, to=to: (src, self.dst(), self.osend, self.orecv + i, f, to), z == r)

            @pl.when(z == r)
            def _():
                local(src, self.dst(), self.lid)

        def relay(self):
            got = self.dst()

            @pl.when(z == xn)
            def _():
                cp.arrived(got, self.orecv, f, r)

            cp.start(lambda: (got, got, self.osend, self.orecv + 1, f, cn), z == xn)

        def done(self):
            @pl.when(jnp.logical_or(z == cn, z == dn))
            def _():
                cp.arrived(self.dst(), self.orecv + 1, f, r)

            @pl.when(z == r)
            def _():
                pltpu.make_async_copy(self.grad.at[self.rows(y)], self.dst(), k.locals.at[self.lid]).wait()

        def register(self, *deps):
            chain = task(*deps)(self.chain)
            task(task(chain)(self.final))(self.relay)

    class RowReduce:
        def __init__(self, grad, yr, zr, out, row, height, pitch):
            self.grad, self.yr, self.zr, self.out = grad, yr, zr, out
            self.row, self.height, self.pitch = row, height, pitch
            self.yrecv, self.zrecv, self.orecv = cp.recv(), cp.recv(4), cp.recv(2)
            self.ysend, self.zsend, self.osend = cp.send(), cp.send(2), cp.send()
            self.lid = lid()
            one = self.grad.at[self.rows(y)]
            cp.at_end(one, self.ysend, z == r)
            for n in range(2):
                cp.at_end(one, self.zsend + n, z != r)
            cp.at_end(self.grad.at[pl.ds(0, 2 * height)], self.osend, z == r)
            cp.at_end(one, self.osend, z == xn)

        def rows(self, yy):
            return at(yy * self.pitch + self.row, self.height)

        def add(self, yy, way):
            cp.arrived(self.zr.at[way, yy], self.zrecv + 2 * way + yy, f, r)
            add_into(self.grad, yy * self.pitch + self.row, self.zr.at[way, yy], self.height)

        def chain(self, far):
            yy = 1 - y if far else y
            src = self.grad.at[self.rows(yy)]
            for way, (toward, behind, step) in enumerate(((z < r, z > 0, 2), (z > r, z < NZ - 1, -2))):

                @pl.when(jnp.logical_and(toward, behind))
                def _(way=way):
                    self.add(yy, way)

                cp.start(
                    lambda way=way, step=step: (
                        src, self.zr.at[way, yy], self.zsend + far, self.zrecv + 2 * way + yy, f + step, r
                    ),
                    toward,
                )

        def gathered(self, yy):
            for way, cond in enumerate((z > 0, z < NZ - 1)):

                @pl.when(jnp.logical_and(z == r, cond))
                def _(way=way):
                    self.add(yy, way)

        def cross(self):
            self.gathered(1 - y)
            cp.start(lambda: (self.grad.at[self.rows(1 - y)], self.yr, self.ysend, self.yrecv, yn, r), z == r)

        def dst(self):
            return self.out.at[at(self.row, self.height)]

        def final(self):
            self.gathered(y)

            @pl.when(z == r)
            def _():
                cp.arrived(self.yr, self.yrecv, f, r)
                add_into(self.grad, y * self.pitch + self.row, self.yr, self.height)

            src = self.grad.at[self.rows(y)]
            for i, to in enumerate((xn, cn)):
                cp.start(lambda i=i, to=to: (src, self.dst(), self.osend, self.orecv + i, f, to), z == r)

            @pl.when(z == r)
            def _():
                local(src, self.dst(), self.lid)

        def relay(self):
            got = self.dst()

            @pl.when(z == xn)
            def _():
                cp.arrived(got, self.orecv, f, r)

            cp.start(lambda: (got, got, self.osend, self.orecv + 1, f, cn), z == xn)

        def done(self):
            @pl.when(jnp.logical_or(z == cn, z == dn))
            def _():
                cp.arrived(self.dst(), self.orecv + 1, f, r)

            @pl.when(z == r)
            def _():
                pltpu.make_async_copy(self.grad.at[self.rows(y)], self.dst(), k.locals.at[self.lid]).wait()

        def register(self, *deps):
            chains = [task(*deps)(lambda far=far: self.chain(far)) for far in (1, 0)]
            cross = task(*chains)(self.cross)
            task(task(cross)(self.final))(self.relay)

    class Deal:
        def __init__(self, src, dst):
            self.src, self.dst, self.recvs, self.sends = src, dst, cp.recv(micro), cp.send(micro)
            self.lid = lid(micro)
            self.local = {}
            for m in micros:
                cp.at_end(self.most(), self.sends + m)

        def most(self):
            return self.dst.at[pl.ds(0, (NF - 1) * part)]

        def start(self, m):
            dst = self.dst.at[at(m * slot + f * part, part)]
            for o in others:
                cp.start(lambda o=o: (self.src.at[m, o], dst, self.sends + m, self.recvs + m, o, r))
            self.local[m] = local(self.src.at[m, f], dst, self.lid + m)

        def done(self, m):
            cp.arrived(self.most(), self.recvs + m, f, r)
            self.local[m].wait()

    class Back:
        def __init__(self, src, dst):
            self.src, self.dst, self.recvs, self.sends = src, dst, cp.recv(micro), cp.send(micro)
            self.lid = lid(micro)
            for m in micros:
                cp.at_end(self.most(), self.sends + m)

        def most(self):
            return self.src.at[pl.ds(0, (NF - 1) * part)]

        def start(self, m):
            for o in others:
                cp.start(
                    lambda o=o: (
                        self.src.at[at(m * slot + o * part, part)], self.dst.at[m, f], self.sends + m, self.recvs + m, o, r
                    )
                )
            ends.append(local(self.src.at[at(m * slot + f * part, part)], self.dst.at[m, f], self.lid + m))

        def done(self):
            for m in micros:
                cp.arrived(self.dst.at[m, pl.ds(0, NF - 1)], self.recvs + m, f, r)

    count = iter(range(k.locals.shape[0]))

    def lid(n=1):
        first = next(count)
        for _ in range(n - 1):
            next(count)
        return first

    t2 = 2 * sz.tile
    hq = sz.hq
    third, half = sz.ffp // 3, sh // 2
    smalls, lens, gains = k.smalls, k.lens, k.gains
    aall, hall, call, yall = k.aall, k.hall, k.call, k.yall
    part_, gg, slope, dw, dqkv = k.part, k.gg, k.slope, k.dw, k.dqkv
    gd, gi, go, gq, dg = k.gd, k.gi, k.go, k.gq, k.dg
    xs, cs, hbuf, dhbuf, mx, gt = k.xs, k.cs, k.hbuf, k.dhbuf, k.mx, k.gt
    qkv, pbuf, obuf = k.qkv, k.pbuf, k.obuf
    g_q = ColumnGather(wq, 0, 3 * hq)
    g_o = [RowGather(wo, i * half, half, sh) for i in range(2)]
    g_i = [ColumnGather(wi, n * t2, t2) for n in range(sz.ntile)]
    g_d = [LongRowGather(wd, i * third, third, sz.ffp) for i in range(3)]
    r_d = [LongRowReduce(gd, k.yrd.at[i], k.zrd.at[i], k.rd, i * third, third, sz.ffp) for i in range(3)]
    r_i = [
        ColumnReduce(gi.at[n], k.yri.at[n], k.zri.at[n], k.ri, n * t2, t2) for n in range(sz.ntile)
    ]
    r_o = [RowReduce(go, k.yro.at[i], k.zro.at[i], k.ro, i * half, half, sh) for i in range(2)]
    r_q = [ColumnReduce(gq.at[n], k.yrq.at[n], k.zrq.at[n], k.rq, n * hq, hq) for n in range(3)]
    small_in, len_in, gs_in, gr_in = (cp.recv() for _ in range(4))
    small_out, len_out, gs_out, gr_out = (cp.send() for _ in range(4))
    cp.at_end(smalls.at[pl.ds(0, NF - 1)], small_out)
    cp.at_end(lens.at[pl.ds(0, NR - 1)], len_out)
    cp.at_end(k.gsend.at[pl.ds(0, NF - 1)], gs_out)
    cp.at_end(k.greps.at[pl.ds(0, NR - 1)], gr_out)
    deal_x, deal_c = Deal(k.tok, xs), Deal(k.cot, cs)
    back_m, back_t = Back(mx, k.o_mixed), Back(gt, k.o_gtok)
    e_a, e_c, e_h, e_y = Spread(aall), Spread(call), Spread(hall), Spread(yall)
    s_1 = Sum(part_, k.sib0, k.xsend, k.xrecv0)
    s_m = Sum(part_, k.sib1, k.xsend, k.xrecv1)
    s_h = Sum(part_, k.sib0, k.xsend, k.xrecv0)
    s_a = Sum(part_, k.sib0, k.xsend, k.xrecv0)
    blocks = [dn, xn, cn, r]

    lane = lax.broadcasted_iota(jnp.int32, (1, 128), 1)
    front = lax.rem(lane, 64) < 32
    low = lane < 64
    low_b = low.astype(F32).astype(BF16)
    high_b = (1.0 - low.astype(F32)).astype(BF16)
    npair = hq // 128
    scale = 64 ** (-0.5)
    tile_ = sz.tile
    NL = 32

    def live(m, t, n):
        pos = lax.broadcasted_iota(jnp.int32, (n, 1), 0) + t * n
        return pos.astype(F32) < lens[r, m : m + 1, 0:1]

    def normed(v):
        center = v - jnp.mean(v, axis=-1, keepdims=True)
        root = lax.rsqrt(jnp.mean(center * center, axis=-1, keepdims=True) + NORM_EPS)
        return center * root, root

    def norm_back(dy, gain, vhat, root):
        e = dy * gain
        return root * (e - jnp.mean(e, axis=-1, keepdims=True) - vhat * jnp.mean(e * vhat, axis=-1, keepdims=True))

    def swap(v):
        return jnp.where(front, pltpu.roll(v, 96, 1), pltpu.roll(v, 32, 1))

    def both(v):
        return jnp.concatenate([v * low_b, v * high_b], axis=0)

    def joined(v):
        return jnp.where(low, v[:slot], v[slot:])

    def fold(v):
        return jnp.sum(v.reshape(NL // 8, 8, d), axis=0)

    def triple(s, p):
        return [qkv[at(s * slot, slot), i * hq + p * 128 : i * hq + (p + 1) * 128] for i in range(3)]

    own_small = local(k.small, smalls.at[f], lid())
    qf, of = k.hbuf.at[pl.ds(0, sh)], k.hbuf.at[pl.ds(sh, sh)]
    q_in = [local(k.fq.at[:, at(i * d + r * hq, hq, 128)], qf.at[:, pl.ds(i * hq, hq)], lid()) for i in range(3)]
    o_lid, i_in, d_lid = lid(), [], lid(2)
    mine = z == r
    df = [k.sib1.at[0], k.sib1.at[1, pl.ds(0, sz.ffs - rows)]]
    d_parts = [(k.fd.at[pl.ds(0, rows)], df[0]), (k.fd.at[pl.ds(rows, sz.ffs - rows)], df[1])]

    @pl.when(mine)
    def _():
        local(k.fo, of, o_lid)

    shifts = []
    for i in range(2):
        first = i * NF * sz.ffs + r * 2 * sz.ffs
        base = lax.div(first, 128) * 128
        shifts.append(first - base)
        i_in.append(local(k.fi.at[:, at(base, sz.fq, 128)], k.dhbuf.at[pl.ds(i * sh, sh), pl.ds(0, sz.fq)], lid()))

    @pl.when(mine)
    def _():
        for n, (src, dst) in enumerate(d_parts):
            local(src, dst, d_lid + n)

    @task()
    def met():
        pl.semaphore_wait(barrier, len(friends))
        for o in others:
            cp.start(lambda o=o: (k.small, smalls.at[f], small_out, small_in, o, r))

    @task()
    def prepare_q():
        for copy in q_in:
            copy.wait()

        def cast_q(t):
            wq[at(f * sh + t * 32, 32), :] = qf[at(t * 32, 32), pl.ds(0, 3 * hq)].astype(BF16)

        loop(sh // 32, cast_q)

    @task()
    def prepare_o():
        @pl.when(mine)
        def _():
            pltpu.make_async_copy(k.fo, of, k.locals.at[o_lid]).wait()

            def cast_o(t):
                wo[at(y * sh + t * 32, 32), :] = of[at(t * 32, 32), :].astype(BF16)

            loop(sh // 32, cast_o)

    @task()
    def prepare_i():
        for i in range(2):
            i_in[i].wait()
        lane_f = lax.broadcasted_iota(jnp.int32, (1, sz.fq), 1)
        first = lane_f < sz.ffs
        second = jnp.logical_and(lane_f >= sz.ffp, lane_f < sz.ffp + sz.ffs)

        def cast_i(t):
            for i in range(2):
                v = k.dhbuf[at(i * sh + t * 32, 32), pl.ds(0, sz.fq)]
                v = pltpu.roll(v, lax.rem(sz.fq - shifts[i], sz.fq), 1)
                v = jnp.where(first, v, jnp.where(second, pltpu.roll(v, sz.ffp - sz.ffs, 1), 0.0)).astype(BF16)
                for n in range(sz.ntile):
                    wi[at(f * sh + t * 32, 32), n * t2 + i * tile_ : n * t2 + (i + 1) * tile_] = v[
                        :, n * tile_ : (n + 1) * tile_
                    ]

        loop(sh // 32, cast_i)

    @task()
    def prepare_d():
        @pl.when(mine)
        def _():
            for n, (src, dst) in enumerate(d_parts):
                pltpu.make_async_copy(src, dst, k.locals.at[d_lid + n]).wait()
            for n, ref in enumerate(df):

                def cast_d(t, n=n, ref=ref):
                    wd[at(y * sz.ffp + n * rows + t * 16, 16), :] = ref[at(t * 16, 16), :].astype(BF16)

                loop(ref.shape[0] // 16, cast_d)
            left = sz.ffs % 16
            if left:
                v = df[1][ref.shape[0] - left :, :]
                v = jnp.concatenate([v, jnp.zeros((sz.ffp - sz.ffs, d), F32)], axis=0)
                wd[at(y * sz.ffp + sz.ffp - 16, 16), :] = v.astype(BF16)

    g_q.register(met, prepare_q)
    for u in g_o:
        u.register(met, prepare_o)
    for u in g_i:
        u.register(met, prepare_i)
    for u in g_d:
        u.register(met, prepare_d)
    q_needs, o_needs, i_needs, d_needs = [[n for u in g for n in u.needs] for g in ([g_q], g_o, g_i, g_d)]

    @task()
    def zero():
        wd[pl.ds(2 * sz.ffp, sz.fq - 2 * sz.ffp), :] = jnp.zeros((sz.fq - 2 * sz.ffp, d), BF16)
        dg[...] = jnp.zeros_like(dg)

    deals = [task(met)(lambda m=m: deal_x.start(m)) for m in micros]

    @task(met)
    def small():
        own_small.wait()
        cp.arrived(smalls.at[pl.ds(0, NF - 1)], small_in, f, r)
        for j in range(NF):
            gains[0:2, j * sh : (j + 1) * sh] = smalls[j, 0:2, :]
        sub = lax.broadcasted_iota(jnp.int32, (NF, 128), 0)
        row8 = lax.broadcasted_iota(jnp.int32, (8, 128), 0)
        ownrow = smalls[f]
        len_tab = smalls[:, 2, :]
        table = jnp.zeros((8, 128), F32)
        for m in micros:
            dealt = jnp.sum(jnp.where(lane == f, ownrow[3 + m : 4 + m, :], 0.0), axis=1, keepdims=True)
            col = jnp.sum(jnp.where(sub.astype(F32) == dealt, len_tab, 0.0), axis=0, keepdims=True)
            length = jnp.sum(jnp.where(lane == m, col, 0.0), axis=1, keepdims=True)
            table = jnp.where(row8 == m, length, table)
        lens[r] = table
        for to in (xn, dn, cn):
            cp.start(lambda to=to: (lens.at[r], lens.at[r], len_out, len_in, f, to))

    @task(small)
    def lengths():
        cp.arrived(lens.at[pl.ds(0, NR - 1)], len_in, f, r)

    norm1s = []
    for m in micros:

        @task(small, deals[m])
        def step(m=m):
            deal_x.done(m)

            def norm1(t):
                vhat, _ = normed(xs[at(m * slot + t * NL, NL), :].astype(F32))
                aall[at(r * rows + m * slot + t * NL, NL), :] = (vhat * gains[0:1, :]).astype(BF16)

            loop(slot // NL, norm1)
            e_a.start(m)

        norm1s.append(step)
    e_a.register(norm1s)

    def project(b):
        a = aall[block(b), :]
        for i in range(3):
            t = nn(a, wq[:, i * hq : (i + 1) * hq])
            for p in range(npair):
                v = t[:, p * 128 : (p + 1) * 128]
                for m in micros:
                    u = v[m * slot : (m + 1) * slot]
                    if i < 2:
                        u = u * k.cos[...] + swap(u) * k.sin[...]
                    qkv[at(b * rows + m * slot, slot), i * hq + p * 128 : i * hq + (p + 1) * 128] = u.astype(BF16)

    def attend(b):
        def attend_one(m):
            s = b * micro + m
            length = lens[b, pl.ds(m, 1), :]
            for p in range(npair):
                q_, k_, v_ = triple(s, p)
                scores = nt(both(q_), k_) * scale
                scores = jnp.where(lane.astype(F32) < length, scores, -1e30)
                e = jnp.exp(scores - jnp.max(scores, axis=-1, keepdims=True))
                prob = e / jnp.sum(e, axis=-1, keepdims=True)
                pbuf[s, p] = prob
                out = nn(prob.astype(BF16), v_)
                obuf[at(s * slot, slot), p * 128 : (p + 1) * 128] = joined(out).astype(BF16)

        loop(micro, attend_one)

    def branch_one(b):
        def branch_tile(n):
            cols = at(n * 256, 256, 128)
            part_[block(b), cols] = nn(obuf[block(b), :], wo[:, cols])

        loop(d // 256, branch_tile)

    firsts = []
    for w in range(NR):

        @task(*e_a.need[w], *q_needs)
        def projected(w=w):
            project(blocks[w])

        @task(projected, lengths, *o_needs)
        def attended(w=w):
            attend(blocks[w])
            branch_one(blocks[w])
            s_1.ready(w)

        firsts.append(attended)
    crossed = task(firsts[DN], firsts[XN])(s_1.over_x)

    masks = []
    for m in micros:
        dealt = task(met)(lambda m=m: deal_c.start(m))

        @task(dealt, small)
        def step(m=m):
            deal_c.done(m)

            def mask_c(t):
                s = at(m * slot + t * NL, NL)
                masked = jnp.where(live(m, t, NL), cs[s, :].astype(F32), 0.0)
                call[at(r * rows + m * slot + t * NL, NL), :] = masked.astype(BF16)

            loop(slot // NL, mask_c)

        masks.append(step)

    @task(*masks)
    def spread_c():
        for m in micros:
            e_c.start(m)

    e_c.register([spread_c])

    norm2s = []
    for m in micros:

        @task(crossed, *firsts, *norm2s)
        def step(m=m):
            s_1.done(m)

            def norm2(t):
                row = m * slot + t * NL
                s = at(row, NL)
                h = xs[s, :].astype(F32) + jnp.where(live(m, t, NL), s_1.value(row, NL), 0.0)
                hbuf[s, :] = h
                vhat, _ = normed(h)
                hall[at(r * rows + row, NL), :] = (vhat * gains[1:2, :]).astype(BF16)

            loop(slot // NL, norm2)
            e_h.start(m)

        norm2s.append(step)
    freed = task(*norm2s)(s_1.free)
    e_h.register(norm2s)

    feeds = []
    for w in range(NR):

        @task(freed, *e_h.need[w], *i_needs)
        def step(w=w):
            rs = block(blocks[w])

            def feed(n):
                v = nn(hall[rs, :], wi[:, at(n * t2, t2, 128)])
                w1, w2 = v[:, :tile_], v[:, tile_:]
                cdf = 0.5 * (1.0 + lax.erf(w1 * (0.5**0.5)))
                act = w1 * cdf
                pdf = jnp.exp(-0.5 * w1 * w1) * 0.3989422804014327
                cols = at(n * tile_, tile_, 128)
                gg[rs, cols] = (act * w2).astype(BF16)
                part_[rs, cols] = act
                slope[rs, cols] = w2 * (cdf + w1 * pdf)

            loop(sz.ntile, feed)

        feeds.append(step)

    @task(*feeds, *e_c.all)
    def gdown():
        def grad_down(i):
            m, n = lax.div(i, 2), lax.rem(i, 2)
            cols = at(n * (d // 2), d // 2, 128)
            gd[at(m * 256, 256), cols] = tn(gg[:, at(m * 256, 256, 128)], call[:, cols]).astype(BF16)

        loop(sz.fq // 256 * 2, grad_down)
        for u in r_d:
            u.send()

    hids = []
    for w in range(NR):

        @task(feeds[w], zero, *e_c.need[w], *d_needs)
        def step(w=w):
            rs = block(blocks[w])

            def hidden(n):
                cols = at(n * tile_, tile_, 128)
                dgg = nt(call[rs, :], wd[at(n * tile_, tile_), :])
                dw[rs, at(n * t2, tile_, 128)] = (dgg * slope[rs, cols]).astype(BF16)
                dw[rs, at(n * t2 + tile_, tile_, 128)] = (dgg * part_[rs, cols]).astype(BF16)

            loop(sz.ntile, hidden)

        hids.append(step)

    gins = []
    for n in range(sz.ntile):
        for which in range(2):

            @task(*hids, *e_h.all)
            def step(n=n, which=which):
                def grad_in(i):
                    j = 2 * i + (y if which else 1 - y)
                    gi[n, at(j * sh, sh), :] = tn(
                        hall[:, at(j * sh, sh, 128)], dw[:, at(n * t2, t2, 128)]
                    ).astype(BF16)

                loop(NZ, grad_in)
                if not which:
                    for owner in order_z:
                        r_i[n].send(2 * owner + 1 - y)

            gins.append(step)

    dhns = []
    for w in range(NR):

        @task(hids[w])
        def step(w=w):
            b = blocks[w]

            def dhn_tile(n):
                part_[block(b), at(n * 256, 256, 128)] = nt(dw[block(b), :], wi[at(n * 256, 256), :])

            loop(d // 256, dhn_tile)
            s_h.ready(w)

        dhns.append(step)
    crossed = task(dhns[DN], dhns[XN])(s_h.over_x)
    back2s = []
    for m in micros:

        @task(crossed, zero, *dhns, *back2s)
        def step(m=m):
            s_h.done(m)

            def back2(t):
                row = m * slot + t * NL
                s = at(row, NL)
                dy = s_h.value(row, NL)
                vhat, root = normed(hbuf[s, :])
                dg[1] += fold(dy * vhat)
                dh = cs[s, :].astype(F32) + norm_back(dy, gains[1:2, :], vhat, root)
                dhbuf[s, :] = dh
                yall[at(r * rows + row, NL), :] = jnp.where(live(m, t, NL), dh, 0.0).astype(BF16)

            loop(slot // NL, back2)
            e_y.start(m)

        back2s.append(step)
    freed = task(*back2s)(s_h.free)
    e_y.register(back2s)

    mixes = []
    for w in range(NR):

        @task(freed, zero, feeds[w], *d_needs)
        def step(w=w):
            b = blocks[w]

            def mix_tile(n):
                cols = at(n * 256, 256, 128)
                part_[block(b), cols] = nn(gg[block(b), :], wd[:, cols])

            loop(d // 256, mix_tile)
            s_m.ready(w)

        mixes.append(step)
    crossed = task(mixes[DN], mixes[XN])(s_m.over_x)
    mixeds = []
    for m in micros:

        @task(crossed, *mixes, *mixeds)
        def step(m=m):
            s_m.done(m)

            def mix(t):
                row = m * slot + t * NL
                s = at(row, NL)
                mx[s, :] = (hbuf[s, :] + jnp.where(live(m, t, NL), s_m.value(row, NL), 0.0)).astype(BF16)

            loop(slot // NL, mix)

        mixeds.append(step)
        task(step)(lambda m=m: back_m.start(m))
    freed = task(*mixeds)(s_m.free)

    @task(*firsts, *e_y.all)
    def gout():
        def grad_out(i):
            cols = at(i * 256, 256, 128)
            go[:, cols] = tn(obuf[...], yall[:, cols]).astype(BF16)

        loop(d // 256, grad_out)

    abacks = []
    for w in range(NR):

        @task(firsts[w], *e_y.need[w])
        def step(w=w):
            def attend_back(m):
                s = blocks[w] * micro + m
                do_all = nt(yall[at(s * slot, slot), :], wo[...]).astype(BF16)
                for p in range(npair):
                    q_, k_, v_ = triple(s, p)
                    q2, do2 = both(q_), both(do_all[:, p * 128 : (p + 1) * 128])
                    prob = pbuf[s, p]
                    dp = nt(do2, v_)
                    ds = (prob * (dp - jnp.sum(dp * prob, axis=-1, keepdims=True))).astype(BF16)
                    dq = joined(nn(ds, k_)) * scale
                    dk = tn(ds, q2) * scale
                    dv = tn(prob.astype(BF16), do2)
                    cosine, sine = k.cos[...], k.sin[...]
                    dq = dq * cosine - swap(dq) * sine
                    dk = dk * cosine - swap(dk) * sine
                    for i, v in enumerate((dq, dk, dv)):
                        dqkv[at(s * slot, slot), i * hq + p * 128 : i * hq + (p + 1) * 128] = v.astype(BF16)

            loop(micro, attend_back)

        abacks.append(step)

    gqkvs = []
    for which in range(2):

        @task(*abacks, *e_a.all)
        def step(which=which):
            def grad_qkv(i):
                j = 2 * i + (y if which else 1 - y)
                g = tn(aall[:, at(j * sh, sh, 128)], dqkv[...]).astype(BF16)
                for n in range(3):
                    gq[n, at(j * sh, sh), :] = g[:, n * hq : (n + 1) * hq]

            loop(NZ, grad_qkv)
            if not which:
                for n in range(3):
                    for owner in order_z:
                        r_q[n].send(2 * owner + 1 - y)

        gqkvs.append(step)

    das = []
    for w in range(NR):

        @task(abacks[w], freed)
        def step(w=w):
            b = blocks[w]

            def da_tile(n):
                part_[block(b), at(n * 256, 256, 128)] = nt(dqkv[block(b), :], wq[at(n * 256, 256), :])

            loop(d // 256, da_tile)
            s_a.ready(w)

        das.append(step)
    crossed = task(das[DN], das[XN])(s_a.over_x)
    back1s = []
    for m in micros:

        @task(crossed, *das, *back1s)
        def step(m=m):
            s_a.done(m)

            def back1(t):
                row = m * slot + t * NL
                s = at(row, NL)
                dy = s_a.value(row, NL)
                vhat, root = normed(xs[s, :].astype(F32))
                dg[0] += fold(dy * vhat)
                gt[s, :] = (dhbuf[s, :] + norm_back(dy, gains[0:1, :], vhat, root)).astype(BF16)

            loop(slot // NL, back1)
            back_t.start(m)

        back1s.append(step)

    gsend, gslots, greps, gout_ = k.gsend, k.gslots, k.greps, k.gout

    @task(*back1s, *back2s)
    def gain_parts():
        for which in range(2):
            total = jnp.sum(dg[which], axis=0, keepdims=True)
            for j in range(NF):
                gsend[j, which : which + 1, :] = total[:, j * sh : (j + 1) * sh]
        for o in others:
            cp.start(lambda o=o: (gsend.at[o], gslots.at[f], gs_out, gs_in, o, r))
        gslots[f] = gsend[f]

    @task(gain_parts)
    def gain_sums():
        cp.arrived(gslots.at[pl.ds(0, NF - 1)], gs_in, f, r)
        total = gslots[0]
        for j in range(1, NF):
            total = total + gslots[j]
        greps[r] = total
        for to in (xn, dn, cn):
            cp.start(lambda to=to: (greps.at[r], greps.at[r], gr_out, gr_in, f, to))

    glid = lid()

    @task(gain_sums)
    def gain_totals():
        cp.arrived(greps.at[pl.ds(0, NR - 1)], gr_in, f, r)
        gout_[...] = greps[0] + greps[1] + greps[2] + greps[3]
        ends.append(local(gout_, k.o_small, glid))

    for u in r_d:
        u.register(gdown)
    for n, u in enumerate(r_i):
        u.register(*gins[2 * n : 2 * n + 2])
    for u in r_o:
        u.register(gout)
    for u in r_q:
        u.register(*gqkvs)

    @task(*range(len(tasks)))
    def end():
        for u in r_d + r_i + r_o + r_q + [back_m, back_t]:
            u.done()
        s_a.free()
        for e in (e_a, e_c, e_h, e_y):
            e.free()
        for ref, send, cond in cp.left:
            cp.gone(ref, send, f, r, cond)
        for copy in ends:
            copy.wait()

    run_tasks(tasks)


def fused(sz, tok, cot, small, cos, sin, fq, fo, fi, fd):
    d, sh, all_, rows = sz.d, sz.shard, sz.all, sz.rows
    t2 = 2 * sz.tile
    third, half = sz.ffp // 3, sh // 2
    hq3 = 3 * sz.hq
    bf = lambda *s: pltpu.VMEM(s, BF16)
    fl = lambda *s: pltpu.VMEM(s, F32)
    ins = dict(tok=tok, cot=cot, small=small, cos=cos, sin=sin, fq=fq, fo=fo, fi=fi, fd=fd)
    outs = dict(
        o_mixed=jax.ShapeDtypeStruct((sz.micro, NF, sz.part, d), BF16),
        o_gtok=jax.ShapeDtypeStruct((sz.micro, NF, sz.part, d), BF16),
        o_small=jax.ShapeDtypeStruct((8, 128), F32),
        rq=jax.ShapeDtypeStruct((NR, sh, hq3), BF16),
        ro=jax.ShapeDtypeStruct((sh, d), BF16),
        ri=jax.ShapeDtypeStruct((NR, sh, sz.ntile * t2), BF16),
        rd=jax.ShapeDtypeStruct((sz.ffp, d), BF16),
    )
    scratch = dict(
        wq=bf(d, hq3), wo=bf(2 * sh, d), wi=bf(d, sz.ntile * t2), wd=bf(sz.fq, d),
        xs=bf(rows, d), cs=bf(rows, d), mx=bf(rows, d), gt=bf(rows, d),
        aall=bf(all_, d), hall=bf(all_, d), call=bf(all_, d), yall=bf(all_, d),
        smalls=fl(NF, 8, 128), lens=fl(NR, 8, 128), gains=fl(8, d),
        qkv=bf(all_, hq3), pbuf=fl(NR * sz.micro, sz.hq // 128, 2 * sz.slot, 128), obuf=bf(all_, sz.hq),
        part=fl(all_, d), sib0=fl(2, rows, d), sib1=fl(2, rows, d),
        xsend=bf(rows, d), xrecv0=bf(rows, d), xrecv1=bf(rows, d),
        hbuf=fl(rows, d), dhbuf=fl(rows, d), dg=fl(2, 8, d),
        gg=bf(all_, sz.fq), slope=fl(all_, sz.fq), dw=bf(all_, sz.ntile * t2), dqkv=bf(all_, hq3),
        gd=bf(sz.fq, d), gi=bf(sz.ntile, d, t2), go=bf(2 * sh, d), gq=bf(3, d, sz.hq),
        yrd=bf(3, third, d), zrd=bf(3, 2, third, d),
        yri=bf(sz.ntile, NZ, sh, t2), zri=bf(sz.ntile, NZ + 1, sh, t2),
        yro=bf(2, half, d), zro=bf(2, 2, 2, half, d),
        yrq=bf(3, NZ, sh, sz.hq), zrq=bf(3, NZ + 1, sh, sz.hq),
        gsend=fl(NF, 8, 128), gslots=fl(NF, 8, 128), greps=fl(NR, 8, 128), gout=fl(8, 128),
        sends=pltpu.SemaphoreType.DMA((96,)), recvs=pltpu.SemaphoreType.DMA((184,)),
        locals=pltpu.SemaphoreType.DMA((32,)),
    )
    any_ = pl.BlockSpec(memory_space=pl.ANY)
    vmem = pl.BlockSpec(memory_space=pltpu.VMEM)
    names = (*ins, *outs, *scratch)
    return pl.pallas_call(
        functools.partial(kernel, sz, names),
        out_shape=list(outs.values()),
        in_specs=[any_] * 3 + [vmem] * 2 + [any_] * 4,
        out_specs=[any_] * len(outs),
        scratch_shapes=list(scratch.values()),
        compiler_params=pltpu.CompilerParams(collective_id=0, has_side_effects=True, vmem_limit_bytes=64 * MIB),
    )(*ins.values())


def finish_kernel(sz, rq, ro, ri, rd, gq, go, gi, gd):
    hq, t, ffs, ffp = sz.hq, sz.tile, sz.ffs, sz.ffp
    for i in range(3):
        for q in range(NR):
            gq[:, i * sz.d + q * hq : i * sz.d + (q + 1) * hq] = rq[q, :, i * hq : (i + 1) * hq].astype(F32)
    go[...] = ro[...].astype(F32)
    gd[...] = rd[...].astype(F32)
    pieces = []
    for i in range(2):
        for q in range(NR):
            v = [ri[q, :, (2 * n + i) * t : (2 * n + i + 1) * t].astype(F32) for n in range(sz.ntile)]
            v = jnp.concatenate(v, axis=1)
            pieces += [v[:, :ffs], v[:, ffp : ffp + ffs]]
    gi[...] = jnp.concatenate(pieces, axis=1)


def finish(sz, rq, ro, ri, rd):
    d, sh = sz.d, sz.shard
    steps, n = sh // 16, sz.ffp // 16
    down = -(-n // steps) * 16
    last = -(-sz.ffp // down) - 1
    row = lambda w: pl.BlockSpec((16, w), lambda i: (i, 0))
    low = pl.BlockSpec((down, d), lambda i: (jnp.minimum(i, last), 0))
    quarters = lambda w: pl.BlockSpec((NR, 16, w), lambda i: (0, i, 0))
    return pl.pallas_call(
        functools.partial(finish_kernel, sz),
        grid=(steps,),
        out_shape=[
            jax.ShapeDtypeStruct((sh, 3 * d), F32),
            jax.ShapeDtypeStruct((sh, d), F32),
            jax.ShapeDtypeStruct((sh, 2 * NF * sz.ffs), F32),
            jax.ShapeDtypeStruct((sz.ffs, d), F32),
        ],
        in_specs=[quarters(rq.shape[2]), row(d), quarters(ri.shape[2]), low],
        out_specs=[row(3 * d), row(d), row(2 * NF * sz.ffs), low],
        compiler_params=pltpu.CompilerParams(vmem_limit_bytes=60 * MIB),
    )(rq, ro, ri, rd)


def routed(tokens, cotangent, deal, lengths, ln1_gain, w_qkv, w_out, ln2_gain, w_in, w_down):
    micro, _, part, d = tokens.shape
    ffs = w_down.shape[0]
    sz = Sizes(micro, part, d, ffs)
    gain = [lax.reduce_precision(g, 8, 7)[None] for g in (ln1_gain, ln2_gain)]
    wide = lambda v: jnp.pad(v.astype(F32), ((0, 0), (0, 128 - v.shape[1])))
    small = jnp.concatenate(gain + [wide(lengths[:, 0, 0][None]), wide(deal[:, 0]), jnp.zeros((5 - micro, 128), F32)])
    half = d // HEADS // 2
    freq = np.float32(ROPE_BASE) ** (-(np.arange(half, dtype=np.float32) * np.float32(2.0 / (2 * half))))
    angles = np.arange(sz.slot, dtype=np.float32)[:, None] * freq[None, :]
    cos = jnp.asarray(np.tile(np.cos(angles), (1, 4)))
    sin = jnp.asarray(np.tile(np.concatenate([-np.sin(angles), np.sin(angles)], axis=1), (1, 2)))
    mixed, gtok, osmall, rq, ro, ri, rd = fused(sz, tokens, cotangent, small, cos, sin, w_qkv, w_out, w_in, w_down)
    g_qkv, g_out, g_in, g_down = finish(sz, rq, ro, ri, rd)
    return mixed, gtok, osmall[0], g_qkv, g_out, osmall[1], g_in, g_down


def solution(mesh):
    small = mesh.shape["fsdp"] == NF and mesh.shape["rep"] == NR
    rows = P(None, "rep", "fsdp", None)
    return jax.shard_map(
        routed if small else plain,
        mesh=mesh,
        in_specs=(
            rows, rows, P(None, "rep", None), P(None, "rep", "fsdp"),
            P("fsdp"), P("fsdp", None), P("fsdp", None), P("fsdp"), P("fsdp", None), P("fsdp", None),
        ),
        out_specs=(rows, rows, P("fsdp"), P("fsdp", None), P("fsdp", None), P("fsdp"), P("fsdp", None), P("fsdp", None)),
        check_vma=False,
    )
```

time: 1420 us -> 239 us (0.17)
  waiting for transfers between devices: 1100 us -> 0 us
  Pallas kernels: 0 us -> 232 us
  matrix products: 119 us -> 0 us
  blocking collectives: 72.5 us -> 0 us
  other arithmetic: 42.7 us -> 2.01 us
  local copies, waits for them, and re-layouts: 37 us -> 3.49 us
  starting transfers between devices: 24.5 us -> 0 us
  between operations: 16.2 us -> 0.65 us
    reduce_scatter x4 -> x0, waiting for transfers between devices: 762 us -> none  [on_device(): lax.psum_scatter(totals, 'fsdp', scatter_dimension=0, tiled=True)]
    all_gather x4 -> x0, waiting for transfers between devices: 287 us -> none  [the longest x1 146 us: on_device(): lax.all_gather(shards[4], 'fsdp', axis=0, tiled=True)]
    pallas_call x0 -> x2, Pallas kernels: none -> 232 us  [the longest x1 224 us: fused(): pl.pallas_call(functools.partial(kernel, sz, names), out_shape=list(outs....]
    dot_general x36 -> x0, matrix products: 119 us -> none  [the longest x2 24.8 us: backward_pass(): jnp.einsum('sd,sf->df', ffn_low, hidden_low, preferred_element_type=jnp.f...]
    all_gather x2 -> x0, blocking collectives: 45.1 us -> none  [the longest x1 34.4 us: on_device(): lax.all_gather(shards[3], 'fsdp', axis=0, tiled=True)]
    convert_element_type x28 -> x2, other arithmetic: 29.2 us -> 1.34 us  [routed(): wide = lambda v: jnp.pad(v.astype(F32), ((0, 0), (0, 128 - v.shape[1])))]
    psum x1 -> x0, waiting for transfers between devices: 26.6 us -> none  [on_device(): lax.psum(shortened(owned_total), 'rep')]
    all_to_all x4 -> x0, starting transfers between devices: 24 us -> none  [the longest x1 8.99 us: on_device(): lax.all_to_all(sent_grads, 'fsdp', split_axis=1, concat_axis=2, tiled=True)]
  transfers between devices with their start and end apart: 13 -> 0, of which waited for: 10 -> 0; matrix products, arithmetic and copies ran while one was open for 9% -> 0% of each run, Pallas kernels for 0% -> 0%
where the time goes in v3:
time: 239 us; the launch traced here: 238 us
  Pallas kernels  232 us (97%)
  local copies, waits for them, and re-layouts  3.49 us (1%)
    pallas_call x1, Pallas kernels, fused(): pl.pallas_call(functools.partial(kernel, sz, names), out_shape=list(outs....  224 us
    pallas_call x1, Pallas kernels, finish(): pl.pallas_call(functools.partial(finish_kernel, sz), grid=(steps,), out_s...  7.42 us

profile of v3, /device:TPU:17, one launch (start us, length us, event | category | flops | bytes accessed | tf_op | source)
XLA Modules:
  0.0 238.0 jit_solution(9208113822059034974)
XLA Ops:
  0.6 0.7 convert_bitcast_fusion
  1.3 0.7 convert_element_type.26
  2.0 0.7 reduce-precision_bitcast_fusion
  2.7 0.6 concatenate.3.refs_2_
  3.3 224.4 %shard_map.179 = (bf16[2,8,16,1024]{3,2,1,0:T(8,128)(2,1)}, bf16[2,8,16,1024]{3,2,1,0:T(8,128)(2,1)}, f32[8,128]{1,0:T(8,128)}, bf16[4,128,768]{2,1,0:T(8,128)(2...) custom-call(bf16[2,8,16,1024]{3,2,1,0:T(8,128)(2,1)} %refs_0_.1, ...), custom_call_target="tpu_custom_call" | custom-call | tf_op jit(solution)/shard_map/pallas_call | solution.py:1434
  227.7 1.3 slice_bitcast_fusion
  229.0 0.0 copy-start.1
  229.0 0.0 copy-start
  229.0 7.4 %shard_map.180 = (f32[128,3072]{1,0:T(8,128)}, f32[128,1024]{1,0:T(8,128)}, f32[128,5248]{1,0:T(8,128)}, f32[328,1024]{1,0:T(8,128)}) custom-call(bf16[4,128,768]{2,1,0:T(8,128)(2,1)} %get-tuple-element.22.rq, bf16[128,1024]{1,0:T(8,128)(2,1)} %get-tuple-element.23.ro, bf16[4,128,1536]{2,1,0:T(8,128)(2,1)} %get-tuple-element.24.ri, ...), custom_call_target="tpu_custom_call" | custom-call | tf_op jit(solution)/shard_map/pallas_call | solution.py:1468
  236.4 0.0 copy-done.1
  236.4 0.8 copy.22
  237.2 0.0 copy-done
  237.2 0.8 copy.23
  (3 shorter events, 0.0 us)
Async XLA Ops:
  229.0 7.4 %copy-start.1 = (bf16[2,8,16,1024]{3,2,1,0:T(8,128)(2,1)S(1)}, bf16[2,8,16,1024]{3,2,1,0:T(8,128)(2,1)}, u32[]{:S(2)}) copy-start(bf16[2,8,16,1024]{3,2,1,0:T(8,128)(2,1)} %get-tuple-element.42) | copy-start | bytes 1572868
  229.0 8.2 %copy-start = (bf16[2,8,16,1024]{3,2,1,0:T(8,128)(2,1)S(1)}, bf16[2,8,16,1024]{3,2,1,0:T(8,128)(2,1)}, u32[]{:S(2)}) copy-start(bf16[2,8,16,1024]{3,2,1,0:T(8,128)(2,1)} %get-tuple-element.43) | copy-start | bytes 1572868

commit v4 on v3

--- a/solution.py
+++ b/solution.py
@@ -163,6 +163,10 @@
     return lax.dot_general(a, b, (((0,), (0,)), ((), ())), preferred_element_type=F32)
 
 
+def once(i, body):
+    body(i)
+
+
 def loop(n, body):
     def step(i, carry):
         body(i)
@@ -172,14 +176,14 @@
 
 
 ORDER = (
-    2, 0, 14, 15, 62, 1, 10, 43, 4, 44, 5, 6, 3, 7, 45, 47, 23, 64, 48, 49, 63, 8, 12, 16, 50, 42, 11, 17, 65, 25,
-    52, 13, 9, 59, 24, 66, 28, 33, 51, 39, 36, 18, 57, 55, 46, 53, 54, 56, 19, 30, 61, 60, 20, 69, 21, 29, 58, 67,
-    31, 71, 22, 26, 34, 72, 68, 76, 70, 40, 75, 32, 73, 74, 27, 80, 79, 37, 81, 41, 77, 78, 82, 38, 35, 86, 83, 93,
-    85, 84, 94, 97, 132, 95, 90, 87, 138, 88, 89, 96, 135, 98, 99, 119, 141, 100, 105, 142, 103, 118, 146, 92, 136,
-    133, 101, 106, 102, 147, 143, 91, 104, 115, 162, 109, 116, 161, 107, 156, 148, 117, 157, 137, 120, 144, 152,
-    121, 108, 110, 111, 166, 139, 167, 112, 114, 122, 123, 171, 149, 163, 113, 176, 124, 126, 168, 151, 172, 173,
-    134, 177, 169, 178, 140, 145, 125, 158, 153, 127, 128, 150, 174, 179, 129, 159, 170, 160, 164, 154, 130, 155,
-    175, 180, 131, 165, 181,
+    2, 0, 24, 25, 72, 1, 20, 53, 4, 54, 5, 10, 15, 6, 11, 16, 3, 7, 12, 17, 55, 57, 33, 74, 58, 59, 73, 8, 13, 18,
+    22, 26, 60, 52, 21, 27, 75, 35, 62, 23, 9, 14, 19, 69, 34, 76, 38, 43, 61, 49, 46, 28, 67, 65, 56, 63, 64, 66,
+    29, 40, 71, 70, 30, 79, 31, 39, 68, 77, 41, 81, 32, 36, 44, 82, 78, 86, 80, 50, 85, 42, 83, 84, 37, 90, 89, 47,
+    91, 51, 87, 88, 92, 48, 45, 96, 93, 103, 95, 94, 104, 107, 141, 105, 100, 97, 147, 98, 99, 106, 144, 108, 109,
+    128, 150, 110, 115, 151, 113, 127, 155, 102, 145, 142, 111, 116, 112, 156, 152, 101, 114, 124, 171, 119, 125,
+    170, 117, 165, 157, 126, 166, 146, 129, 153, 161, 130, 118, 120, 121, 175, 148, 176, 122, 131, 132, 180, 158,
+    172, 123, 185, 133, 135, 177, 160, 181, 182, 143, 186, 178, 187, 149, 154, 134, 167, 162, 136, 137, 159, 183,
+    188, 138, 168, 179, 169, 173, 163, 139, 164, 184, 189, 140, 174, 190,
 )
 
 
@@ -212,6 +216,24 @@
         self.tile = 256
         self.ntile = -(-(2 * self.ffp) // self.tile)
         self.fq = self.ntile * self.tile
+        last = 2 * self.ffp - (self.ntile - 1) * self.tile
+        self.shift = -(-last // 64) * 64 if last <= self.tile - 64 else self.tile
+        self.units = [(n * 2 * self.tile, 2 * self.tile) for n in range(self.ntile - 1)]
+        self.units.append(((self.ntile - 1) * 2 * self.tile, 2 * self.shift))
+        self.iw = sum(w for _, w in self.units)
+
+
+def side_by_side(sz, n, one, two):
+    if sz.units[n][1] == 2 * sz.tile:
+        return jnp.concatenate([one, two], axis=1)
+    room = jnp.zeros((one.shape[0], sz.units[n][1] - sz.tile), F32)
+    return jnp.concatenate([one, room], axis=1) + pltpu.roll(jnp.concatenate([two, room], axis=1), sz.shift, 1)
+
+
+def apart(sz, n, v):
+    if sz.units[n][1] == 2 * sz.tile:
+        return v[:, : sz.tile], v[:, sz.tile :]
+    return v[:, : sz.tile], pltpu.roll(v, v.shape[1] - sz.shift, 1)[:, : sz.tile]
 
 
 class Copies:
@@ -801,13 +823,16 @@
     gd, gi, go, gq, dg = k.gd, k.gi, k.go, k.gq, k.dg
     xs, cs, hbuf, dhbuf, mx, gt = k.xs, k.cs, k.hbuf, k.dhbuf, k.mx, k.gt
     qkv, pbuf, obuf = k.qkv, k.pbuf, k.obuf
-    g_q = ColumnGather(wq, 0, 3 * hq)
+    g_q = [ColumnGather(wq, i * hq, hq) for i in range(3)]
     g_o = [RowGather(wo, i * half, half, sh) for i in range(2)]
-    g_i = [ColumnGather(wi, n * t2, t2) for n in range(sz.ntile)]
+    g_i = [ColumnGather(wi, col, w) for col, w in sz.units]
     g_d = [LongRowGather(wd, i * third, third, sz.ffp) for i in range(3)]
     r_d = [LongRowReduce(gd, k.yrd.at[i], k.zrd.at[i], k.rd, i * third, third, sz.ffp) for i in range(3)]
     r_i = [
-        ColumnReduce(gi.at[n], k.yri.at[n], k.zri.at[n], k.ri, n * t2, t2) for n in range(sz.ntile)
+        ColumnReduce(
+            gi.at[:, pl.ds(col, w)], k.yri.at[n, :, :, pl.ds(0, w)], k.zri.at[n, :, :, pl.ds(0, w)], k.ri, col, w
+        )
+        for n, (col, w) in enumerate(sz.units)
     ]
     r_o = [RowReduce(go, k.yro.at[i], k.zro.at[i], k.ro, i * half, half, sh) for i in range(2)]
     r_q = [ColumnReduce(gq.at[n], k.yrq.at[n], k.zrq.at[n], k.rq, n * hq, hq) for n in range(3)]
@@ -821,7 +846,7 @@
     back_m, back_t = Back(mx, k.o_mixed), Back(gt, k.o_gtok)
     e_a, e_c, e_h, e_y = Spread(aall), Spread(call), Spread(hall), Spread(yall)
     s_1 = Sum(part_, k.sib0, k.xsend, k.xrecv0)
-    s_m = Sum(part_, k.sib1, k.xsend, k.xrecv1)
+    s_m = Sum(k.part2, k.sib1, k.xsend2, k.xrecv1)
     s_h = Sum(part_, k.sib0, k.xsend, k.xrecv0)
     s_a = Sum(part_, k.sib0, k.xsend, k.xrecv0)
     blocks = [dn, xn, cn, r]
@@ -864,13 +889,18 @@
     def triple(s, p):
         return [qkv[at(s * slot, slot), i * hq + p * 128 : i * hq + (p + 1) * 128] for i in range(3)]
 
-    own_small = local(k.small, smalls.at[f], lid())
+    mini = k.mini
+    mini[...] = jnp.zeros_like(mini)
+    mini[0:1, :] = k.g1[...].astype(BF16).astype(F32)
+    mini[1:2, :] = k.g2[...].astype(BF16).astype(F32)
+    for m in micros:
+        mini[2:3, :] += jnp.where(lane == m, k.len[0:1, m : m + 1].astype(F32), 0.0)
+    smalls[f] = mini[...]
     qf, of = k.hbuf.at[pl.ds(0, sh)], k.hbuf.at[pl.ds(sh, sh)]
     q_in = [local(k.fq.at[:, at(i * d + r * hq, hq, 128)], qf.at[:, pl.ds(i * hq, hq)], lid()) for i in range(3)]
-    o_lid, i_in, d_lid = lid(), [], lid(2)
+    o_lid, i_in, d_lid = lid(), [], lid()
     mine = z == r
-    df = [k.sib1.at[0], k.sib1.at[1, pl.ds(0, sz.ffs - rows)]]
-    d_parts = [(k.fd.at[pl.ds(0, rows)], df[0]), (k.fd.at[pl.ds(rows, sz.ffs - rows)], df[1])]
+    df = k.part2.at[pl.ds(0, sz.ffs)]
 
     @pl.when(mine)
     def _():
@@ -885,14 +915,13 @@
 
     @pl.when(mine)
     def _():
-        for n, (src, dst) in enumerate(d_parts):
-            local(src, dst, d_lid + n)
+        local(k.fd, df, d_lid)
 
     @task()
     def met():
         pl.semaphore_wait(barrier, len(friends))
         for o in others:
-            cp.start(lambda o=o: (k.small, smalls.at[f], small_out, small_in, o, r))
+            cp.start(lambda o=o: (mini, smalls.at[f], small_out, small_in, o, r))
 
     @task()
     def prepare_q():
@@ -924,14 +953,14 @@
         second = jnp.logical_and(lane_f >= sz.ffp, lane_f < sz.ffp + sz.ffs)
 
         def cast_i(t):
+            halves = []
             for i in range(2):
                 v = k.dhbuf[at(i * sh + t * 32, 32), pl.ds(0, sz.fq)]
                 v = pltpu.roll(v, lax.rem(sz.fq - shifts[i], sz.fq), 1)
-                v = jnp.where(first, v, jnp.where(second, pltpu.roll(v, sz.ffp - sz.ffs, 1), 0.0)).astype(BF16)
-                for n in range(sz.ntile):
-                    wi[at(f * sh + t * 32, 32), n * t2 + i * tile_ : n * t2 + (i + 1) * tile_] = v[
-                        :, n * tile_ : (n + 1) * tile_
-                    ]
+                halves.append(jnp.where(first, v, jnp.where(second, pltpu.roll(v, sz.ffp - sz.ffs, 1), 0.0)))
+            for n, (col, w) in enumerate(sz.units):
+                one, two = [v[:, n * tile_ : (n + 1) * tile_] for v in halves]
+                wi[at(f * sh + t * 32, 32), pl.ds(col, w)] = side_by_side(sz, n, one, two).astype(BF16)
 
         loop(sh // 32, cast_i)
 
@@ -939,28 +968,27 @@
     def prepare_d():
         @pl.when(mine)
         def _():
-            for n, (src, dst) in enumerate(d_parts):
-                pltpu.make_async_copy(src, dst, k.locals.at[d_lid + n]).wait()
-            for n, ref in enumerate(df):
-
-                def cast_d(t, n=n, ref=ref):
-                    wd[at(y * sz.ffp + n * rows + t * 16, 16), :] = ref[at(t * 16, 16), :].astype(BF16)
-
-                loop(ref.shape[0] // 16, cast_d)
+            pltpu.make_async_copy(k.fd, df, k.locals.at[d_lid]).wait()
+
+            def cast_d(t):
+                wd[at(y * sz.ffp + t * 16, 16), :] = df[at(t * 16, 16), :].astype(BF16)
+
+            loop(sz.ffs // 16, cast_d)
             left = sz.ffs % 16
             if left:
-                v = df[1][ref.shape[0] - left :, :]
+                v = df[pl.ds(sz.ffs - left, left), :]
                 v = jnp.concatenate([v, jnp.zeros((sz.ffp - sz.ffs, d), F32)], axis=0)
                 wd[at(y * sz.ffp + sz.ffp - 16, 16), :] = v.astype(BF16)
 
-    g_q.register(met, prepare_q)
+    for u in g_q:
+        u.register(met, prepare_q)
     for u in g_o:
         u.register(met, prepare_o)
     for u in g_i:
         u.register(met, prepare_i)
     for u in g_d:
         u.register(met, prepare_d)
-    q_needs, o_needs, i_needs, d_needs = [[n for u in g for n in u.needs] for g in ([g_q], g_o, g_i, g_d)]
+    q_needs, o_needs, i_needs, d_needs = [[n for u in g for n in u.needs] for g in (g_q, g_o, g_i, g_d)]
 
     @task()
     def zero():
@@ -971,17 +999,17 @@
 
     @task(met)
     def small():
-        own_small.wait()
         cp.arrived(smalls.at[pl.ds(0, NF - 1)], small_in, f, r)
         for j in range(NF):
             gains[0:2, j * sh : (j + 1) * sh] = smalls[j, 0:2, :]
         sub = lax.broadcasted_iota(jnp.int32, (NF, 128), 0)
         row8 = lax.broadcasted_iota(jnp.int32, (8, 128), 0)
-        ownrow = smalls[f]
+        lane8 = lax.broadcasted_iota(jnp.int32, (1, NF), 1)
         len_tab = smalls[:, 2, :]
         table = jnp.zeros((8, 128), F32)
         for m in micros:
-            dealt = jnp.sum(jnp.where(lane == f, ownrow[3 + m : 4 + m, :], 0.0), axis=1, keepdims=True)
+            dealt = jnp.where(lane8 == f, k.deal[m : m + 1, :].astype(F32), 0.0)
+            dealt = jnp.sum(dealt, axis=1, keepdims=True)
             col = jnp.sum(jnp.where(sub.astype(F32) == dealt, len_tab, 0.0), axis=0, keepdims=True)
             length = jnp.sum(jnp.where(lane == m, col, 0.0), axis=1, keepdims=True)
             table = jnp.where(row8 == m, length, table)
@@ -1115,17 +1143,18 @@
             rs = block(blocks[w])
 
             def feed(n):
-                v = nn(hall[rs, :], wi[:, at(n * t2, t2, 128)])
-                w1, w2 = v[:, :tile_], v[:, tile_:]
+                col, w = sz.units[n]
+                w1, w2 = apart(sz, n, nn(hall[rs, :], wi[:, pl.ds(col, w)]))
                 cdf = 0.5 * (1.0 + lax.erf(w1 * (0.5**0.5)))
                 act = w1 * cdf
                 pdf = jnp.exp(-0.5 * w1 * w1) * 0.3989422804014327
-                cols = at(n * tile_, tile_, 128)
+                cols = pl.ds(n * tile_, tile_)
                 gg[rs, cols] = (act * w2).astype(BF16)
                 part_[rs, cols] = act
                 slope[rs, cols] = w2 * (cdf + w1 * pdf)
 
-            loop(sz.ntile, feed)
+            for n in range(sz.ntile):
+                once(n, feed)
 
         feeds.append(step)
 
@@ -1148,12 +1177,13 @@
             rs = block(blocks[w])
 
             def hidden(n):
-                cols = at(n * tile_, tile_, 128)
-                dgg = nt(call[rs, :], wd[at(n * tile_, tile_), :])
-                dw[rs, at(n * t2, tile_, 128)] = (dgg * slope[rs, cols]).astype(BF16)
-                dw[rs, at(n * t2 + tile_, tile_, 128)] = (dgg * part_[rs, cols]).astype(BF16)
-
-            loop(sz.ntile, hidden)
+                cols = pl.ds(n * tile_, tile_)
+                dgg = nt(call[rs, :], wd[pl.ds(n * tile_, tile_), :])
+                v = side_by_side(sz, n, dgg * slope[rs, cols], dgg * part_[rs, cols])
+                dw[rs, pl.ds(*sz.units[n])] = v.astype(BF16)
+
+            for n in range(sz.ntile):
+                once(n, hidden)
 
         hids.append(step)
 
@@ -1165,9 +1195,8 @@
             def step(n=n, which=which):
                 def grad_in(i):
                     j = 2 * i + (y if which else 1 - y)
-                    gi[n, at(j * sh, sh), :] = tn(
-                        hall[:, at(j * sh, sh, 128)], dw[:, at(n * t2, t2, 128)]
-                    ).astype(BF16)
+                    cols = pl.ds(*sz.units[n])
+                    gi[at(j * sh, sh), cols] = tn(hall[:, at(j * sh, sh, 128)], dw[:, cols]).astype(BF16)
 
                 loop(NZ, grad_in)
                 if not which:
@@ -1218,13 +1247,13 @@
     mixes = []
     for w in range(NR):
 
-        @task(freed, zero, feeds[w], *d_needs)
+        @task(zero, feeds[w], *d_needs)
         def step(w=w):
             b = blocks[w]
 
             def mix_tile(n):
                 cols = at(n * 256, 256, 128)
-                part_[block(b), cols] = nn(gg[block(b), :], wd[:, cols])
+                k.part2[block(b), cols] = nn(gg[block(b), :], wd[:, cols])
 
             loop(d // 256, mix_tile)
             s_m.ready(w)
@@ -1247,7 +1276,6 @@
 
         mixeds.append(step)
         task(step)(lambda m=m: back_m.start(m))
-    freed = task(*mixeds)(s_m.free)
 
     @task(*firsts, *e_y.all)
     def gout():
@@ -1382,6 +1410,7 @@
         for u in r_d + r_i + r_o + r_q + [back_m, back_t]:
             u.done()
         s_a.free()
+        s_m.free()
         for e in (e_a, e_c, e_h, e_y):
             e.free()
         for ref, send, cond in cp.left:
@@ -1392,40 +1421,40 @@
     run_tasks(tasks)
 
 
-def fused(sz, tok, cot, small, cos, sin, fq, fo, fi, fd):
+def fused(sz, tok, cot, g1, g2, length, deal, cos, sin, fq, fo, fi, fd):
     d, sh, all_, rows = sz.d, sz.shard, sz.all, sz.rows
     t2 = 2 * sz.tile
     third, half = sz.ffp // 3, sh // 2
     hq3 = 3 * sz.hq
     bf = lambda *s: pltpu.VMEM(s, BF16)
     fl = lambda *s: pltpu.VMEM(s, F32)
-    ins = dict(tok=tok, cot=cot, small=small, cos=cos, sin=sin, fq=fq, fo=fo, fi=fi, fd=fd)
+    ins = dict(tok=tok, cot=cot, g1=g1, g2=g2, len=length, deal=deal, cos=cos, sin=sin, fq=fq, fo=fo, fi=fi, fd=fd)
     outs = dict(
         o_mixed=jax.ShapeDtypeStruct((sz.micro, NF, sz.part, d), BF16),
         o_gtok=jax.ShapeDtypeStruct((sz.micro, NF, sz.part, d), BF16),
         o_small=jax.ShapeDtypeStruct((8, 128), F32),
         rq=jax.ShapeDtypeStruct((NR, sh, hq3), BF16),
         ro=jax.ShapeDtypeStruct((sh, d), BF16),
-        ri=jax.ShapeDtypeStruct((NR, sh, sz.ntile * t2), BF16),
+        ri=jax.ShapeDtypeStruct((NR, sh, sz.iw), BF16),
         rd=jax.ShapeDtypeStruct((sz.ffp, d), BF16),
     )
     scratch = dict(
-        wq=bf(d, hq3), wo=bf(2 * sh, d), wi=bf(d, sz.ntile * t2), wd=bf(sz.fq, d),
+        wq=bf(d, hq3), wo=bf(2 * sh, d), wi=bf(d, sz.iw), wd=bf(sz.fq, d),
         xs=bf(rows, d), cs=bf(rows, d), mx=bf(rows, d), gt=bf(rows, d),
         aall=bf(all_, d), hall=bf(all_, d), call=bf(all_, d), yall=bf(all_, d),
-        smalls=fl(NF, 8, 128), lens=fl(NR, 8, 128), gains=fl(8, d),
+        smalls=fl(NF, 8, 128), mini=fl(8, 128), lens=fl(NR, 8, 128), gains=fl(8, d),
         qkv=bf(all_, hq3), pbuf=fl(NR * sz.micro, sz.hq // 128, 2 * sz.slot, 128), obuf=bf(all_, sz.hq),
-        part=fl(all_, d), sib0=fl(2, rows, d), sib1=fl(2, rows, d),
-        xsend=bf(rows, d), xrecv0=bf(rows, d), xrecv1=bf(rows, d),
+        part=fl(all_, d), part2=fl(all_, d), sib0=fl(2, rows, d), sib1=fl(2, rows, d),
+        xsend=bf(rows, d), xsend2=bf(rows, d), xrecv0=bf(rows, d), xrecv1=bf(rows, d),
         hbuf=fl(rows, d), dhbuf=fl(rows, d), dg=fl(2, 8, d),
-        gg=bf(all_, sz.fq), slope=fl(all_, sz.fq), dw=bf(all_, sz.ntile * t2), dqkv=bf(all_, hq3),
-        gd=bf(sz.fq, d), gi=bf(sz.ntile, d, t2), go=bf(2 * sh, d), gq=bf(3, d, sz.hq),
+        gg=bf(all_, sz.fq), slope=fl(all_, sz.fq), dw=bf(all_, sz.iw), dqkv=bf(all_, hq3),
+        gd=bf(sz.fq, d), gi=bf(d, sz.iw), go=bf(2 * sh, d), gq=bf(3, d, sz.hq),
         yrd=bf(3, third, d), zrd=bf(3, 2, third, d),
         yri=bf(sz.ntile, NZ, sh, t2), zri=bf(sz.ntile, NZ + 1, sh, t2),
         yro=bf(2, half, d), zro=bf(2, 2, 2, half, d),
         yrq=bf(3, NZ, sh, sz.hq), zrq=bf(3, NZ + 1, sh, sz.hq),
         gsend=fl(NF, 8, 128), gslots=fl(NF, 8, 128), greps=fl(NR, 8, 128), gout=fl(8, 128),
-        sends=pltpu.SemaphoreType.DMA((96,)), recvs=pltpu.SemaphoreType.DMA((184,)),
+        sends=pltpu.SemaphoreType.DMA((90,)), recvs=pltpu.SemaphoreType.DMA((187,)),
         locals=pltpu.SemaphoreType.DMA((32,)),
     )
     any_ = pl.BlockSpec(memory_space=pl.ANY)
@@ -1434,67 +1463,76 @@
     return pl.pallas_call(
         functools.partial(kernel, sz, names),
         out_shape=list(outs.values()),
-        in_specs=[any_] * 3 + [vmem] * 2 + [any_] * 4,
+        in_specs=[any_] * 2 + [vmem] * 6 + [any_] * 4,
         out_specs=[any_] * len(outs),
         scratch_shapes=list(scratch.values()),
         compiler_params=pltpu.CompilerParams(collective_id=0, has_side_effects=True, vmem_limit_bytes=64 * MIB),
     )(*ins.values())
 
 
-def finish_kernel(sz, rq, ro, ri, rd, gq, go, gi, gd):
-    hq, t, ffs, ffp = sz.hq, sz.tile, sz.ffs, sz.ffp
+def finish_kernel(sz, small, mixed, gtok, rq, ro, ri, rd, out_m, out_t, g1, gq, go, g2, gi, gd):
+    hq, ffs, ffp = sz.hq, sz.ffs, sz.ffp
     for i in range(3):
         for q in range(NR):
             gq[:, i * sz.d + q * hq : i * sz.d + (q + 1) * hq] = rq[q, :, i * hq : (i + 1) * hq].astype(F32)
+    g1[...], g2[...] = small[0:1, :], small[1:2, :]
+    out_m[...], out_t[...] = mixed[...], gtok[...]
     go[...] = ro[...].astype(F32)
     gd[...] = rd[...].astype(F32)
-    pieces = []
-    for i in range(2):
-        for q in range(NR):
-            v = [ri[q, :, (2 * n + i) * t : (2 * n + i + 1) * t].astype(F32) for n in range(sz.ntile)]
-            v = jnp.concatenate(v, axis=1)
-            pieces += [v[:, :ffs], v[:, ffp : ffp + ffs]]
-    gi[...] = jnp.concatenate(pieces, axis=1)
-
-
-def finish(sz, rq, ro, ri, rd):
+    pieces = [[], []]
+    for q in range(NR):
+        tiles = [apart(sz, n, ri[q, :, col : col + w].astype(F32)) for n, (col, w) in enumerate(sz.units)]
+        for i in range(2):
+            v = jnp.concatenate([two[i] for two in tiles], axis=1)
+            pieces[i] += [v[:, :ffs], v[:, ffp : ffp + ffs]]
+    gi[...] = jnp.concatenate(pieces[0] + pieces[1], axis=1)
+
+
+def finish(sz, small, mixed, gtok, rq, ro, ri, rd):
     d, sh = sz.d, sz.shard
     steps, n = sh // 16, sz.ffp // 16
     down = -(-n // steps) * 16
     last = -(-sz.ffp // down) - 1
     row = lambda w: pl.BlockSpec((16, w), lambda i: (i, 0))
     low = pl.BlockSpec((down, d), lambda i: (jnp.minimum(i, last), 0))
+    rows = sz.micro * NF * sz.part // steps
+    each = pl.BlockSpec((rows, d), lambda i: (i, 0))
+    one = lambda n: pl.BlockSpec((n, sh), lambda i: (0, 0))
     quarters = lambda w: pl.BlockSpec((NR, 16, w), lambda i: (0, i, 0))
     return pl.pallas_call(
         functools.partial(finish_kernel, sz),
         grid=(steps,),
         out_shape=[
+            jax.ShapeDtypeStruct((rows * steps, d), BF16),
+            jax.ShapeDtypeStruct((rows * steps, d), BF16),
+            jax.ShapeDtypeStruct((1, sh), F32),
             jax.ShapeDtypeStruct((sh, 3 * d), F32),
             jax.ShapeDtypeStruct((sh, d), F32),
+            jax.ShapeDtypeStruct((1, sh), F32),
             jax.ShapeDtypeStruct((sh, 2 * NF * sz.ffs), F32),
             jax.ShapeDtypeStruct((sz.ffs, d), F32),
         ],
-        in_specs=[quarters(rq.shape[2]), row(d), quarters(ri.shape[2]), low],
-        out_specs=[row(3 * d), row(d), row(2 * NF * sz.ffs), low],
+        in_specs=[one(8), each, each, quarters(rq.shape[2]), row(d), quarters(ri.shape[2]), low],
+        out_specs=[each, each, one(1), row(3 * d), row(d), one(1), row(2 * NF * sz.ffs), low],
         compiler_params=pltpu.CompilerParams(vmem_limit_bytes=60 * MIB),
-    )(rq, ro, ri, rd)
+    )(small, mixed.reshape(-1, d), gtok.reshape(-1, d), rq, ro, ri, rd)
 
 
 def routed(tokens, cotangent, deal, lengths, ln1_gain, w_qkv, w_out, ln2_gain, w_in, w_down):
     micro, _, part, d = tokens.shape
     ffs = w_down.shape[0]
     sz = Sizes(micro, part, d, ffs)
-    gain = [lax.reduce_precision(g, 8, 7)[None] for g in (ln1_gain, ln2_gain)]
-    wide = lambda v: jnp.pad(v.astype(F32), ((0, 0), (0, 128 - v.shape[1])))
-    small = jnp.concatenate(gain + [wide(lengths[:, 0, 0][None]), wide(deal[:, 0]), jnp.zeros((5 - micro, 128), F32)])
     half = d // HEADS // 2
     freq = np.float32(ROPE_BASE) ** (-(np.arange(half, dtype=np.float32) * np.float32(2.0 / (2 * half))))
     angles = np.arange(sz.slot, dtype=np.float32)[:, None] * freq[None, :]
     cos = jnp.asarray(np.tile(np.cos(angles), (1, 4)))
     sin = jnp.asarray(np.tile(np.concatenate([-np.sin(angles), np.sin(angles)], axis=1), (1, 2)))
-    mixed, gtok, osmall, rq, ro, ri, rd = fused(sz, tokens, cotangent, small, cos, sin, w_qkv, w_out, w_in, w_down)
-    g_qkv, g_out, g_in, g_down = finish(sz, rq, ro, ri, rd)
-    return mixed, gtok, osmall[0], g_qkv, g_out, osmall[1], g_in, g_down
+    mixed, gtok, osmall, rq, ro, ri, rd = fused(
+        sz, tokens, cotangent, ln1_gain[None], ln2_gain[None], lengths.reshape(1, micro), deal[:, 0],
+        cos, sin, w_qkv, w_out, w_in, w_down,
+    )
+    mixed, gtok, g_1, g_qkv, g_out, g_2, g_in, g_down = finish(sz, osmall, mixed, gtok, rq, ro, ri, rd)
+    return mixed.reshape(tokens.shape), gtok.reshape(tokens.shape), g_1[0], g_qkv, g_out, g_2[0], g_in, g_down
 
 
 def solution(mesh):

time: 239 us -> 228 us (0.954)
  Pallas kernels: 232 us -> 226 us
  local copies, waits for them, and re-layouts: 3.49 us -> 0 us
    pallas_call x1, Pallas kernels: 224 us -> 218 us  [fused(): pl.pallas_call(functools.partial(kernel, sz, names), out_shape=list(outs....]
where the time goes in v4:
time: 228 us; the launch traced here: 227 us
  Pallas kernels  226 us (99%)
    pallas_call x1, Pallas kernels, fused(): pl.pallas_call(functools.partial(kernel, sz, names), out_shape=list(outs....  218 us
    pallas_call x1, Pallas kernels, finish(): pl.pallas_call(functools.partial(finish_kernel, sz), grid=(steps,), out_s...  8.04 us

profile of v4, /device:TPU:17, one launch (start us, length us, event | category | flops | bytes accessed | tf_op | source)
XLA Modules:
  0.0 226.8 jit_solution(2309371897714868353)
XLA Ops:
  0.6 217.9 %shard_map.179 = (bf16[2,8,16,1024]{3,2,1,0:T(8,128)(2,1)}, bf16[2,8,16,1024]{3,2,1,0:T(8,128)(2,1)}, f32[8,128]{1,0:T(8,128)}, bf16[4,128,768]{2,1,0:T(8,128)(2...) custom-call(bf16[2,8,16,1024]{3,2,1,0:T(8,128)(2,1)} %refs_0_.1, ...), custom_call_target="tpu_custom_call" | custom-call | tf_op jit(solution)/shard_map/pallas_call | solution.py:1463
  218.6 8.0 %shard_map.180 = (bf16[256,1024]{1,0:T(8,128)(2,1)}, bf16[256,1024]{1,0:T(8,128)(2,1)}, f32[1,128]{1,0:T(1,128)}, f32[128,3072]{1,0:T(8,128)}, f32[128,1024]{1,0...) custom-call(f32[8,128]{1,0:T(8,128)} %get-tuple-element.23.small, ...), custom_call_target="tpu_custom_call" | custom-call | tf_op jit(solution)/shard_map/pallas_call | solution.py:1502

commit v5 on v4

--- a/solution.py
+++ b/solution.py
@@ -176,14 +176,14 @@
 
 
 ORDER = (
-    2, 0, 24, 25, 72, 1, 20, 53, 4, 54, 5, 10, 15, 6, 11, 16, 3, 7, 12, 17, 55, 57, 33, 74, 58, 59, 73, 8, 13, 18,
-    22, 26, 60, 52, 21, 27, 75, 35, 62, 23, 9, 14, 19, 69, 34, 76, 38, 43, 61, 49, 46, 28, 67, 65, 56, 63, 64, 66,
-    29, 40, 71, 70, 30, 79, 31, 39, 68, 77, 41, 81, 32, 36, 44, 82, 78, 86, 80, 50, 85, 42, 83, 84, 37, 90, 89, 47,
-    91, 51, 87, 88, 92, 48, 45, 96, 93, 103, 95, 94, 104, 107, 141, 105, 100, 97, 147, 98, 99, 106, 144, 108, 109,
-    128, 150, 110, 115, 151, 113, 127, 155, 102, 145, 142, 111, 116, 112, 156, 152, 101, 114, 124, 171, 119, 125,
-    170, 117, 165, 157, 126, 166, 146, 129, 153, 161, 130, 118, 120, 121, 175, 148, 176, 122, 131, 132, 180, 158,
-    172, 123, 185, 133, 135, 177, 160, 181, 182, 143, 186, 178, 187, 149, 154, 134, 167, 162, 136, 137, 159, 183,
-    188, 138, 168, 179, 169, 173, 163, 139, 164, 184, 189, 140, 174, 190,
+    3, 1, 2, 0, 24, 4, 15, 10, 5, 16, 54, 28, 17, 20, 53, 72, 12, 55, 11, 58, 18, 7, 6, 57, 56, 60, 74, 30, 13, 8,
+    25, 21, 22, 73, 19, 59, 26, 75, 76, 33, 14, 27, 23, 52, 9, 62, 29, 38, 63, 64, 39, 61, 65, 35, 34, 66, 31, 71,
+    46, 67, 40, 68, 49, 69, 36, 77, 70, 41, 78, 43, 47, 81, 82, 83, 50, 37, 86, 79, 42, 80, 32, 91, 90, 84, 44, 48,
+    85, 87, 88, 89, 92, 51, 45, 93, 103, 94, 104, 141, 107, 96, 95, 105, 97, 144, 106, 116, 115, 108, 147, 99, 98,
+    150, 100, 109, 128, 152, 111, 151, 112, 155, 101, 113, 142, 102, 114, 124, 171, 119, 165, 148, 126, 127, 145,
+    166, 125, 160, 129, 156, 161, 130, 117, 153, 170, 175, 110, 162, 118, 134, 131, 133, 176, 120, 167, 180, 122,
+    123, 149, 172, 132, 185, 181, 135, 157, 154, 186, 136, 177, 187, 143, 158, 168, 173, 182, 137, 138, 121, 146,
+    174, 169, 163, 159, 178, 188, 183, 164, 139, 179, 189, 184, 140, 190,
 )
 
 
@@ -1490,15 +1490,16 @@
 
 def finish(sz, small, mixed, gtok, rq, ro, ri, rd):
     d, sh = sz.d, sz.shard
-    steps, n = sh // 16, sz.ffp // 16
+    grain = 32
+    steps, n = sh // grain, sz.ffp // 16
     down = -(-n // steps) * 16
     last = -(-sz.ffp // down) - 1
-    row = lambda w: pl.BlockSpec((16, w), lambda i: (i, 0))
+    row = lambda w: pl.BlockSpec((grain, w), lambda i: (i, 0))
     low = pl.BlockSpec((down, d), lambda i: (jnp.minimum(i, last), 0))
     rows = sz.micro * NF * sz.part // steps
     each = pl.BlockSpec((rows, d), lambda i: (i, 0))
     one = lambda n: pl.BlockSpec((n, sh), lambda i: (0, 0))
-    quarters = lambda w: pl.BlockSpec((NR, 16, w), lambda i: (0, i, 0))
+    quarters = lambda w: pl.BlockSpec((NR, grain, w), lambda i: (0, i, 0))
     return pl.pallas_call(
         functools.partial(finish_kernel, sz),
         grid=(steps,),

time: 228 us -> 213 us (0.934)
  Pallas kernels: 226 us -> 211 us
    pallas_call x1, Pallas kernels: 218 us -> 206 us  [fused(): pl.pallas_call(functools.partial(kernel, sz, names), out_shape=list(outs....]
    pallas_call x1, Pallas kernels: 8.04 us -> 5.7 us  [finish(): pl.pallas_call(functools.partial(finish_kernel, sz), grid=(steps,), out_s...]
where the time goes in v5:
time: 213 us; the launch traced here: 212 us
  Pallas kernels  211 us (99%)
    pallas_call x1, Pallas kernels, fused(): pl.pallas_call(functools.partial(kernel, sz, names), out_shape=list(outs....  206 us
    pallas_call x1, Pallas kernels, finish(): pl.pallas_call(functools.partial(finish_kernel, sz), grid=(steps,), out_s...  5.7 us

profile of v5, /device:TPU:17, one launch (start us, length us, event | category | flops | bytes accessed | tf_op | source)
XLA Modules:
  0.0 212.2 jit_solution(9335870463425171351)
XLA Ops:
  0.6 205.7 %shard_map.179 = (bf16[2,8,16,1024]{3,2,1,0:T(8,128)(2,1)}, bf16[2,8,16,1024]{3,2,1,0:T(8,128)(2,1)}, f32[8,128]{1,0:T(8,128)}, bf16[4,128,768]{2,1,0:T(8,128)(2...) custom-call(bf16[2,8,16,1024]{3,2,1,0:T(8,128)(2,1)} %refs_0_.1, ...), custom_call_target="tpu_custom_call" | custom-call | tf_op jit(solution)/shard_map/pallas_call | solution.py:1463
  206.4 5.7 %shard_map.180 = (bf16[256,1024]{1,0:T(8,128)(2,1)}, bf16[256,1024]{1,0:T(8,128)(2,1)}, f32[1,128]{1,0:T(1,128)}, f32[128,3072]{1,0:T(8,128)}, f32[128,1024]{1,0...) custom-call(f32[8,128]{1,0:T(8,128)} %get-tuple-element.23.small, ...), custom_call_target="tpu_custom_call" | custom-call | tf_op jit(solution)/shard_map/pallas_call | solution.py:1503

commit v6 on v5

--- a/solution.py
+++ b/solution.py
@@ -176,14 +176,14 @@
 
 
 ORDER = (
-    3, 1, 2, 0, 24, 4, 15, 10, 5, 16, 54, 28, 17, 20, 53, 72, 12, 55, 11, 58, 18, 7, 6, 57, 56, 60, 74, 30, 13, 8,
-    25, 21, 22, 73, 19, 59, 26, 75, 76, 33, 14, 27, 23, 52, 9, 62, 29, 38, 63, 64, 39, 61, 65, 35, 34, 66, 31, 71,
-    46, 67, 40, 68, 49, 69, 36, 77, 70, 41, 78, 43, 47, 81, 82, 83, 50, 37, 86, 79, 42, 80, 32, 91, 90, 84, 44, 48,
-    85, 87, 88, 89, 92, 51, 45, 93, 103, 94, 104, 141, 107, 96, 95, 105, 97, 144, 106, 116, 115, 108, 147, 99, 98,
-    150, 100, 109, 128, 152, 111, 151, 112, 155, 101, 113, 142, 102, 114, 124, 171, 119, 165, 148, 126, 127, 145,
-    166, 125, 160, 129, 156, 161, 130, 117, 153, 170, 175, 110, 162, 118, 134, 131, 133, 176, 120, 167, 180, 122,
-    123, 149, 172, 132, 185, 181, 135, 157, 154, 186, 136, 177, 187, 143, 158, 168, 173, 182, 137, 138, 121, 146,
-    174, 169, 163, 159, 178, 188, 183, 164, 139, 179, 189, 184, 140, 190,
+    1, 0, 15, 2, 24, 3, 10, 5, 52, 16, 54, 20, 28, 17, 53, 72, 55, 56, 12, 58, 11, 18, 6, 7, 57, 60, 74, 30, 13, 8,
+    25, 59, 26, 22, 21, 27, 73, 75, 76, 4, 33, 19, 23, 29, 38, 62, 14, 9, 63, 64, 34, 79, 39, 69, 65, 35, 66, 31,
+    71, 46, 49, 61, 67, 68, 40, 36, 70, 78, 77, 41, 81, 47, 82, 43, 32, 83, 50, 42, 37, 91, 86, 90, 84, 80, 44, 85,
+    87, 88, 48, 89, 92, 51, 45, 93, 103, 94, 104, 141, 96, 107, 95, 105, 144, 106, 97, 115, 147, 108, 98, 150, 109,
+    99, 151, 128, 111, 100, 152, 110, 113, 116, 112, 155, 101, 102, 114, 124, 165, 171, 125, 127, 145, 166, 126,
+    160, 119, 129, 161, 133, 170, 167, 142, 156, 146, 117, 162, 134, 131, 153, 148, 130, 175, 118, 176, 120, 122,
+    123, 180, 132, 135, 185, 181, 157, 186, 177, 136, 158, 143, 182, 172, 178, 187, 137, 138, 163, 183, 188, 173,
+    168, 184, 179, 164, 154, 121, 139, 169, 189, 149, 140, 159, 174, 190,
 )
 
 

time: 213 us -> 210 us (0.986)
  Pallas kernels: 211 us -> 208 us
    pallas_call x1, Pallas kernels: 206 us -> 202 us  [fused(): pl.pallas_call(functools.partial(kernel, sz, names), out_shape=list(outs....]
where the time goes in v6:
time: 210 us; the launch traced here: 208 us
  Pallas kernels  208 us (99%)
    pallas_call x1, Pallas kernels, fused(): pl.pallas_call(functools.partial(kernel, sz, names), out_shape=list(outs....  202 us
    pallas_call x1, Pallas kernels, finish(): pl.pallas_call(functools.partial(finish_kernel, sz), grid=(steps,), out_s...  5.7 us

profile of v6, /device:TPU:17, one launch (start us, length us, event | category | flops | bytes accessed | tf_op | source)
XLA Modules:
  0.0 208.4 jit_solution(10025630023886988329)
XLA Ops:
  0.6 201.9 %shard_map.179 = (bf16[2,8,16,1024]{3,2,1,0:T(8,128)(2,1)}, bf16[2,8,16,1024]{3,2,1,0:T(8,128)(2,1)}, f32[8,128]{1,0:T(8,128)}, bf16[4,128,768]{2,1,0:T(8,128)(2...) custom-call(bf16[2,8,16,1024]{3,2,1,0:T(8,128)(2,1)} %refs_0_.1, ...), custom_call_target="tpu_custom_call" | custom-call | tf_op jit(solution)/shard_map/pallas_call | solution.py:1463
  202.6 5.7 %shard_map.180 = (bf16[256,1024]{1,0:T(8,128)(2,1)}, bf16[256,1024]{1,0:T(8,128)(2,1)}, f32[1,128]{1,0:T(1,128)}, f32[128,3072]{1,0:T(8,128)}, f32[128,1024]{1,0...) custom-call(f32[8,128]{1,0:T(8,128)} %get-tuple-element.23.small, ...), custom_call_target="tpu_custom_call" | custom-call | tf_op jit(solution)/shard_map/pallas_call | solution.py:1503

commit v7 on v6

--- a/solution.py
+++ b/solution.py
@@ -1490,7 +1490,7 @@
 
 def finish(sz, small, mixed, gtok, rq, ro, ri, rd):
     d, sh = sz.d, sz.shard
-    grain = 32
+    grain = 64
     steps, n = sh // grain, sz.ffp // 16
     down = -(-n // steps) * 16
     last = -(-sz.ffp // down) - 1

time: 210 us -> 209 us (level)
  no operation moved by 1% of the time
where the time goes in v7:
time: 209 us; the launch traced here: 208 us
  Pallas kernels  207 us (99%)
    pallas_call x1, Pallas kernels, fused(): pl.pallas_call(functools.partial(kernel, sz, names), out_shape=list(outs....  202 us
    pallas_call x1, Pallas kernels, finish(): pl.pallas_call(functools.partial(finish_kernel, sz), grid=(steps,), out_s...  4.83 us

profile of v7, /device:TPU:17, one launch (start us, length us, event | category | flops | bytes accessed | tf_op | source)
XLA Modules:
  0.0 207.6 jit_solution(16294723523710375635)
XLA Ops:
  0.6 201.9 %shard_map.179 = (bf16[2,8,16,1024]{3,2,1,0:T(8,128)(2,1)}, bf16[2,8,16,1024]{3,2,1,0:T(8,128)(2,1)}, f32[8,128]{1,0:T(8,128)}, bf16[4,128,768]{2,1,0:T(8,128)(2...) custom-call(bf16[2,8,16,1024]{3,2,1,0:T(8,128)(2,1)} %refs_0_.1, ...), custom_call_target="tpu_custom_call" | custom-call | tf_op jit(solution)/shard_map/pallas_call | solution.py:1463
  202.6 4.8 %shard_map.180 = (bf16[256,1024]{1,0:T(8,128)(2,1)}, bf16[256,1024]{1,0:T(8,128)(2,1)}, f32[1,128]{1,0:T(1,128)}, f32[128,3072]{1,0:T(8,128)}, f32[128,1024]{1,0...) custom-call(f32[8,128]{1,0:T(8,128)} %get-tuple-element.23.small, ...), custom_call_target="tpu_custom_call" | custom-call | tf_op jit(solution)/shard_map/pallas_call | solution.py:1503
